TPU v7x, 128 devices: a whole 4x4x4 slice. The times are simulated.
128 devices in a mesh: gx: 32 (over x, y_lo, z), gy: 4 (over y_hi, core).
Axes of the slice: x: 4, y: 4 (y_hi: 2, y_lo: 2; y = y_hi * 2 + y_lo), z: 4, core: 2. Of those that a mesh axis runs over, the one named last changes fastest.
Arguments:
- pressure: float32 [512, 128, 512], P('gx', 'gy'), may hold values from -2.5 to 2.5
- velocity: float32 [3, 512, 128, 512], P(None, 'gx', 'gy'), may hold values from -2.5 to 2.5
- stretch: float32 [131072, 256], P(('gx', 'gy')), may hold values from 0.8 to 1.25
- rest_radius: float32 [131072, 256], P(('gx', 'gy')), may hold values from 1 to 3
- wall_speed: float32 [131072, 256], P(('gx', 'gy')), may hold values from -2.5 to 2.5
- block_cells: int32 [131072], P(('gx', 'gy')), may hold values from -1 to 1023, as said below
- depart_slot: int32 [4, 32, 4, 8], P(None, 'gx', 'gy'), may hold values from -1 to 1023, as said below
- depart_way: int32 [4, 32, 4, 8], P(None, 'gx', 'gy'), may hold values from 0 to 3, as said below
Outputs:
- pressure_out: float32 [512, 128, 512], P('gx', 'gy')
- velocity_out: float32 [3, 512, 128, 512], P(None, 'gx', 'gy')
- radius_out: float32 [131072, 256], P(('gx', 'gy'))
- speed_out: float32 [131072, 256], P(('gx', 'gy'))
- cells_out: int32 [131072], P(('gx', 'gy'))
Inputs may be any that keep to these rules, and one draw needn't show every extreme that they name: `block_cells`: each tile has at most 896 occupied slots at the start and at least 896 // 3 (a third of it, rounded down); some tile has exactly 896. `depart_slot`: A used entry names a slot occupied at the start whose block has not left before; each slot is named by at most one entry in the whole window. Every tile has room for its arrivals. `depart_way`: tiles at the ends of the second tile index never send past them.
All inputs are finite; a program needn't handle non-finite values.
Results may differ from a plain program's by a relative error of at most 0.0003.
Values sent between devices are 32-bit elements; how exact they have to be, the bound alone decides.
A program may use at most 128 MiB of HBM per device.

v0:
```python
import functools
import math

import jax
import jax.numpy as jnp
from jax import lax
from jax.experimental import pallas as pl
from jax.experimental.pallas import tpu as pltpu
from jax.sharding import PartitionSpec as P

MESH = pl.DeviceIdType.MESH
f32 = jnp.float32
bf16 = jnp.bfloat16

STEPS = 4
DEP = 8
SLOTS = 1024
BLOCK = 256
LANES = 128
ARRIVE = STEPS * 4 * DEP
ROWS = SLOTS + ARRIVE
SLOT_BLOCKS = SLOTS // LANES
WAY_OF = (1, 0, 3, 2)

time_step = 0.04
half_gain = 0.2
source_scale = 0.004 * 12.566370614359172
exponent = 4.2
inv_ln2 = 1.0 / math.log(2.0)


def split(value):
    high = value.astype(bf16)
    return high, (value - high.astype(f32)).astype(bf16)


def wall_update(radius, speed, level, pressure):
    one_less = 1.0 - 0.05 * speed
    divisor = one_less * radius
    inverse = pl.reciprocal(divisor, approx=True)
    inverse = inverse * (2.0 - divisor * inverse)
    inv_radius = inverse * one_less
    wall = jnp.exp2(level - (exponent * inv_ln2) * jnp.log(radius))
    excess = wall - (0.2 + 0.08 * speed) * inv_radius - (1.0 + pressure)
    driving = (2.0 - one_less) * excess - (1.0 + 0.5 * one_less) * (speed * speed)
    speed = speed + time_step * (driving * inverse)
    radius = radius + time_step * speed
    return radius, speed, source_scale * (radius * radius) * speed


def kernel(
    cells_h, slot_h, way_h, cells_b, press, vel, stretch, rest, speed0,
    p_out, VX, VY, VZ, R, S, c_out,
    PR, A, AR, SB, OH, OHT, PHL, PG, VHL, SRC, YS, YR, VYS, VYR,
    MT, MR, MSK, AMSK, LT, LR, PLACE, CAT, cells_s, slot_s, way_s, cells_v,
    in_sem, meta_s, meta_r, xs, xr, vs, vr, ds_, dr,
):
    _, cx, cy, nz = vel.shape
    nq = nz // LANES
    half = cx * cy
    ncol = 2 * half
    jbs = cy // 16
    gx, gy = lax.axis_index("gx"), lax.axis_index("gy")
    ngx, ngy = lax.axis_size("gx"), lax.axis_size("gy")
    has_lo, has_hi = gy > 0, gy < ngy - 1
    targets = (
        (lax.rem(gx + 1, ngx), gy),
        (lax.rem(gx + ngx - 1, ngx), gy),
        (gx, lax.rem(gy + 1, ngy)),
        (gx, lax.rem(gy + ngy - 1, ngy)),
    )
    sends = (None, None, has_hi, has_lo)
    takes = (None, None, has_lo, has_hi)

    def under(flag, action):
        if flag is None:
            action()
        else:
            pl.when(flag)(action)

    barrier = pltpu.get_barrier_semaphore()
    for d in range(4):
        under(
            sends[d],
            lambda d=d: pl.semaphore_signal(
                barrier, inc=1, device_id=targets[d], device_id_type=MESH
            ),
        )

    inputs = [(cells_h, cells_s), (slot_h, slot_s), (way_h, way_s), (cells_b, cells_v)]
    for q in range(nq):
        inputs.append((press.at[:, :, pl.ds(q * LANES, LANES)], PR.at[0, q, pl.ds(2, cx), pl.ds(8, cy), :]))
    inputs.append((rest, A))
    inputs.append((stretch, R))
    inputs.append((speed0, S))
    for comp in range(3):
        for q in range(nq):
            dst = (
                VX.at[q, pl.ds(1, cx), :, :],
                VY.at[q, :, pl.ds(8, cy), :],
                VZ.at[q],
            )[comp]
            inputs.append((vel.at[comp, :, :, pl.ds(q * LANES, LANES)], dst))
    loads = [pltpu.make_async_copy(a, b, in_sem.at[k]) for k, (a, b) in enumerate(inputs)]
    for load in loads:
        load.start()

    for load in loads[:4]:
        load.wait()
    loads = loads[4:]

    lane8 = lax.broadcasted_iota(jnp.int32, (8, LANES), 1)
    sub8 = lax.broadcasted_iota(jnp.int32, (8, LANES), 0)
    slot_id = sub8 * LANES + lane8
    label = cells_v[...] + 1
    leave_at = jnp.where(label > 0, STEPS, -1)
    entry_of = (lane8 // 32) * DEP + lane8 % DEP
    wanted = (lane8 // DEP) % 4
    wanted = jnp.where(wanted < 2, 1 - wanted, 5 - wanted)
    meta = jnp.zeros((8, LANES), jnp.int32)
    for e in range(STEPS * DEP):
        slot = slot_s[e // DEP, 0, 0, e % DEP]
        moved = jnp.where(slot >= 0, cells_s[jnp.maximum(slot, 0)] + 1, 0)
        meta = jnp.where((entry_of == e) & (wanted == way_s[e // DEP, 0, 0, e % DEP]), moved, meta)
        leave_at = jnp.where(slot_id == slot, e // DEP, leave_at)
    MT[...] = meta.astype(f32)

    @pl.when(jnp.logical_not(has_lo))
    def _():
        MR[2] = jnp.zeros((8, LANES), f32)
        YR[:, 0] = jnp.zeros(YR.shape[:1] + YR.shape[2:], f32)
        VYR[0] = jnp.zeros(VYR.shape[1:], f32)

    @pl.when(jnp.logical_not(has_hi))
    def _():
        MR[3] = jnp.zeros((8, LANES), f32)
        YR[:, 1] = jnp.zeros(YR.shape[:1] + YR.shape[2:], f32)
        VYR[1] = jnp.zeros(VYR.shape[1:], f32)

    pl.semaphore_wait(barrier, 2 + has_lo.astype(jnp.int32) + has_hi.astype(jnp.int32))

    def remote(src, dst, send_sem, recv_sem, d):
        return pltpu.make_async_remote_copy(
            src_ref=src, dst_ref=dst, send_sem=send_sem, recv_sem=recv_sem,
            device_id=targets[d], device_id_type=MESH,
        )

    def meta_copy(d):
        return remote(MT, MR.at[d], meta_s.at[d], meta_r.at[d], d)

    def p_copy(t, par, d):
        if d < 2:
            src = PR.at[par, :, pl.ds((cx, 2)[d], 2), pl.ds(8, cy), :]
            dst = PR.at[par, :, pl.ds((0, cx + 2)[d], 2), pl.ds(8, cy), :]
        else:
            src, dst = YS.at[t, 3 - d], YR.at[t, d - 2]
        return remote(src, dst, xs.at[t, d], xr.at[t, d], d)

    def v_copy(d):
        if d < 2:
            src = VX.at[:, pl.ds((cx, 1)[d], 1), :, :]
            dst = VX.at[:, pl.ds((0, cx + 1)[d], 1), :, :]
        else:
            src, dst = VYS.at[3 - d], VYR.at[d - 2]
        return remote(src, dst, vs.at[d], vr.at[d], d)

    def dep_copy(t, d):
        return remote(
            SB.at[t], AR.at[:, pl.ds(t * 32 + d * DEP, DEP), :], ds_.at[t, d], dr.at[t, d], d
        )

    def start(make):
        for d in range(4):
            under(sends[d], lambda d=d: make(d).start())

    def wait_sent(make):
        for d in range(4):
            under(sends[d], lambda d=d: make(d).wait_send())

    def wait_taken(make):
        for d in range(4):
            under(takes[d], lambda d=d: make(d).wait_recv())

    start(meta_copy)

    def pack_rows(t, par):
        def body(i, carry):
            for q in range(nq):
                YS[t, 0, q, i] = PR[par, q, i + 2, 8:10, :]
                YS[t, 1, q, i] = PR[par, q, i + 2, 6 + cy : 8 + cy, :]
            return carry

        lax.fori_loop(0, cx, body, 0, unroll=4)

    def keep_parts(i, jb, q, value):
        high, low = split(value)
        row = pl.multiple_of((q // 2) * half + i * cy + jb * 16, 16)
        col = (q % 2) * LANES
        PHL[pl.ds(row, 16), col : col + LANES] = high
        PHL[pl.ds(pl.multiple_of(row + ncol, 16), 16), col : col + LANES] = low

    for k in range(nq):
        loads[k].wait()
    pack_rows(0, 0)
    start(lambda d: p_copy(0, 0, d))

    def first_split(n, carry):
        i, jb = n // jbs, n % jbs
        for q in range(nq):
            keep_parts(i, jb, q, PR[0, q, i + 2, pl.ds(pl.multiple_of(8 + jb * 16, 8), 16), :])
        return carry

    lax.fori_loop(0, cx * jbs, first_split, 0, unroll=4)

    for k in range(nq, nq + 3):
        loads[k].wait()

    def first_state(n, carry):
        rows = pl.ds(pl.multiple_of(n * 16, 16), 16)
        rest_now = A[rows, :]
        R[rows, :] = R[rows, :] * rest_now
        A[rows, :] = inv_ln2 * (jnp.log(1.0 + 0.2 / rest_now) + exponent * jnp.log(rest_now))
        return carry

    lax.fori_loop(0, SLOTS // 16, first_state, 0, unroll=4)
    VHL[pl.ds(SLOTS, ARRIVE), :] = jnp.zeros((ARRIVE, BLOCK), bf16)
    VHL[pl.ds(ROWS + SLOTS, ARRIVE), :] = jnp.zeros((ARRIVE, BLOCK), bf16)

    for k in range(nq + 3, nq + 3 + 3 * nq):
        loads[k].wait()

    def pack_flow(i, carry):
        for q in range(nq):
            VYS[0, q, i] = VY[q, i, 8:9, :]
            VYS[1, q, i] = VY[q, i, 7 + cy : 8 + cy, :]
        return carry

    lax.fori_loop(0, cx, pack_flow, 0, unroll=4)
    start(v_copy)

    wait_taken(meta_copy)
    came = (lane8 // DEP) % 4
    alab = jnp.where(
        came == 0, MR[0], jnp.where(came == 1, MR[1], jnp.where(came == 2, MR[2], MR[3]))
    )
    present = alab > 0.0
    lrow = lax.broadcasted_iota(jnp.int32, (LANES, LANES), 0)
    lcol = lax.broadcasted_iota(jnp.int32, (LANES, LANES), 1)
    upper = jnp.where(lrow <= lcol, 1.0, 0.0)
    upper_block = jnp.where(lrow // 32 == lcol // 32, upper, 0.0).astype(bf16)
    upper = upper.astype(bf16)
    ones = jnp.ones((LANES, LANES), bf16)
    present_f = jnp.where(present, 1.0, 0.0)
    arank = jnp.dot(present_f.astype(bf16), upper_block, preferred_element_type=f32) - 1.0
    arank = jnp.where(present, arank, -5.0)
    vacant = label == 0
    ranks = []
    for t in range(STEPS):
        vacant = vacant | (leave_at == t)
        flag = jnp.where(vacant, 1.0, 0.0).astype(bf16)
        rank = jnp.dot(flag, upper, preferred_element_type=f32) - 1.0
        total = jnp.dot(flag, ones, preferred_element_type=f32)
        for r in range(SLOT_BLOCKS - 1):
            rank = rank + jnp.where(sub8 > r, total[r : r + 1, :], 0.0)
        ranks.append(jnp.where(vacant, rank, -1.0))
        count = jnp.sum(jnp.where(lane8 // 32 == t, present_f, 0.0), axis=1, keepdims=True)
        vacant = vacant & (rank >= count)

    def code_of(lab):
        cell = lab - 1
        return jnp.where(lab > 0, (cell & 1) * half + (cell >> 1), -1).astype(f32)

    code = code_of(label)
    acode = code_of(alab.astype(jnp.int32))
    stack = [code, leave_at.astype(f32)] + ranks + [acode, alab]
    stack = stack + [jnp.zeros((8, LANES), f32)] * (16 - len(stack))
    LT[...] = jnp.concatenate(stack, axis=0).T
    LR[0:8, :] = code
    LR[8:16, :] = acode

    wide = lax.broadcasted_iota(jnp.int32, (16, ncol), 1).astype(f32)
    for r in range(SLOT_BLOCKS + 1):
        at = r if r < SLOT_BLOCKS else 48

        def one_hot_rows(m, carry, r=r, at=at):
            rows = pl.ds(pl.multiple_of(m * 16, 16), 16)
            column = LT[rows, at : at + 1]
            hot = jnp.where(column == wide, 1.0, 0.0).astype(bf16)
            OH[pl.ds(pl.multiple_of(r * LANES + m * 16, 16), 16), :] = hot
            return carry

        lax.fori_loop(0, LANES // 16, one_hot_rows, 0, unroll=2)

    tall = lax.broadcasted_iota(jnp.int32, (LANES, LANES), 0)

    def one_hot_columns(m, carry):
        ident = (tall + m * LANES).astype(f32)
        rows = pl.ds(pl.multiple_of(m * LANES, LANES), LANES)
        for r in range(SLOT_BLOCKS + 1):
            hot = jnp.where(ident == LR[r : r + 1, :], 1.0, 0.0).astype(bf16)
            OHT[rows, r * LANES : (r + 1) * LANES] = hot
        return carry

    lax.fori_loop(0, ncol // LANES, one_hot_columns, 0)

    group = lcol // 32
    for r in range(SLOT_BLOCKS):
        MSK[r * LANES : (r + 1) * LANES, :] = jnp.broadcast_to(
            LT[:, 8 + r : 9 + r], (LANES, LANES)
        )
        mine = jnp.broadcast_to(LT[:, 16 + r : 17 + r], (LANES, LANES))
        for t in range(1, STEPS):
            mine = jnp.where(group == t, LT[:, 16 + 8 * t + r : 17 + 8 * t + r], mine)
        hot = jnp.where(mine == arank[0:1, :], 1.0, 0.0).astype(bf16)
        PLACE[r * LANES : (r + 1) * LANES, 0:LANES] = hot
        PLACE[r * LANES : (r + 1) * LANES, LANES : 2 * LANES] = hot
    AMSK[...] = jnp.broadcast_to(LT[:, 56:57], (LANES, LANES))

    alab_high, alab_low = split(alab)
    final = jnp.where(leave_at == STEPS, label, 0).astype(f32)
    for r in range(SLOT_BLOCKS):
        hot = PLACE[r * LANES : (r + 1) * LANES, 0:LANES]
        nt = (((1,), (1,)), ((), ()))
        placed = lax.dot_general(alab_high, hot, nt, preferred_element_type=f32)
        placed = placed + lax.dot_general(alab_low, hot, nt, preferred_element_type=f32)
        final = final + jnp.where(sub8 == r, placed, 0.0)
    c_out[...] = final.astype(jnp.int32) - 1

    lane16 = lax.broadcasted_iota(jnp.int32, (16, LANES), 1)
    first_lane, last_lane = lane16 == 0, lane16 == LANES - 1

    def slope_z(tiles):
        zero = jnp.zeros((16, LANES), f32)
        ahead = [pltpu.roll(v, LANES - 1, 1) for v in tiles] + [zero]
        behind = [zero] + [pltpu.roll(v, 1, 1) for v in tiles]
        return [
            jnp.where(last_lane, ahead[q + 1], ahead[q])
            - jnp.where(first_lane, behind[q], behind[q + 1])
            for q in range(nq)
        ]

    low_gate = jnp.where(has_lo, 1.0, 0.0).astype(f32)
    high_gate = jnp.where(has_hi, 1.0, 0.0).astype(f32)
    chunk = 384
    part = min(256, ncol)

    def step(t, carry):
        par = lax.rem(t, 2)
        new = 1 - par

        def gather(m, carry):
            rows = pl.ds(pl.multiple_of(m * chunk, chunk), chunk)
            hot = OH[rows, :]
            hot = jnp.concatenate([hot, hot], axis=1)
            PG[rows, :] = jnp.dot(hot, PHL[...], preferred_element_type=f32)
            return carry

        lax.fori_loop(0, ROWS // chunk, gather, 0)

        @pl.when(t > 0)
        def _():
            wait_taken(lambda d: dep_copy(t - 1, d))

        limit = t.astype(f32)

        def bubbles(n, carry):
            rows = pl.ds(pl.multiple_of(n * 16, 16), 16)
            radius, speed, rate = wall_update(R[rows, :], S[rows, :], A[rows, :], PG[rows, :])
            R[rows, :] = radius
            S[rows, :] = speed
            keep = MSK[rows, :]
            keep = jnp.concatenate([keep, keep], axis=1) >= limit
            high, low = split(jnp.where(keep, rate, 0.0))
            VHL[rows, :] = high
            VHL[pl.ds(pl.multiple_of(ROWS + n * 16, 16), 16), :] = low
            return carry

        lax.fori_loop(0, SLOTS // 16, bubbles, 0, unroll=4)

        for k in range(DEP):
            row = pl.ds(jnp.maximum(slot_s[t, 0, 0, k], 0), 1)
            SB[t, 0, k : k + 1, :] = R[row, :]
            SB[t, 1, k : k + 1, :] = S[row, :]
            SB[t, 2, k : k + 1, :] = A[row, :]
        start(lambda d: dep_copy(t, d))

        def arrived(n, carry):
            rows = pl.ds(pl.multiple_of(n * 16, 16), 16)
            low_rows = pl.ds(pl.multiple_of(SLOTS + n * 16, 16), 16)
            radius, speed, rate = wall_update(
                AR[0, rows, :], AR[1, rows, :], AR[2, rows, :], PG[low_rows, :]
            )
            AR[0, rows, :] = radius
            AR[1, rows, :] = speed
            keep = AMSK[rows, :]
            keep = jnp.concatenate([keep, keep], axis=1) > 0.0
            high, low = split(jnp.where(keep, rate, 0.0))
            VHL[low_rows, :] = high
            VHL[pl.ds(pl.multiple_of(ROWS + SLOTS + n * 16, 16), 16), :] = low
            return carry

        lax.fori_loop(0, 2 * t, arrived, 0)

        def scatter(m, carry):
            rows = pl.ds(pl.multiple_of(m * part, part), part)
            hot = OHT[rows, :]
            hot = jnp.concatenate([hot, hot], axis=1)
            SRC[rows, :] = jnp.dot(hot, VHL[...], preferred_element_type=f32)
            return carry

        lax.fori_loop(0, ncol // part, scatter, 0)

        wait_taken(lambda d: p_copy(t, par, d))
        wait_sent(lambda d: p_copy(t, par, d))

        @pl.when(t == 0)
        def _():
            wait_taken(v_copy)
            wait_sent(v_copy)

            def unpack(i, carry):
                for q in range(nq):
                    VY[q, i, 7:8, :] = VYR[0, q, i]
                    VY[q, i, 8 + cy : 9 + cy, :] = VYR[1, q, i]
                return carry

            lax.fori_loop(0, cx, unpack, 0)

        def flow_x(n, carry):
            i, jb = n // jbs, n % jbs
            rows = pl.ds(pl.multiple_of(jb * 16, 16), 16)
            at = pl.ds(pl.multiple_of(8 + jb * 16, 8), 16)
            for q in range(nq):
                VX[q, i, rows, :] = VX[q, i, rows, :] - half_gain * (
                    PR[par, q, i + 2, at, :] - PR[par, q, i, at, :]
                )
            return carry

        lax.fori_loop(0, (cx + 2) * jbs, flow_x, 0, unroll=4)

        def side_rows(i, carry):
            for q in range(nq):
                PR[par, q, i + 2, 6:8, :] = YR[t, 0, q, i]
                PR[par, q, i + 2, 8 + cy : 10 + cy, :] = YR[t, 1, q, i]
                VY[q, i, 7:8, :] = low_gate * (
                    VY[q, i, 7:8, :]
                    - half_gain * (PR[par, q, i + 2, 8:9, :] - YR[t, 0, q, i, 0:1, :])
                )
                VY[q, i, 8 + cy : 9 + cy, :] = high_gate * (
                    VY[q, i, 8 + cy : 9 + cy, :]
                    - half_gain * (YR[t, 1, q, i, 1:2, :] - PR[par, q, i + 2, 7 + cy : 8 + cy, :])
                )
            return carry

        lax.fori_loop(0, cx, side_rows, 0, unroll=4)

        def flow_yz(n, carry):
            i, jb = n // jbs, n % jbs
            rows = pl.ds(pl.multiple_of(jb * 16, 16), 16)
            at = pl.ds(pl.multiple_of(8 + jb * 16, 8), 16)
            after, before = pl.ds(9 + jb * 16, 16), pl.ds(7 + jb * 16, 16)
            slopes = slope_z([PR[par, q, i + 2, at, :] for q in range(nq)])
            for q in range(nq):
                VZ[q, i, rows, :] = VZ[q, i, rows, :] - half_gain * slopes[q]
                VY[q, i, at, :] = VY[q, i, at, :] - half_gain * (
                    PR[par, q, i + 2, after, :] - PR[par, q, i + 2, before, :]
                )
            return carry

        lax.fori_loop(0, cx * jbs, flow_yz, 0, unroll=4)

        def pressure(final, n, carry):
            i, jb = n // jbs, n % jbs
            rows = pl.ds(pl.multiple_of(jb * 16, 16), 16)
            at = pl.ds(pl.multiple_of(8 + jb * 16, 8), 16)
            after, before = pl.ds(9 + jb * 16, 16), pl.ds(7 + jb * 16, 16)
            slopes = slope_z([VZ[q, i, rows, :] for q in range(nq)])
            for q in range(nq):
                rise = (
                    (VX[q, i + 2, rows, :] - VX[q, i, rows, :])
                    + (VY[q, i, after, :] - VY[q, i, before, :])
                    + slopes[q]
                )
                row = pl.multiple_of((q // 2) * half + i * cy + jb * 16, 16)
                col = (q % 2) * LANES
                value = (
                    PR[par, q, i + 2, at, :]
                    - half_gain * rise
                    + SRC[pl.ds(row, 16), col : col + LANES]
                )
                if final:
                    p_out[i, rows, q * LANES : (q + 1) * LANES] = value
                else:
                    PR[new, q, i + 2, at, :] = value
                    keep_parts(i, jb, q, value)
            return carry

        @pl.when(t == STEPS - 1)
        def _():
            lax.fori_loop(0, cx * jbs, functools.partial(pressure, True), 0, unroll=4)

        @pl.when(t < STEPS - 1)
        def _():
            lax.fori_loop(0, cx * jbs, functools.partial(pressure, False), 0, unroll=4)

        @pl.when(t < STEPS - 1)
        def _():
            pack_rows(t + 1, new)
            start(lambda d: p_copy(t + 1, new, d))

        return carry

    lax.fori_loop(0, STEPS, step, 0)

    wait_taken(lambda d: dep_copy(STEPS - 1, d))
    keep = AMSK[...] > 0.0
    for k in range(2):
        for w in range(2):
            col = slice(w * LANES, (w + 1) * LANES)
            high, low = split(jnp.where(keep, AR[k, :, col], 0.0))
            to = slice(k * BLOCK + w * LANES, k * BLOCK + (w + 1) * LANES)
            CAT[0:ARRIVE, to] = high
            CAT[ARRIVE : 2 * ARRIVE, to] = low

    def finish(m, carry):
        rows = pl.ds(pl.multiple_of(m * LANES, LANES), LANES)
        placed = jnp.dot(PLACE[rows, :], CAT[...], preferred_element_type=f32)
        keep = MSK[rows, :]
        keep = jnp.concatenate([keep, keep], axis=1) >= float(STEPS)
        R[rows, :] = jnp.where(keep, R[rows, :], 0.0) + placed[:, :BLOCK]
        S[rows, :] = jnp.where(keep, S[rows, :], 0.0) + placed[:, BLOCK:]
        return carry

    lax.fori_loop(0, SLOT_BLOCKS, finish, 0)
    wait_sent(meta_copy)
    for t in range(STEPS):
        wait_sent(lambda d, t=t: dep_copy(t, d))


def write_out(p, vx, vy, vz, r, s, c, p_out, v_out, r_out, s_out, c_out, sems):
    _, cx, cy, nz = v_out.shape
    pairs = [(p, p_out), (r, r_out), (s, s_out), (c, c_out)]
    for q in range(nz // LANES):
        lanes = pl.ds(q * LANES, LANES)
        pairs.append((vx.at[q, pl.ds(1, cx), :, :], v_out.at[0, :, :, lanes]))
        pairs.append((vy.at[q, :, pl.ds(8, cy), :], v_out.at[1, :, :, lanes]))
        pairs.append((vz.at[q], v_out.at[2, :, :, lanes]))
    copies = [pltpu.make_async_copy(a, b, sems.at[k]) for k, (a, b) in enumerate(pairs)]
    for copy in copies:
        copy.start()
    for copy in copies:
        copy.wait()


def on_device(
    pressure, velocity, stretch, rest_radius, wall_speed, block_cells, depart_slot, depart_way
):
    cx, cy, nz = pressure.shape
    nq = nz // LANES
    ncol = 2 * cx * cy
    vmem = pl.BlockSpec(memory_space=pltpu.VMEM)
    hbm = pl.BlockSpec(memory_space=pl.ANY)
    dma = pltpu.SemaphoreType.DMA
    vmem_out = pltpu.VMEM
    parts = pl.pallas_call(
        kernel,
        out_shape=(
            vmem_out(pressure.shape, f32),
            vmem_out((nq, cx + 2, cy, LANES), f32),
            vmem_out((nq, cx, cy + 16, LANES), f32),
            vmem_out((nq, cx, cy, LANES), f32),
            vmem_out((SLOTS, BLOCK), f32),
            vmem_out((SLOTS, BLOCK), f32),
            vmem_out((SLOT_BLOCKS, LANES), jnp.int32),
        ),
        in_specs=[pl.BlockSpec(memory_space=pltpu.HBM)] * 9,
        out_specs=(vmem,) * 7,
        scratch_shapes=[
            pltpu.VMEM((2, nq, cx + 4, cy + 16, LANES), f32),
            pltpu.VMEM((SLOTS, BLOCK), f32),
            pltpu.VMEM((3, ARRIVE, BLOCK), f32),
            pltpu.VMEM((STEPS, 3, DEP, BLOCK), f32),
            pltpu.VMEM((ROWS, ncol), bf16),
            pltpu.VMEM((ncol, ROWS), bf16),
            pltpu.VMEM((2 * ncol, BLOCK), bf16),
            pltpu.VMEM((ROWS, BLOCK), f32),
            pltpu.VMEM((2 * ROWS, BLOCK), bf16),
            pltpu.VMEM((ncol, BLOCK), f32),
            pltpu.VMEM((STEPS, 2, nq, cx, 2, LANES), f32),
            pltpu.VMEM((STEPS, 2, nq, cx, 2, LANES), f32),
            pltpu.VMEM((2, nq, cx, 1, LANES), f32),
            pltpu.VMEM((2, nq, cx, 1, LANES), f32),
            pltpu.VMEM((8, LANES), f32),
            pltpu.VMEM((4, 8, LANES), f32),
            pltpu.VMEM((SLOTS, LANES), f32),
            pltpu.VMEM((ARRIVE, LANES), f32),
            pltpu.VMEM((LANES, LANES), f32),
            pltpu.VMEM((16, LANES), f32),
            pltpu.VMEM((SLOTS, 2 * ARRIVE), bf16),
            pltpu.VMEM((2 * ARRIVE, 2 * BLOCK), bf16),
            pltpu.SMEM((SLOTS,), jnp.int32),
            pltpu.SMEM((STEPS, 1, 1, DEP), jnp.int32),
            pltpu.SMEM((STEPS, 1, 1, DEP), jnp.int32),
            pltpu.VMEM((SLOT_BLOCKS, LANES), jnp.int32),
            dma((4 * nq + 7,)),
            dma((4,)),
            dma((4,)),
            dma((STEPS, 4)),
            dma((STEPS, 4)),
            dma((4,)),
            dma((4,)),
            dma((STEPS, 4)),
            dma((STEPS, 4)),
        ],
        compiler_params=pltpu.CompilerParams(
            collective_id=0, has_side_effects=True, vmem_limit_bytes=36 * 2**20
        ),
        cost_estimate=pl.CostEstimate(
            flops=10 * 2**30, bytes_accessed=13 * 2**20, transcendentals=2**22
        ),
    )(
        *(
            pltpu.with_memory_space_constraint(value, pltpu.HBM)
            for value in (
                block_cells,
                depart_slot,
                depart_way,
                block_cells.reshape(SLOT_BLOCKS, LANES),
                pressure,
                velocity,
                stretch,
                rest_radius,
                wall_speed,
            )
        )
    )
    parts = [pltpu.with_memory_space_constraint(part, pltpu.VMEM) for part in parts]
    p, v, r, s, c = pl.pallas_call(
        write_out,
        out_shape=(
            jax.ShapeDtypeStruct(pressure.shape, f32),
            jax.ShapeDtypeStruct(velocity.shape, f32),
            jax.ShapeDtypeStruct(stretch.shape, f32),
            jax.ShapeDtypeStruct(stretch.shape, f32),
            jax.ShapeDtypeStruct((SLOT_BLOCKS, LANES), jnp.int32),
        ),
        in_specs=[vmem] * 7,
        out_specs=(hbm,) * 5,
        scratch_shapes=[dma((3 * nq + 4,))],
        compiler_params=pltpu.CompilerParams(vmem_limit_bytes=4 * 2**20),
        cost_estimate=pl.CostEstimate(flops=0, bytes_accessed=13 * 2**20, transcendentals=0),
    )(*parts)
    return p, v, r, s, c.reshape(-1)


def solution(mesh):
    placed = (
        P("gx", "gy", None),
        P(None, "gx", "gy", None),
        P(("gx", "gy"), None),
        P(("gx", "gy"), None),
        P(("gx", "gy"), None),
        P(("gx", "gy")),
        P(None, "gx", "gy", None),
        P(None, "gx", "gy", None),
    )
    return jax.shard_map(
        on_device,
        mesh=mesh,
        in_specs=placed,
        out_specs=(
            P("gx", "gy", None),
            P(None, "gx", "gy", None),
            P(("gx", "gy"), None),
            P(("gx", "gy"), None),
            P(("gx", "gy")),
        ),
        check_vma=False,
    )
```

profile of v0, /device:TPU:1, one launch (start us, length us, event | category | flops | bytes accessed | tf_op | source)
XLA Modules:
  0.0 61.5 jit_solution(1921582796185663308)
XLA Ops:
  0.6 58.1 %shard_map.119 = (f32[16,32,512]{2,1,0:T(8,128)S(1)}, f32[4,18,32,128]{3,2,1,0:T(8,128)S(1)}, f32[4,16,48,128]{3,2,1,0:T(8,128)S(1)}, f32[4,16,32,128]{3,2,1,0:T...) custom-call(s32[1024]{0:T(1024)} %cells_h.1, s32[4,1,1,8]{3,2,1,0:T(1,128)} %slot_h.1, ...), custom_call_target="tpu_custom_call" | custom-call | flops 10737418240 | bytes 13631488 | tf_op jit(solution)/shard_map/pallas_call | solution.py:565
  58.7 2.8 %shard_map.120 = (f32[16,32,512]{2,1,0:T(8,128)}, f32[3,16,32,512]{3,2,1,0:T(8,128)}, f32[1024,256]{1,0:T(8,128)}, f32[1024,256]{1,0:T(8,128)}, s32[8,128]{1,0:T(8,128)}) custom-call(f32[16,32,512]{2,1,0:T(8,128)S(1)} %get-tuple-element.17.p, f32[4,18,32,128]{3,2,1,0:T(8,128)S(1)} %get-tuple-element.18.vx, f32[4,16,48,128]{3,2,1,0:T(8,128)S(1)} %get-tuple-element.19.vy, ...), custom_call_target="tpu_custom_call" | custom-call | bytes 13631488 | tf_op jit(solution)/shard_map/pallas_call | solution.py:638
where the time goes:
time: 61.8 us; the launch traced here: 61.5 us
  Pallas kernels  60.9 us (99%)
  between operations  0.64 us (1%)
    pallas_call x1, Pallas kernels, on_device(): pl.pallas_call(kernel, out_shape=(vmem_out(pressure.shape, f32), vmem_out...  58.1 us
    pallas_call x1, Pallas kernels, on_device(): pl.pallas_call(write_out, out_shape=(jax.ShapeDtypeStruct(pressure.shape,...  2.78 us

commit v1 on v0

--- a/solution.py
+++ b/solution.py
@@ -50,8 +50,8 @@
 
 def kernel(
     cells_h, slot_h, way_h, cells_b, press, vel, stretch, rest, speed0,
-    p_out, VX, VY, VZ, R, S, c_out,
-    PR, A, AR, SB, OH, OHT, PHL, PG, VHL, SRC, YS, YR, VYS, VYR,
+    PR, VX, VY, VZ, R, S, c_out,
+    A, AR, SB, OH, OHT, PHL, PG, VHL, SRC, XR, YS, YR, VYS, VYR,
     MT, MR, MSK, AMSK, LT, LR, PLACE, CAT, cells_s, slot_s, way_s, cells_v,
     in_sem, meta_s, meta_r, xs, xr, vs, vr, ds_, dr,
 ):
@@ -60,6 +60,11 @@
     half = cx * cy
     ncol = 2 * half
     jbs = cy // 16
+    part = min(256, ncol)
+    planes = part // (2 * cy)
+    groups = cx // planes
+    shift = (planes * cy).bit_length() - 1
+    zero_row = lax.axis_index("gx") // 4096
     gx, gy = lax.axis_index("gx"), lax.axis_index("gy")
     ngx, ngy = lax.axis_size("gx"), lax.axis_size("gy")
     has_lo, has_hi = gy > 0, gy < ngy - 1
@@ -89,7 +94,7 @@
 
     inputs = [(cells_h, cells_s), (slot_h, slot_s), (way_h, way_s), (cells_b, cells_v)]
     for q in range(nq):
-        inputs.append((press.at[:, :, pl.ds(q * LANES, LANES)], PR.at[0, q, pl.ds(2, cx), pl.ds(8, cy), :]))
+        inputs.append((press.at[:, :, pl.ds(q * LANES, LANES)], PR.at[q, :, pl.ds(8, cy), :]))
     inputs.append((rest, A))
     inputs.append((stretch, R))
     inputs.append((speed0, S))
@@ -148,13 +153,11 @@
     def meta_copy(d):
         return remote(MT, MR.at[d], meta_s.at[d], meta_r.at[d], d)
 
-    def p_copy(t, par, d):
+    def p_copy(t, d):
         if d < 2:
-            src = PR.at[par, :, pl.ds((cx, 2)[d], 2), pl.ds(8, cy), :]
-            dst = PR.at[par, :, pl.ds((0, cx + 2)[d], 2), pl.ds(8, cy), :]
-        else:
-            src, dst = YS.at[t, 3 - d], YR.at[t, d - 2]
-        return remote(src, dst, xs.at[t, d], xr.at[t, d], d)
+            src = PR.at[:, pl.ds((cx - 2, 0)[d], 2), pl.ds(8, cy), :]
+            return remote(src, XR.at[t, d], xs.at[t, d], xr.at[t, d], d)
+        return remote(YS.at[t, 3 - d], YR.at[t, d - 2], xs.at[t, d], xr.at[t, d], d)
 
     def v_copy(d):
         if d < 2:
@@ -183,34 +186,45 @@
 
     start(meta_copy)
 
-    def pack_rows(t, par):
-        def body(i, carry):
+    def pack_rows(t):
+        for i in range(cx):
             for q in range(nq):
-                YS[t, 0, q, i] = PR[par, q, i + 2, 8:10, :]
-                YS[t, 1, q, i] = PR[par, q, i + 2, 6 + cy : 8 + cy, :]
-            return carry
-
-        lax.fori_loop(0, cx, body, 0, unroll=4)
+                YS[t, 0, q, i] = PR[q, i, 8:10, :]
+                YS[t, 1, q, i] = PR[q, i, 6 + cy : 8 + cy, :]
+
+    def column_row(i, h, jb):
+        return (i // planes) * part + (h * planes + i % planes) * cy + jb * 16
 
     def keep_parts(i, jb, q, value):
         high, low = split(value)
-        row = pl.multiple_of((q // 2) * half + i * cy + jb * 16, 16)
+        row = column_row(i, q // 2, jb)
         col = (q % 2) * LANES
-        PHL[pl.ds(row, 16), col : col + LANES] = high
-        PHL[pl.ds(pl.multiple_of(row + ncol, 16), 16), col : col + LANES] = low
+        PHL[row : row + 16, col : col + LANES] = high
+        PHL[row + ncol : row + ncol + 16, col : col + LANES] = low
+
+    def rows_of(jb):
+        return slice(jb * 16, jb * 16 + 16), slice(8 + jb * 16, 24 + jb * 16)
 
     for k in range(nq):
         loads[k].wait()
-    pack_rows(0, 0)
-    start(lambda d: p_copy(0, 0, d))
-
-    def first_split(n, carry):
-        i, jb = n // jbs, n % jbs
+    pack_rows(0)
+    start(lambda d: p_copy(0, d))
+    for i in range(cx):
+        for jb in range(jbs):
+            for q in range(nq):
+                keep_parts(i, jb, q, PR[q, i, rows_of(jb)[1], :])
+
+    for k in range(nq + 3, nq + 3 + 3 * nq):
+        loads[k].wait()
+
+    def pack_flow(i, carry):
         for q in range(nq):
-            keep_parts(i, jb, q, PR[0, q, i + 2, pl.ds(pl.multiple_of(8 + jb * 16, 8), 16), :])
+            VYS[0, q, i] = VY[q, i, 8:9, :]
+            VYS[1, q, i] = VY[q, i, 7 + cy : 8 + cy, :]
         return carry
 
-    lax.fori_loop(0, cx * jbs, first_split, 0, unroll=4)
+    lax.fori_loop(0, cx, pack_flow, 0, unroll=4)
+    start(v_copy)
 
     for k in range(nq, nq + 3):
         loads[k].wait()
@@ -225,18 +239,6 @@
     lax.fori_loop(0, SLOTS // 16, first_state, 0, unroll=4)
     VHL[pl.ds(SLOTS, ARRIVE), :] = jnp.zeros((ARRIVE, BLOCK), bf16)
     VHL[pl.ds(ROWS + SLOTS, ARRIVE), :] = jnp.zeros((ARRIVE, BLOCK), bf16)
-
-    for k in range(nq + 3, nq + 3 + 3 * nq):
-        loads[k].wait()
-
-    def pack_flow(i, carry):
-        for q in range(nq):
-            VYS[0, q, i] = VY[q, i, 8:9, :]
-            VYS[1, q, i] = VY[q, i, 7 + cy : 8 + cy, :]
-        return carry
-
-    lax.fori_loop(0, cx, pack_flow, 0, unroll=4)
-    start(v_copy)
 
     wait_taken(meta_copy)
     came = (lane8 // DEP) % 4
@@ -268,7 +270,9 @@
 
     def code_of(lab):
         cell = lab - 1
-        return jnp.where(lab > 0, (cell & 1) * half + (cell >> 1), -1).astype(f32)
+        place = cell >> 1
+        row = (place >> shift) * part + (cell & 1) * (planes * cy)
+        return jnp.where(lab > 0, row + (place & (planes * cy - 1)), -1).astype(f32)
 
     code = code_of(label)
     acode = code_of(alab.astype(jnp.int32))
@@ -341,30 +345,23 @@
 
     low_gate = jnp.where(has_lo, 1.0, 0.0).astype(f32)
     high_gate = jnp.where(has_hi, 1.0, 0.0).astype(f32)
-    chunk = 384
-    part = min(256, ncol)
+    chunk = 256
+
+    def gather(low_row, count):
+        hot = OH[low_row : low_row + count, :]
+        hot = jnp.concatenate([hot, hot], axis=1)
+        PG[low_row : low_row + count, :] = jnp.dot(hot, PHL[...], preferred_element_type=f32)
+
+    def scatter(m):
+        hot = OHT[m * part : (m + 1) * part, :]
+        hot = jnp.concatenate([hot, hot], axis=1)
+        SRC[m * part : (m + 1) * part, :] = jnp.dot(hot, VHL[...], preferred_element_type=f32)
 
     def step(t, carry):
-        par = lax.rem(t, 2)
-        new = 1 - par
-
-        def gather(m, carry):
-            rows = pl.ds(pl.multiple_of(m * chunk, chunk), chunk)
-            hot = OH[rows, :]
-            hot = jnp.concatenate([hot, hot], axis=1)
-            PG[rows, :] = jnp.dot(hot, PHL[...], preferred_element_type=f32)
-            return carry
-
-        lax.fori_loop(0, ROWS // chunk, gather, 0)
-
-        @pl.when(t > 0)
-        def _():
-            wait_taken(lambda d: dep_copy(t - 1, d))
-
         limit = t.astype(f32)
 
-        def bubbles(n, carry):
-            rows = pl.ds(pl.multiple_of(n * 16, 16), 16)
+        def bubbles(first):
+            rows = slice(first, first + 16)
             radius, speed, rate = wall_update(R[rows, :], S[rows, :], A[rows, :], PG[rows, :])
             R[rows, :] = radius
             S[rows, :] = speed
@@ -372,10 +369,16 @@
             keep = jnp.concatenate([keep, keep], axis=1) >= limit
             high, low = split(jnp.where(keep, rate, 0.0))
             VHL[rows, :] = high
-            VHL[pl.ds(pl.multiple_of(ROWS + n * 16, 16), 16), :] = low
-            return carry
-
-        lax.fori_loop(0, SLOTS // 16, bubbles, 0, unroll=4)
+            VHL[ROWS + first : ROWS + first + 16, :] = low
+
+        gather(0, chunk)
+        for m in range(SLOTS // chunk):
+            if m + 1 < SLOTS // chunk:
+                gather((m + 1) * chunk, chunk)
+            else:
+                gather(SLOTS, ARRIVE)
+            for b in range(chunk // 16):
+                bubbles(m * chunk + b * 16)
 
         for k in range(DEP):
             row = pl.ds(jnp.maximum(slot_s[t, 0, 0, k], 0), 1)
@@ -384,129 +387,124 @@
             SB[t, 2, k : k + 1, :] = A[row, :]
         start(lambda d: dep_copy(t, d))
 
+        @pl.when(t > 0)
+        def _():
+            wait_taken(lambda d: dep_copy(t - 1, d))
+
         def arrived(n, carry):
-            rows = pl.ds(pl.multiple_of(n * 16, 16), 16)
-            low_rows = pl.ds(pl.multiple_of(SLOTS + n * 16, 16), 16)
-            radius, speed, rate = wall_update(
-                AR[0, rows, :], AR[1, rows, :], AR[2, rows, :], PG[low_rows, :]
-            )
-            AR[0, rows, :] = radius
-            AR[1, rows, :] = speed
-            keep = AMSK[rows, :]
-            keep = jnp.concatenate([keep, keep], axis=1) > 0.0
-            high, low = split(jnp.where(keep, rate, 0.0))
-            VHL[low_rows, :] = high
-            VHL[pl.ds(pl.multiple_of(ROWS + SLOTS + n * 16, 16), 16), :] = low
+            for b in range(2):
+                first = n * 32 + b * 16
+                rows = pl.ds(pl.multiple_of(first, 16), 16)
+                low_rows = pl.ds(pl.multiple_of(SLOTS + first, 16), 16)
+                radius, speed, rate = wall_update(
+                    AR[0, rows, :], AR[1, rows, :], AR[2, rows, :], PG[low_rows, :]
+                )
+                AR[0, rows, :] = radius
+                AR[1, rows, :] = speed
+                keep = AMSK[rows, :]
+                keep = jnp.concatenate([keep, keep], axis=1) > 0.0
+                high, low = split(jnp.where(keep, rate, 0.0))
+                VHL[low_rows, :] = high
+                VHL[pl.ds(pl.multiple_of(ROWS + SLOTS + first, 16), 16), :] = low
             return carry
 
-        lax.fori_loop(0, 2 * t, arrived, 0)
-
-        def scatter(m, carry):
-            rows = pl.ds(pl.multiple_of(m * part, part), part)
-            hot = OHT[rows, :]
-            hot = jnp.concatenate([hot, hot], axis=1)
-            SRC[rows, :] = jnp.dot(hot, VHL[...], preferred_element_type=f32)
-            return carry
-
-        lax.fori_loop(0, ncol // part, scatter, 0)
-
-        wait_taken(lambda d: p_copy(t, par, d))
-        wait_sent(lambda d: p_copy(t, par, d))
+        lax.fori_loop(0, t, arrived, 0)
+
+        def flow_x(i, after, before):
+            for q in range(nq):
+                for jb in range(jbs):
+                    rows, at = rows_of(jb)
+                    ahead = PR[q, i + 1, at, :] if after is None else XR[t, 1, q, after, rows, :]
+                    back = PR[q, i - 1, at, :] if before is None else XR[t, 0, q, before, rows, :]
+                    VX[q, i + 1, rows, :] = VX[q, i + 1, rows, :] - half_gain * (ahead - back)
+
+        def flow_z(i, jb):
+            rows, at = rows_of(jb)
+            slopes = slope_z([PR[q, i, at, :] for q in range(nq)])
+            for q in range(nq):
+                VZ[q, i, rows, :] = VZ[q, i, rows, :] - half_gain * slopes[q]
+
+        def flow_y(i, jb):
+            _, at = rows_of(jb)
+            for q in range(nq):
+                VY[q, i, at, :] = VY[q, i, at, :] - half_gain * (
+                    PR[q, i, pl.ds(9 + jb * 16 + zero_row, 16), :]
+                    - PR[q, i, pl.ds(7 + jb * 16 + zero_row, 16), :]
+                )
+
+        def side_rows(i):
+            for q in range(nq):
+                below, above = YR[t, 0, q, i], YR[t, 1, q, i]
+                PR[q, i, 6:8, :] = below
+                PR[q, i, 8 + cy : 10 + cy, :] = above
+                VY[q, i, 7:8, :] = low_gate * (
+                    VY[q, i, 7:8, :] - half_gain * (PR[q, i, 8:9, :] - below[0:1, :])
+                )
+                VY[q, i, 8 + cy : 9 + cy, :] = high_gate * (
+                    VY[q, i, 8 + cy : 9 + cy, :]
+                    - half_gain * (above[1:2, :] - PR[q, i, 7 + cy : 8 + cy, :])
+                )
+
+        def pressure(i, jb):
+            rows, at = rows_of(jb)
+            slopes = slope_z([VZ[q, i, rows, :] for q in range(nq)])
+            for q in range(nq):
+                rise = (
+                    (VX[q, i + 2, rows, :] - VX[q, i, rows, :])
+                    + (
+                        VY[q, i, pl.ds(9 + jb * 16 + zero_row, 16), :]
+                        - VY[q, i, pl.ds(7 + jb * 16 + zero_row, 16), :]
+                    )
+                    + slopes[q]
+                )
+                row = column_row(i, q // 2, jb)
+                col = (q % 2) * LANES
+                value = PR[q, i, at, :] - half_gain * rise + SRC[row : row + 16, col : col + LANES]
+                PR[q, i, at, :] = value
+                keep_parts(i, jb, q, value)
+
+        early = max(1, groups // 2)
+        for m in range(early):
+            scatter(m)
+            for i in range(m * cx // early, (m + 1) * cx // early):
+                if 0 < i < cx - 1:
+                    flow_x(i, None, None)
+                for jb in range(jbs):
+                    flow_z(i, jb)
+
+        wait_taken(lambda d: p_copy(t, d))
+        wait_sent(lambda d: p_copy(t, d))
 
         @pl.when(t == 0)
         def _():
             wait_taken(v_copy)
             wait_sent(v_copy)
-
-            def unpack(i, carry):
+            for i in range(cx):
                 for q in range(nq):
                     VY[q, i, 7:8, :] = VYR[0, q, i]
                     VY[q, i, 8 + cy : 9 + cy, :] = VYR[1, q, i]
-                return carry
-
-            lax.fori_loop(0, cx, unpack, 0)
-
-        def flow_x(n, carry):
-            i, jb = n // jbs, n % jbs
-            rows = pl.ds(pl.multiple_of(jb * 16, 16), 16)
-            at = pl.ds(pl.multiple_of(8 + jb * 16, 8), 16)
-            for q in range(nq):
-                VX[q, i, rows, :] = VX[q, i, rows, :] - half_gain * (
-                    PR[par, q, i + 2, at, :] - PR[par, q, i, at, :]
-                )
-            return carry
-
-        lax.fori_loop(0, (cx + 2) * jbs, flow_x, 0, unroll=4)
-
-        def side_rows(i, carry):
-            for q in range(nq):
-                PR[par, q, i + 2, 6:8, :] = YR[t, 0, q, i]
-                PR[par, q, i + 2, 8 + cy : 10 + cy, :] = YR[t, 1, q, i]
-                VY[q, i, 7:8, :] = low_gate * (
-                    VY[q, i, 7:8, :]
-                    - half_gain * (PR[par, q, i + 2, 8:9, :] - YR[t, 0, q, i, 0:1, :])
-                )
-                VY[q, i, 8 + cy : 9 + cy, :] = high_gate * (
-                    VY[q, i, 8 + cy : 9 + cy, :]
-                    - half_gain * (YR[t, 1, q, i, 1:2, :] - PR[par, q, i + 2, 7 + cy : 8 + cy, :])
-                )
-            return carry
-
-        lax.fori_loop(0, cx, side_rows, 0, unroll=4)
-
-        def flow_yz(n, carry):
-            i, jb = n // jbs, n % jbs
-            rows = pl.ds(pl.multiple_of(jb * 16, 16), 16)
-            at = pl.ds(pl.multiple_of(8 + jb * 16, 8), 16)
-            after, before = pl.ds(9 + jb * 16, 16), pl.ds(7 + jb * 16, 16)
-            slopes = slope_z([PR[par, q, i + 2, at, :] for q in range(nq)])
-            for q in range(nq):
-                VZ[q, i, rows, :] = VZ[q, i, rows, :] - half_gain * slopes[q]
-                VY[q, i, at, :] = VY[q, i, at, :] - half_gain * (
-                    PR[par, q, i + 2, after, :] - PR[par, q, i + 2, before, :]
-                )
-            return carry
-
-        lax.fori_loop(0, cx * jbs, flow_yz, 0, unroll=4)
-
-        def pressure(final, n, carry):
-            i, jb = n // jbs, n % jbs
-            rows = pl.ds(pl.multiple_of(jb * 16, 16), 16)
-            at = pl.ds(pl.multiple_of(8 + jb * 16, 8), 16)
-            after, before = pl.ds(9 + jb * 16, 16), pl.ds(7 + jb * 16, 16)
-            slopes = slope_z([VZ[q, i, rows, :] for q in range(nq)])
-            for q in range(nq):
-                rise = (
-                    (VX[q, i + 2, rows, :] - VX[q, i, rows, :])
-                    + (VY[q, i, after, :] - VY[q, i, before, :])
-                    + slopes[q]
-                )
-                row = pl.multiple_of((q // 2) * half + i * cy + jb * 16, 16)
-                col = (q % 2) * LANES
-                value = (
-                    PR[par, q, i + 2, at, :]
-                    - half_gain * rise
-                    + SRC[pl.ds(row, 16), col : col + LANES]
-                )
-                if final:
-                    p_out[i, rows, q * LANES : (q + 1) * LANES] = value
-                else:
-                    PR[new, q, i + 2, at, :] = value
-                    keep_parts(i, jb, q, value)
-            return carry
-
-        @pl.when(t == STEPS - 1)
-        def _():
-            lax.fori_loop(0, cx * jbs, functools.partial(pressure, True), 0, unroll=4)
+
+        if early < groups:
+            scatter(early)
+        flow_x(-1, None, 0)
+        flow_x(0, None, 1)
+        flow_x(cx - 1, 0, None)
+        flow_x(cx, 1, None)
+        for i in range(cx):
+            side_rows(i)
+            for jb in range(jbs):
+                flow_y(i, jb)
+        for m in range(groups):
+            if early < m + 1 < groups:
+                scatter(m + 1)
+            for i in range(m * planes, (m + 1) * planes):
+                for jb in range(jbs):
+                    pressure(i, jb)
 
         @pl.when(t < STEPS - 1)
         def _():
-            lax.fori_loop(0, cx * jbs, functools.partial(pressure, False), 0, unroll=4)
-
-        @pl.when(t < STEPS - 1)
-        def _():
-            pack_rows(t + 1, new)
-            start(lambda d: p_copy(t + 1, new, d))
+            pack_rows(t + 1)
+            start(lambda d: p_copy(t + 1, d))
 
         return carry
 
@@ -539,12 +537,13 @@
 
 def write_out(p, vx, vy, vz, r, s, c, p_out, v_out, r_out, s_out, c_out, sems):
     _, cx, cy, nz = v_out.shape
-    pairs = [(p, p_out), (r, r_out), (s, s_out), (c, c_out)]
+    pairs = [(r, r_out), (s, s_out), (c, c_out)]
     for q in range(nz // LANES):
         lanes = pl.ds(q * LANES, LANES)
         pairs.append((vx.at[q, pl.ds(1, cx), :, :], v_out.at[0, :, :, lanes]))
         pairs.append((vy.at[q, :, pl.ds(8, cy), :], v_out.at[1, :, :, lanes]))
         pairs.append((vz.at[q], v_out.at[2, :, :, lanes]))
+        pairs.append((p.at[q, :, pl.ds(8, cy), :], p_out.at[:, :, lanes]))
     copies = [pltpu.make_async_copy(a, b, sems.at[k]) for k, (a, b) in enumerate(pairs)]
     for copy in copies:
         copy.start()
@@ -565,7 +564,7 @@
     parts = pl.pallas_call(
         kernel,
         out_shape=(
-            vmem_out(pressure.shape, f32),
+            vmem_out((nq, cx, cy + 16, LANES), f32),
             vmem_out((nq, cx + 2, cy, LANES), f32),
             vmem_out((nq, cx, cy + 16, LANES), f32),
             vmem_out((nq, cx, cy, LANES), f32),
@@ -576,7 +575,6 @@
         in_specs=[pl.BlockSpec(memory_space=pltpu.HBM)] * 9,
         out_specs=(vmem,) * 7,
         scratch_shapes=[
-            pltpu.VMEM((2, nq, cx + 4, cy + 16, LANES), f32),
             pltpu.VMEM((SLOTS, BLOCK), f32),
             pltpu.VMEM((3, ARRIVE, BLOCK), f32),
             pltpu.VMEM((STEPS, 3, DEP, BLOCK), f32),
@@ -586,6 +584,7 @@
             pltpu.VMEM((ROWS, BLOCK), f32),
             pltpu.VMEM((2 * ROWS, BLOCK), bf16),
             pltpu.VMEM((ncol, BLOCK), f32),
+            pltpu.VMEM((STEPS, 2, nq, 2, cy, LANES), f32),
             pltpu.VMEM((STEPS, 2, nq, cx, 2, LANES), f32),
             pltpu.VMEM((STEPS, 2, nq, cx, 2, LANES), f32),
             pltpu.VMEM((2, nq, cx, 1, LANES), f32),
@@ -646,7 +645,7 @@
         ),
         in_specs=[vmem] * 7,
         out_specs=(hbm,) * 5,
-        scratch_shapes=[dma((3 * nq + 4,))],
+        scratch_shapes=[dma((4 * nq + 3,))],
         compiler_params=pltpu.CompilerParams(vmem_limit_bytes=4 * 2**20),
         cost_estimate=pl.CostEstimate(flops=0, bytes_accessed=13 * 2**20, transcendentals=0),
     )(*parts)

time: 61.8 us -> 50.1 us (0.81)
  the two profiles are of different devices: /device:TPU:1 before, /device:TPU:0 now
where the time goes in v1:
time: 50.1 us; the launch traced here: 50 us
  Pallas kernels  49.3 us (98%)
  between operations  0.64 us (1%)
    pallas_call x1, Pallas kernels, on_device(): pl.pallas_call(kernel, out_shape=(vmem_out((nq, cx, cy + 16, LANES), f32)...  46.5 us
    pallas_call x1, Pallas kernels, on_device(): pl.pallas_call(write_out, out_shape=(jax.ShapeDtypeStruct(pressure.shape,...  2.8 us

profile of v1, /device:TPU:0, one launch (start us, length us, event | category | flops | bytes accessed | tf_op | source)
XLA Modules:
  0.0 50.0 jit_solution(16431002904695455218)
XLA Ops:
  0.6 46.5 %shard_map.119 = (f32[4,16,48,128]{3,2,1,0:T(8,128)S(1)}, f32[4,18,32,128]{3,2,1,0:T(8,128)S(1)}, f32[4,16,48,128]{3,2,1,0:T(8,128)S(1)}, f32[4,16,32,128]{3,2,1...) custom-call(s32[1024]{0:T(1024)} %cells_h.1, s32[4,1,1,8]{3,2,1,0:T(1,128)} %slot_h.1, ...), custom_call_target="tpu_custom_call" | custom-call | flops 10737418240 | bytes 13631488 | tf_op jit(solution)/shard_map/pallas_call | solution.py:564
  47.2 2.8 %shard_map.120 = (f32[16,32,512]{2,1,0:T(8,128)}, f32[3,16,32,512]{3,2,1,0:T(8,128)}, f32[1024,256]{1,0:T(8,128)}, f32[1024,256]{1,0:T(8,128)}, s32[8,128]{1,0:T(8,128)}) custom-call(f32[4,16,48,128]{3,2,1,0:T(8,128)S(1)} %get-tuple-element.17.p, f32[4,18,32,128]{3,2,1,0:T(8,128)S(1)} %get-tuple-element.18.vx, f32[4,16,48,128]{3,2,1,0:T(8,128)S(1)} %get-tuple-element.19.vy, ...), custom_call_target="tpu_custom_call" | custom-call | bytes 13631488 | tf_op jit(solution)/shard_map/pallas_call | solution.py:637

commit v2 on v1

--- a/solution.py
+++ b/solution.py
@@ -53,7 +53,7 @@
     PR, VX, VY, VZ, R, S, c_out,
     A, AR, SB, OH, OHT, PHL, PG, VHL, SRC, XR, YS, YR, VYS, VYR,
     MT, MR, MSK, AMSK, LT, LR, PLACE, CAT, cells_s, slot_s, way_s, cells_v,
-    in_sem, meta_s, meta_r, xs, xr, vs, vr, ds_, dr,
+    in_sem, meta_s, meta_r, xs, xr, vs, vr, ds_, dr, fs, fr,
 ):
     _, cx, cy, nz = vel.shape
     nq = nz // LANES
@@ -142,6 +142,9 @@
         YR[:, 1] = jnp.zeros(YR.shape[:1] + YR.shape[2:], f32)
         VYR[1] = jnp.zeros(VYR.shape[1:], f32)
 
+    edge_rows = jnp.zeros((nq, cx, 8, LANES), f32)
+    PR[:, :, 0:8, :] = edge_rows
+    PR[:, :, 8 + cy : 16 + cy, :] = edge_rows
     pl.semaphore_wait(barrier, 2 + has_lo.astype(jnp.int32) + has_hi.astype(jnp.int32))
 
     def remote(src, dst, send_sem, recv_sem, d):
@@ -159,32 +162,47 @@
             return remote(src, XR.at[t, d], xs.at[t, d], xr.at[t, d], d)
         return remote(YS.at[t, 3 - d], YR.at[t, d - 2], xs.at[t, d], xr.at[t, d], d)
 
+    def first_copies(d):
+        side = (cx - 2, 0)[d]
+        for q in range(nq):
+            lanes = pl.ds(q * LANES, LANES)
+            yield remote(
+                press.at[pl.ds(side, 2), :, lanes], XR.at[0, d, q], fs.at[0, d, q], fr.at[0, d, q], d
+            )
+        for q in range(nq):
+            lanes = pl.ds(q * LANES, LANES)
+            yield remote(
+                vel.at[0, pl.ds((cx - 1, 0)[d], 1), :, lanes],
+                VX.at[q, pl.ds((0, cx + 1)[d], 1), :, :],
+                fs.at[1, d, q],
+                fr.at[1, d, q],
+                d,
+            )
+
     def v_copy(d):
-        if d < 2:
-            src = VX.at[:, pl.ds((cx, 1)[d], 1), :, :]
-            dst = VX.at[:, pl.ds((0, cx + 1)[d], 1), :, :]
-        else:
-            src, dst = VYS.at[3 - d], VYR.at[d - 2]
-        return remote(src, dst, vs.at[d], vr.at[d], d)
+        return remote(VYS.at[3 - d], VYR.at[d - 2], vs.at[d], vr.at[d], d)
 
     def dep_copy(t, d):
         return remote(
             SB.at[t], AR.at[:, pl.ds(t * 32 + d * DEP, DEP), :], ds_.at[t, d], dr.at[t, d], d
         )
 
-    def start(make):
-        for d in range(4):
+    def start(make, ways=(0, 1, 2, 3)):
+        for d in ways:
             under(sends[d], lambda d=d: make(d).start())
 
-    def wait_sent(make):
-        for d in range(4):
+    def wait_sent(make, ways=(0, 1, 2, 3)):
+        for d in ways:
             under(sends[d], lambda d=d: make(d).wait_send())
 
-    def wait_taken(make):
-        for d in range(4):
+    def wait_taken(make, ways=(0, 1, 2, 3)):
+        for d in ways:
             under(takes[d], lambda d=d: make(d).wait_recv())
 
     start(meta_copy)
+    for d in range(2):
+        for copy in first_copies(d):
+            copy.start()
 
     def pack_rows(t):
         for i in range(cx):
@@ -208,7 +226,7 @@
     for k in range(nq):
         loads[k].wait()
     pack_rows(0)
-    start(lambda d: p_copy(0, d))
+    start(lambda d: p_copy(0, d), (2, 3))
     for i in range(cx):
         for jb in range(jbs):
             for q in range(nq):
@@ -224,7 +242,7 @@
         return carry
 
     lax.fori_loop(0, cx, pack_flow, 0, unroll=4)
-    start(v_copy)
+    start(v_copy, (2, 3))
 
     for k in range(nq, nq + 3):
         loads[k].wait()
@@ -435,8 +453,10 @@
         def side_rows(i):
             for q in range(nq):
                 below, above = YR[t, 0, q, i], YR[t, 1, q, i]
-                PR[q, i, 6:8, :] = below
-                PR[q, i, 8 + cy : 10 + cy, :] = above
+                VY[q, i, 8:9, :] = VY[q, i, 8:9, :] + half_gain * below[1:2, :]
+                VY[q, i, 7 + cy : 8 + cy, :] = (
+                    VY[q, i, 7 + cy : 8 + cy, :] - half_gain * above[0:1, :]
+                )
                 VY[q, i, 7:8, :] = low_gate * (
                     VY[q, i, 7:8, :] - half_gain * (PR[q, i, 8:9, :] - below[0:1, :])
                 )
@@ -463,48 +483,68 @@
                 PR[q, i, at, :] = value
                 keep_parts(i, jb, q, value)
 
-        early = max(1, groups // 2)
-        for m in range(early):
+        order = [0, groups - 1] + list(range(1, groups - 1)) if groups > 1 else [0]
+        early = order[:2]
+        for k, m in enumerate(early):
             scatter(m)
-            for i in range(m * cx // early, (m + 1) * cx // early):
+            for i in range(k * cx // len(early), (k + 1) * cx // len(early)):
                 if 0 < i < cx - 1:
                     flow_x(i, None, None)
                 for jb in range(jbs):
                     flow_z(i, jb)
-
-        wait_taken(lambda d: p_copy(t, d))
-        wait_sent(lambda d: p_copy(t, d))
+                    flow_y(i, jb)
+
+        wait_taken(lambda d: p_copy(t, d), (2, 3))
+        wait_sent(lambda d: p_copy(t, d), (2, 3))
+
+        @pl.when(t > 0)
+        def _():
+            wait_taken(lambda d: p_copy(t, d), (0, 1))
+            wait_sent(lambda d: p_copy(t, d), (0, 1))
 
         @pl.when(t == 0)
         def _():
-            wait_taken(v_copy)
-            wait_sent(v_copy)
+            for d in range(2):
+                for copy in first_copies(d):
+                    copy.wait_recv()
+                    copy.wait_send()
+            wait_taken(v_copy, (2, 3))
+            wait_sent(v_copy, (2, 3))
             for i in range(cx):
                 for q in range(nq):
                     VY[q, i, 7:8, :] = VYR[0, q, i]
                     VY[q, i, 8 + cy : 9 + cy, :] = VYR[1, q, i]
 
-        if early < groups:
-            scatter(early)
         flow_x(-1, None, 0)
         flow_x(0, None, 1)
         flow_x(cx - 1, 0, None)
         flow_x(cx, 1, None)
-        for i in range(cx):
+        late = order[2:]
+        ends = [0, 1, cx - 2, cx - 1]
+        for m in late[:1]:
+            scatter(m)
+        for i in ends:
             side_rows(i)
             for jb in range(jbs):
-                flow_y(i, jb)
-        for m in range(groups):
-            if early < m + 1 < groups:
-                scatter(m + 1)
+                pressure(i, jb)
+
+        @pl.when(t < STEPS - 1)
+        def _():
+            start(lambda d: p_copy(t + 1, d), (0, 1))
+
+        for m in late[1:]:
+            scatter(m)
+        for m in order:
             for i in range(m * planes, (m + 1) * planes):
-                for jb in range(jbs):
-                    pressure(i, jb)
+                if i not in ends:
+                    side_rows(i)
+                    for jb in range(jbs):
+                        pressure(i, jb)
 
         @pl.when(t < STEPS - 1)
         def _():
             pack_rows(t + 1)
-            start(lambda d: p_copy(t + 1, d))
+            start(lambda d: p_copy(t + 1, d), (2, 3))
 
         return carry
 
@@ -610,6 +650,8 @@
             dma((4,)),
             dma((STEPS, 4)),
             dma((STEPS, 4)),
+            dma((2, 2, nq)),
+            dma((2, 2, nq)),
         ],
         compiler_params=pltpu.CompilerParams(
             collective_id=0, has_side_effects=True, vmem_limit_bytes=36 * 2**20

time: 50.1 us -> 50.1 us (level)
  no operation moved by 1% of the time
where the time goes in v2:
time: 50.1 us; the launch traced here: 50 us
  Pallas kernels  49.4 us (99%)
  between operations  0.64 us (1%)
    pallas_call x1, Pallas kernels, on_device(): pl.pallas_call(kernel, out_shape=(vmem_out((nq, cx, cy + 16, LANES), f32)...  46.6 us
    pallas_call x1, Pallas kernels, on_device(): pl.pallas_call(write_out, out_shape=(jax.ShapeDtypeStruct(pressure.shape,...  2.8 us

profile of v2, /device:TPU:0, one launch (start us, length us, event | category | flops | bytes accessed | tf_op | source)
XLA Modules:
  0.0 50.0 jit_solution(10909541392113119446)
XLA Ops:
  0.6 46.6 %shard_map.119 = (f32[4,16,48,128]{3,2,1,0:T(8,128)S(1)}, f32[4,18,32,128]{3,2,1,0:T(8,128)S(1)}, f32[4,16,48,128]{3,2,1,0:T(8,128)S(1)}, f32[4,16,32,128]{3,2,1...) custom-call(s32[1024]{0:T(1024)} %cells_h.1, s32[4,1,1,8]{3,2,1,0:T(1,128)} %slot_h.1, ...), custom_call_target="tpu_custom_call" | custom-call | flops 10737418240 | bytes 13631488 | tf_op jit(solution)/shard_map/pallas_call | solution.py:604
  47.2 2.8 %shard_map.120 = (f32[16,32,512]{2,1,0:T(8,128)}, f32[3,16,32,512]{3,2,1,0:T(8,128)}, f32[1024,256]{1,0:T(8,128)}, f32[1024,256]{1,0:T(8,128)}, s32[8,128]{1,0:T(8,128)}) custom-call(f32[4,16,48,128]{3,2,1,0:T(8,128)S(1)} %get-tuple-element.17.p, f32[4,18,32,128]{3,2,1,0:T(8,128)S(1)} %get-tuple-element.18.vx, f32[4,16,48,128]{3,2,1,0:T(8,128)S(1)} %get-tuple-element.19.vy, ...), custom_call_target="tpu_custom_call" | custom-call | bytes 13631488 | tf_op jit(solution)/shard_map/pallas_call | solution.py:679

commit v3 on v2

--- a/solution.py
+++ b/solution.py
@@ -34,18 +34,24 @@
     return high, (value - high.astype(f32)).astype(bf16)
 
 
-def wall_update(radius, speed, level, pressure):
-    one_less = 1.0 - 0.05 * speed
+def wall_update(radius, shift, level, pressure):
+    mach = (0.05 / time_step) * shift
+    one_less = 1.0 - mach
     divisor = one_less * radius
     inverse = pl.reciprocal(divisor, approx=True)
     inverse = inverse * (2.0 - divisor * inverse)
     inv_radius = inverse * one_less
     wall = jnp.exp2(level - (exponent * inv_ln2) * jnp.log(radius))
-    excess = wall - (0.2 + 0.08 * speed) * inv_radius - (1.0 + pressure)
-    driving = (2.0 - one_less) * excess - (1.0 + 0.5 * one_less) * (speed * speed)
-    speed = speed + time_step * (driving * inverse)
-    radius = radius + time_step * speed
-    return radius, speed, source_scale * (radius * radius) * speed
+    squared = time_step * time_step
+    excess = (
+        wall
+        - (0.2 * squared + (0.08 * time_step) * shift) * inv_radius
+        - (squared + squared * pressure)
+    )
+    driving = (1.0 + mach) * excess - (1.5 - 0.5 * mach) * (shift * shift)
+    shift = shift + driving * inverse
+    radius = radius + shift
+    return radius, shift, (source_scale / time_step) * (radius * radius) * shift
 
 
 def kernel(
@@ -109,26 +115,7 @@
     loads = [pltpu.make_async_copy(a, b, in_sem.at[k]) for k, (a, b) in enumerate(inputs)]
     for load in loads:
         load.start()
-
-    for load in loads[:4]:
-        load.wait()
-    loads = loads[4:]
-
-    lane8 = lax.broadcasted_iota(jnp.int32, (8, LANES), 1)
-    sub8 = lax.broadcasted_iota(jnp.int32, (8, LANES), 0)
-    slot_id = sub8 * LANES + lane8
-    label = cells_v[...] + 1
-    leave_at = jnp.where(label > 0, STEPS, -1)
-    entry_of = (lane8 // 32) * DEP + lane8 % DEP
-    wanted = (lane8 // DEP) % 4
-    wanted = jnp.where(wanted < 2, 1 - wanted, 5 - wanted)
-    meta = jnp.zeros((8, LANES), jnp.int32)
-    for e in range(STEPS * DEP):
-        slot = slot_s[e // DEP, 0, 0, e % DEP]
-        moved = jnp.where(slot >= 0, cells_s[jnp.maximum(slot, 0)] + 1, 0)
-        meta = jnp.where((entry_of == e) & (wanted == way_s[e // DEP, 0, 0, e % DEP]), moved, meta)
-        leave_at = jnp.where(slot_id == slot, e // DEP, leave_at)
-    MT[...] = meta.astype(f32)
+    small_loads, loads = loads[:4], loads[4:]
 
     @pl.when(jnp.logical_not(has_lo))
     def _():
@@ -145,6 +132,10 @@
     edge_rows = jnp.zeros((nq, cx, 8, LANES), f32)
     PR[:, :, 0:8, :] = edge_rows
     PR[:, :, 8 + cy : 16 + cy, :] = edge_rows
+    VHL[pl.ds(SLOTS, ARRIVE), :] = jnp.zeros((ARRIVE, BLOCK), bf16)
+    VHL[pl.ds(ROWS + SLOTS, ARRIVE), :] = jnp.zeros((ARRIVE, BLOCK), bf16)
+    OHT[:, SLOTS:ROWS] = jnp.zeros((ncol, ARRIVE), bf16)
+    OH[SLOTS:ROWS, :] = jnp.zeros((ARRIVE, ncol), bf16)
     pl.semaphore_wait(barrier, 2 + has_lo.astype(jnp.int32) + has_hi.astype(jnp.int32))
 
     def remote(src, dst, send_sem, recv_sem, d):
@@ -199,10 +190,29 @@
         for d in ways:
             under(takes[d], lambda d=d: make(d).wait_recv())
 
-    start(meta_copy)
     for d in range(2):
         for copy in first_copies(d):
             copy.start()
+    for load in small_loads:
+        load.wait()
+
+    lane8 = lax.broadcasted_iota(jnp.int32, (8, LANES), 1)
+    sub8 = lax.broadcasted_iota(jnp.int32, (8, LANES), 0)
+    slot_id = sub8 * LANES + lane8
+    label = cells_v[...] + 1
+    leave_at = jnp.where(label > 0, STEPS, -1)
+    entry_of = (lane8 // 32) * DEP + lane8 % DEP
+    wanted = (lane8 // DEP) % 4
+    wanted = jnp.where(wanted < 2, 1 - wanted, 5 - wanted)
+    meta = jnp.zeros((8, LANES), jnp.int32)
+    for e in range(STEPS * DEP):
+        slot = slot_s[e // DEP, 0, 0, e % DEP]
+        moved = jnp.where(slot >= 0, cells_s[jnp.maximum(slot, 0)] + 1, 0)
+        meta = jnp.where((entry_of == e) & (wanted == way_s[e // DEP, 0, 0, e % DEP]), moved, meta)
+        leave_at = jnp.where(slot_id == slot, e // DEP, leave_at)
+    MT[...] = meta.astype(f32)
+
+    start(meta_copy)
 
     def pack_rows(t):
         for i in range(cx):
@@ -223,14 +233,62 @@
     def rows_of(jb):
         return slice(jb * 16, jb * 16 + 16), slice(8 + jb * 16, 24 + jb * 16)
 
+    def split_all():
+        for i in range(cx):
+            for jb in range(jbs):
+                for q in range(nq):
+                    keep_parts(i, jb, q, PR[q, i, rows_of(jb)[1], :])
+
     for k in range(nq):
         loads[k].wait()
     pack_rows(0)
     start(lambda d: p_copy(0, d), (2, 3))
-    for i in range(cx):
-        for jb in range(jbs):
-            for q in range(nq):
-                keep_parts(i, jb, q, PR[q, i, rows_of(jb)[1], :])
+    split_all()
+
+    lrow = lax.broadcasted_iota(jnp.int32, (LANES, LANES), 0)
+    lcol = lax.broadcasted_iota(jnp.int32, (LANES, LANES), 1)
+    wide = lax.broadcasted_iota(jnp.int32, (16, ncol), 1).astype(f32)
+
+    def code_of(lab):
+        cell = lab - 1
+        place = cell >> 1
+        row = (place >> shift) * part + (cell & 1) * (planes * cy)
+        return jnp.where(lab > 0, row + (place & (planes * cy - 1)), -1).astype(f32)
+
+    def turn(stack):
+        stack = stack + [jnp.zeros((8, LANES), f32)] * (16 - len(stack))
+        LT[...] = jnp.concatenate(stack, axis=0).T
+
+    def hot_rows(r, at):
+        def body(m, carry):
+            rows = pl.ds(pl.multiple_of(m * 16, 16), 16)
+            hot = jnp.where(LT[rows, at : at + 1] == wide, 1.0, 0.0).astype(bf16)
+            OH[pl.ds(pl.multiple_of(r * LANES + m * 16, 16), 16), :] = hot
+            return carry
+
+        lax.fori_loop(0, LANES // 16, body, 0, unroll=4)
+
+    def hot_columns(first, last):
+        def body(m, carry):
+            ident = (lrow + m * LANES).astype(f32)
+            rows = pl.ds(pl.multiple_of(m * LANES, LANES), LANES)
+            for r in range(first, last):
+                hot = jnp.where(ident == LR[r : r + 1, :], 1.0, 0.0).astype(bf16)
+                OHT[rows, r * LANES : (r + 1) * LANES] = hot
+            return carry
+
+        lax.fori_loop(0, ncol // LANES, body, 0)
+
+    code = code_of(label)
+    turn([code, leave_at.astype(f32)])
+    LR[0:8, :] = code
+    for r in range(SLOT_BLOCKS):
+        hot_rows(r, r)
+    for r in range(SLOT_BLOCKS):
+        MSK[r * LANES : (r + 1) * LANES, :] = jnp.broadcast_to(
+            LT[:, 8 + r : 9 + r], (LANES, LANES)
+        )
+    hot_columns(0, SLOT_BLOCKS)
 
     for k in range(nq + 3, nq + 3 + 3 * nq):
         loads[k].wait()
@@ -251,113 +309,73 @@
         rows = pl.ds(pl.multiple_of(n * 16, 16), 16)
         rest_now = A[rows, :]
         R[rows, :] = R[rows, :] * rest_now
-        A[rows, :] = inv_ln2 * (jnp.log(1.0 + 0.2 / rest_now) + exponent * jnp.log(rest_now))
+        S[rows, :] = time_step * S[rows, :]
+        A[rows, :] = inv_ln2 * (
+            jnp.log((time_step * time_step) * (1.0 + 0.2 / rest_now))
+            + exponent * jnp.log(rest_now)
+        )
         return carry
 
     lax.fori_loop(0, SLOTS // 16, first_state, 0, unroll=4)
-    VHL[pl.ds(SLOTS, ARRIVE), :] = jnp.zeros((ARRIVE, BLOCK), bf16)
-    VHL[pl.ds(ROWS + SLOTS, ARRIVE), :] = jnp.zeros((ARRIVE, BLOCK), bf16)
-
-    wait_taken(meta_copy)
-    came = (lane8 // DEP) % 4
-    alab = jnp.where(
-        came == 0, MR[0], jnp.where(came == 1, MR[1], jnp.where(came == 2, MR[2], MR[3]))
-    )
-    present = alab > 0.0
-    lrow = lax.broadcasted_iota(jnp.int32, (LANES, LANES), 0)
-    lcol = lax.broadcasted_iota(jnp.int32, (LANES, LANES), 1)
-    upper = jnp.where(lrow <= lcol, 1.0, 0.0)
-    upper_block = jnp.where(lrow // 32 == lcol // 32, upper, 0.0).astype(bf16)
-    upper = upper.astype(bf16)
-    ones = jnp.ones((LANES, LANES), bf16)
-    present_f = jnp.where(present, 1.0, 0.0)
-    arank = jnp.dot(present_f.astype(bf16), upper_block, preferred_element_type=f32) - 1.0
-    arank = jnp.where(present, arank, -5.0)
-    vacant = label == 0
-    ranks = []
-    for t in range(STEPS):
-        vacant = vacant | (leave_at == t)
-        flag = jnp.where(vacant, 1.0, 0.0).astype(bf16)
-        rank = jnp.dot(flag, upper, preferred_element_type=f32) - 1.0
-        total = jnp.dot(flag, ones, preferred_element_type=f32)
-        for r in range(SLOT_BLOCKS - 1):
-            rank = rank + jnp.where(sub8 > r, total[r : r + 1, :], 0.0)
-        ranks.append(jnp.where(vacant, rank, -1.0))
-        count = jnp.sum(jnp.where(lane8 // 32 == t, present_f, 0.0), axis=1, keepdims=True)
-        vacant = vacant & (rank >= count)
-
-    def code_of(lab):
-        cell = lab - 1
-        place = cell >> 1
-        row = (place >> shift) * part + (cell & 1) * (planes * cy)
-        return jnp.where(lab > 0, row + (place & (planes * cy - 1)), -1).astype(f32)
-
-    code = code_of(label)
-    acode = code_of(alab.astype(jnp.int32))
-    stack = [code, leave_at.astype(f32)] + ranks + [acode, alab]
-    stack = stack + [jnp.zeros((8, LANES), f32)] * (16 - len(stack))
-    LT[...] = jnp.concatenate(stack, axis=0).T
-    LR[0:8, :] = code
-    LR[8:16, :] = acode
-
-    wide = lax.broadcasted_iota(jnp.int32, (16, ncol), 1).astype(f32)
-    for r in range(SLOT_BLOCKS + 1):
-        at = r if r < SLOT_BLOCKS else 48
-
-        def one_hot_rows(m, carry, r=r, at=at):
-            rows = pl.ds(pl.multiple_of(m * 16, 16), 16)
-            column = LT[rows, at : at + 1]
-            hot = jnp.where(column == wide, 1.0, 0.0).astype(bf16)
-            OH[pl.ds(pl.multiple_of(r * LANES + m * 16, 16), 16), :] = hot
-            return carry
-
-        lax.fori_loop(0, LANES // 16, one_hot_rows, 0, unroll=2)
-
-    tall = lax.broadcasted_iota(jnp.int32, (LANES, LANES), 0)
-
-    def one_hot_columns(m, carry):
-        ident = (tall + m * LANES).astype(f32)
-        rows = pl.ds(pl.multiple_of(m * LANES, LANES), LANES)
-        for r in range(SLOT_BLOCKS + 1):
-            hot = jnp.where(ident == LR[r : r + 1, :], 1.0, 0.0).astype(bf16)
-            OHT[rows, r * LANES : (r + 1) * LANES] = hot
-        return carry
-
-    lax.fori_loop(0, ncol // LANES, one_hot_columns, 0)
-
-    group = lcol // 32
-    for r in range(SLOT_BLOCKS):
-        MSK[r * LANES : (r + 1) * LANES, :] = jnp.broadcast_to(
-            LT[:, 8 + r : 9 + r], (LANES, LANES)
+    def plan():
+        wait_taken(meta_copy)
+        came = (lane8 // DEP) % 4
+        alab = jnp.where(
+            came == 0, MR[0], jnp.where(came == 1, MR[1], jnp.where(came == 2, MR[2], MR[3]))
         )
-        mine = jnp.broadcast_to(LT[:, 16 + r : 17 + r], (LANES, LANES))
-        for t in range(1, STEPS):
-            mine = jnp.where(group == t, LT[:, 16 + 8 * t + r : 17 + 8 * t + r], mine)
-        hot = jnp.where(mine == arank[0:1, :], 1.0, 0.0).astype(bf16)
-        PLACE[r * LANES : (r + 1) * LANES, 0:LANES] = hot
-        PLACE[r * LANES : (r + 1) * LANES, LANES : 2 * LANES] = hot
-    AMSK[...] = jnp.broadcast_to(LT[:, 56:57], (LANES, LANES))
-
-    alab_high, alab_low = split(alab)
-    final = jnp.where(leave_at == STEPS, label, 0).astype(f32)
-    for r in range(SLOT_BLOCKS):
-        hot = PLACE[r * LANES : (r + 1) * LANES, 0:LANES]
+        present = alab > 0.0
+        upper = jnp.where(lrow <= lcol, 1.0, 0.0)
+        upper_block = jnp.where(lrow // 32 == lcol // 32, upper, 0.0).astype(bf16)
+        upper = upper.astype(bf16)
+        ones = jnp.ones((LANES, LANES), bf16)
+        present_f = jnp.where(present, 1.0, 0.0)
+        arank = jnp.dot(present_f.astype(bf16), upper_block, preferred_element_type=f32) - 1.0
+        arank = jnp.where(present, arank, -5.0)
+        vacant = label == 0
+        ranks = []
+        for t in range(STEPS):
+            vacant = vacant | (leave_at == t)
+            flag = jnp.where(vacant, 1.0, 0.0).astype(bf16)
+            rank = jnp.dot(flag, upper, preferred_element_type=f32) - 1.0
+            total = jnp.dot(flag, ones, preferred_element_type=f32)
+            for r in range(SLOT_BLOCKS - 1):
+                rank = rank + jnp.where(sub8 > r, total[r : r + 1, :], 0.0)
+            ranks.append(jnp.where(vacant, rank, -1.0))
+            count = jnp.sum(jnp.where(lane8 // 32 == t, present_f, 0.0), axis=1, keepdims=True)
+            vacant = vacant & (rank >= count)
+
+        acode = code_of(alab.astype(jnp.int32))
+        turn(ranks + [acode, alab])
+        LR[8:16, :] = acode
+        hot_rows(SLOT_BLOCKS, 32)
+        hot_columns(SLOT_BLOCKS, SLOT_BLOCKS + 1)
+        AMSK[...] = jnp.broadcast_to(LT[:, 40:41], (LANES, LANES))
+
+        group = lcol // 32
+        alab_high, alab_low = split(alab)
+        final = jnp.where(leave_at == STEPS, label, 0).astype(f32)
         nt = (((1,), (1,)), ((), ()))
-        placed = lax.dot_general(alab_high, hot, nt, preferred_element_type=f32)
-        placed = placed + lax.dot_general(alab_low, hot, nt, preferred_element_type=f32)
-        final = final + jnp.where(sub8 == r, placed, 0.0)
-    c_out[...] = final.astype(jnp.int32) - 1
-
-    lane16 = lax.broadcasted_iota(jnp.int32, (16, LANES), 1)
-    first_lane, last_lane = lane16 == 0, lane16 == LANES - 1
+        for r in range(SLOT_BLOCKS):
+            mine = jnp.broadcast_to(LT[:, r : r + 1], (LANES, LANES))
+            for t in range(1, STEPS):
+                mine = jnp.where(group == t, LT[:, 8 * t + r : 8 * t + r + 1], mine)
+            hot = jnp.where(mine == arank[0:1, :], 1.0, 0.0).astype(bf16)
+            PLACE[r * LANES : (r + 1) * LANES, 0:LANES] = hot
+            PLACE[r * LANES : (r + 1) * LANES, LANES : 2 * LANES] = hot
+            placed = lax.dot_general(alab_high, hot, nt, preferred_element_type=f32)
+            placed = placed + lax.dot_general(alab_low, hot, nt, preferred_element_type=f32)
+            final = final + jnp.where(sub8 == r, placed, 0.0)
+        c_out[...] = final.astype(jnp.int32) - 1
 
     def slope_z(tiles):
-        zero = jnp.zeros((16, LANES), f32)
+        height = tiles[0].shape[0]
+        lane = lax.broadcasted_iota(jnp.int32, (height, LANES), 1)
+        zero = jnp.zeros((height, LANES), f32)
         ahead = [pltpu.roll(v, LANES - 1, 1) for v in tiles] + [zero]
         behind = [zero] + [pltpu.roll(v, 1, 1) for v in tiles]
         return [
-            jnp.where(last_lane, ahead[q + 1], ahead[q])
-            - jnp.where(first_lane, behind[q], behind[q + 1])
+            jnp.where(lane == LANES - 1, ahead[q + 1], ahead[q])
+            - jnp.where(lane == 0, behind[q], behind[q + 1])
             for q in range(nq)
         ]
 
@@ -465,23 +483,24 @@
                     - half_gain * (above[1:2, :] - PR[q, i, 7 + cy : 8 + cy, :])
                 )
 
-        def pressure(i, jb):
-            rows, at = rows_of(jb)
+
+        def pressure(i, first):
+            rows, at = slice(first, first + 8), slice(8 + first, 16 + first)
             slopes = slope_z([VZ[q, i, rows, :] for q in range(nq)])
             for q in range(nq):
                 rise = (
                     (VX[q, i + 2, rows, :] - VX[q, i, rows, :])
                     + (
-                        VY[q, i, pl.ds(9 + jb * 16 + zero_row, 16), :]
-                        - VY[q, i, pl.ds(7 + jb * 16 + zero_row, 16), :]
+                        VY[q, i, pl.ds(9 + first + zero_row, 8), :]
+                        - VY[q, i, pl.ds(7 + first + zero_row, 8), :]
                     )
                     + slopes[q]
                 )
-                row = column_row(i, q // 2, jb)
+                row = column_row(i, q // 2, 0) + first
                 col = (q % 2) * LANES
-                value = PR[q, i, at, :] - half_gain * rise + SRC[row : row + 16, col : col + LANES]
-                PR[q, i, at, :] = value
-                keep_parts(i, jb, q, value)
+                PR[q, i, at, :] = (
+                    PR[q, i, at, :] - half_gain * rise + SRC[row : row + 8, col : col + LANES]
+                )
 
         order = [0, groups - 1] + list(range(1, groups - 1)) if groups > 1 else [0]
         early = order[:2]
@@ -494,6 +513,7 @@
                     flow_z(i, jb)
                     flow_y(i, jb)
 
+        pl.when(t == 0)(plan)
         wait_taken(lambda d: p_copy(t, d), (2, 3))
         wait_sent(lambda d: p_copy(t, d), (2, 3))
 
@@ -525,8 +545,8 @@
             scatter(m)
         for i in ends:
             side_rows(i)
-            for jb in range(jbs):
-                pressure(i, jb)
+            for first in range(0, cy, 8):
+                pressure(i, first)
 
         @pl.when(t < STEPS - 1)
         def _():
@@ -534,17 +554,24 @@
 
         for m in late[1:]:
             scatter(m)
-        for m in order:
-            for i in range(m * planes, (m + 1) * planes):
-                if i not in ends:
-                    side_rows(i)
-                    for jb in range(jbs):
-                        pressure(i, jb)
+        inner = [i for m in order for i in range(m * planes, (m + 1) * planes) if i not in ends]
+        for i in inner:
+            side_rows(i)
+            for first in sorted({0, cy - 8}):
+                pressure(i, first)
 
         @pl.when(t < STEPS - 1)
         def _():
             pack_rows(t + 1)
             start(lambda d: p_copy(t + 1, d), (2, 3))
+
+        for i in inner:
+            for first in range(8, cy - 8, 8):
+                pressure(i, first)
+
+        @pl.when(t < STEPS - 1)
+        def _():
+            split_all()
 
         return carry
 
@@ -566,7 +593,7 @@
         keep = MSK[rows, :]
         keep = jnp.concatenate([keep, keep], axis=1) >= float(STEPS)
         R[rows, :] = jnp.where(keep, R[rows, :], 0.0) + placed[:, :BLOCK]
-        S[rows, :] = jnp.where(keep, S[rows, :], 0.0) + placed[:, BLOCK:]
+        S[rows, :] = (1.0 / time_step) * (jnp.where(keep, S[rows, :], 0.0) + placed[:, BLOCK:])
         return carry
 
     lax.fori_loop(0, SLOT_BLOCKS, finish, 0)

time: 50.1 us -> 47.7 us (0.952)
  the two profiles are of different devices: /device:TPU:0 before, /device:TPU:1 now
where the time goes in v3:
time: 47.7 us; the launch traced here: 47.6 us
  Pallas kernels  47 us (99%)
  between operations  0.64 us (1%)
    pallas_call x1, Pallas kernels, on_device(): pl.pallas_call(kernel, out_shape=(vmem_out((nq, cx, cy + 16, LANES), f32)...  44.2 us
    pallas_call x1, Pallas kernels, on_device(): pl.pallas_call(write_out, out_shape=(jax.ShapeDtypeStruct(pressure.shape,...  2.8 us

profile of v3, /device:TPU:1, one launch (start us, length us, event | category | flops | bytes accessed | tf_op | source)
XLA Modules:
  0.0 47.6 jit_solution(12078394483135321092)
XLA Ops:
  0.6 44.2 %shard_map.119 = (f32[4,16,48,128]{3,2,1,0:T(8,128)S(1)}, f32[4,18,32,128]{3,2,1,0:T(8,128)S(1)}, f32[4,16,48,128]{3,2,1,0:T(8,128)S(1)}, f32[4,16,32,128]{3,2,1...) custom-call(s32[1024]{0:T(1024)} %cells_h.1, s32[4,1,1,8]{3,2,1,0:T(1,128)} %slot_h.1, ...), custom_call_target="tpu_custom_call" | custom-call | flops 10737418240 | bytes 13631488 | tf_op jit(solution)/shard_map/pallas_call | solution.py:631
  44.8 2.8 %shard_map.120 = (f32[16,32,512]{2,1,0:T(8,128)}, f32[3,16,32,512]{3,2,1,0:T(8,128)}, f32[1024,256]{1,0:T(8,128)}, f32[1024,256]{1,0:T(8,128)}, s32[8,128]{1,0:T(8,128)}) custom-call(f32[4,16,48,128]{3,2,1,0:T(8,128)S(1)} %get-tuple-element.17.p, f32[4,18,32,128]{3,2,1,0:T(8,128)S(1)} %get-tuple-element.18.vx, f32[4,16,48,128]{3,2,1,0:T(8,128)S(1)} %get-tuple-element.19.vy, ...), custom_call_target="tpu_custom_call" | custom-call | bytes 13631488 | tf_op jit(solution)/shard_map/pallas_call | solution.py:706

commit v4 on v3

--- a/solution.py
+++ b/solution.py
@@ -56,8 +56,8 @@
 
 def kernel(
     cells_h, slot_h, way_h, cells_b, press, vel, stretch, rest, speed0,
-    PR, VX, VY, VZ, R, S, c_out,
-    A, AR, SB, OH, OHT, PHL, PG, VHL, SRC, XR, YS, YR, VYS, VYR,
+    PR, VX, VY, VZ, r_out, s_out, c_out,
+    R, S, A, AR, SB, DB, OH, OHT, PHL, PG, VHL, SRC, XR, YS, YR, VYS, VYR,
     MT, MR, MSK, AMSK, LT, LR, PLACE, CAT, cells_s, slot_s, way_s, cells_v,
     in_sem, meta_s, meta_r, xs, xr, vs, vr, ds_, dr, fs, fr,
 ):
@@ -101,9 +101,10 @@
     inputs = [(cells_h, cells_s), (slot_h, slot_s), (way_h, way_s), (cells_b, cells_v)]
     for q in range(nq):
         inputs.append((press.at[:, :, pl.ds(q * LANES, LANES)], PR.at[q, :, pl.ds(8, cy), :]))
-    inputs.append((rest, A))
-    inputs.append((stretch, R))
-    inputs.append((speed0, S))
+    own = pl.ds(0, SLOTS)
+    inputs.append((rest, A.at[own, :]))
+    inputs.append((stretch, R.at[own, :]))
+    inputs.append((speed0, S.at[own, :]))
     for comp in range(3):
         for q in range(nq):
             dst = (
@@ -132,8 +133,11 @@
     edge_rows = jnp.zeros((nq, cx, 8, LANES), f32)
     PR[:, :, 0:8, :] = edge_rows
     PR[:, :, 8 + cy : 16 + cy, :] = edge_rows
-    VHL[pl.ds(SLOTS, ARRIVE), :] = jnp.zeros((ARRIVE, BLOCK), bf16)
-    VHL[pl.ds(ROWS + SLOTS, ARRIVE), :] = jnp.zeros((ARRIVE, BLOCK), bf16)
+    empty = jnp.zeros((ARRIVE, BLOCK), f32)
+    R[SLOTS:ROWS, :] = empty + 1.0
+    S[SLOTS:ROWS, :] = empty
+    A[SLOTS:ROWS, :] = empty
+    MSK[SLOTS:ROWS, :] = jnp.full((ARRIVE, LANES), -1.0, f32)
     OHT[:, SLOTS:ROWS] = jnp.zeros((ncol, ARRIVE), bf16)
     OH[SLOTS:ROWS, :] = jnp.zeros((ARRIVE, ncol), bf16)
     pl.semaphore_wait(barrier, 2 + has_lo.astype(jnp.int32) + has_hi.astype(jnp.int32))
@@ -226,9 +230,9 @@
     def keep_parts(i, jb, q, value):
         high, low = split(value)
         row = column_row(i, q // 2, jb)
-        col = (q % 2) * LANES
+        col = (q % 2) * 2 * LANES
         PHL[row : row + 16, col : col + LANES] = high
-        PHL[row + ncol : row + ncol + 16, col : col + LANES] = low
+        PHL[row : row + 16, col + LANES : col + 2 * LANES] = low
 
     def rows_of(jb):
         return slice(jb * 16, jb * 16 + 16), slice(8 + jb * 16, 24 + jb * 16)
@@ -381,70 +385,75 @@
 
     low_gate = jnp.where(has_lo, 1.0, 0.0).astype(f32)
     high_gate = jnp.where(has_hi, 1.0, 0.0).astype(f32)
-    chunk = 256
-
-    def gather(low_row, count):
-        hot = OH[low_row : low_row + count, :]
-        hot = jnp.concatenate([hot, hot], axis=1)
-        PG[low_row : low_row + count, :] = jnp.dot(hot, PHL[...], preferred_element_type=f32)
-
-    def scatter(m):
-        hot = OHT[m * part : (m + 1) * part, :]
-        hot = jnp.concatenate([hot, hot], axis=1)
-        SRC[m * part : (m + 1) * part, :] = jnp.dot(hot, VHL[...], preferred_element_type=f32)
+
+    def halves(w):
+        return slice(w * LANES, (w + 1) * LANES), slice(2 * w * LANES, 2 * (w + 1) * LANES)
+
+    def gather(w):
+        narrow, pair = halves(w)
+        both = jnp.dot(OH[...], PHL[:, pair], preferred_element_type=f32)
+        PG[:, narrow] = both[:, :LANES] + both[:, LANES:]
+
+    def scatter(w):
+        narrow, pair = halves(w)
+        both = jnp.dot(OHT[...], VHL[:, pair], preferred_element_type=f32)
+        SRC[:, narrow] = both[:, :LANES] + both[:, LANES:]
+
+    def take_arrivals(t):
+        wait_taken(lambda d: dep_copy(t, d))
+        rows = pl.ds(pl.multiple_of(t * 32, 32), 32)
+        to = pl.ds(pl.multiple_of(SLOTS + t * 32, 32), 32)
+        R[to, :] = AR[0, rows, :]
+        S[to, :] = AR[1, rows, :]
+        A[to, :] = AR[2, rows, :]
+        MSK[to, :] = jnp.where(AMSK[rows, :] > 0.0, 2.0 * STEPS, -1.0)
 
     def step(t, carry):
         limit = t.astype(f32)
 
-        def bubbles(first):
+        def bubbles(first, w):
             rows = slice(first, first + 16)
-            radius, speed, rate = wall_update(R[rows, :], S[rows, :], A[rows, :], PG[rows, :])
-            R[rows, :] = radius
-            S[rows, :] = speed
-            keep = MSK[rows, :]
-            keep = jnp.concatenate([keep, keep], axis=1) >= limit
-            high, low = split(jnp.where(keep, rate, 0.0))
-            VHL[rows, :] = high
-            VHL[ROWS + first : ROWS + first + 16, :] = low
-
-        gather(0, chunk)
-        for m in range(SLOTS // chunk):
-            if m + 1 < SLOTS // chunk:
-                gather((m + 1) * chunk, chunk)
-            else:
-                gather(SLOTS, ARRIVE)
-            for b in range(chunk // 16):
-                bubbles(m * chunk + b * 16)
+            col = halves(w)[0]
+            radius, speed, rate = wall_update(R[rows, col], S[rows, col], A[rows, col], PG[rows, col])
+            R[rows, col] = radius
+            S[rows, col] = speed
+            high, low = split(jnp.where(MSK[rows, :] >= limit, rate, 0.0))
+            VHL[rows, 2 * w * LANES : (2 * w + 1) * LANES] = high
+            VHL[rows, (2 * w + 1) * LANES : (2 * w + 2) * LANES] = low
 
         for k in range(DEP):
-            row = pl.ds(jnp.maximum(slot_s[t, 0, 0, k], 0), 1)
-            SB[t, 0, k : k + 1, :] = R[row, :]
-            SB[t, 1, k : k + 1, :] = S[row, :]
-            SB[t, 2, k : k + 1, :] = A[row, :]
+            slot = jnp.maximum(slot_s[t, 0, 0, k], 0)
+            cell = jnp.maximum(cells_s[slot], 0)
+            place = cell >> 1
+            row = pl.ds(slot, 1)
+            DB[0, k : k + 1, :] = R[row, :]
+            DB[1, k : k + 1, :] = S[row, :]
+            DB[2, k : k + 1, :] = A[row, :]
+            for w in range(2):
+                DB[3, k : k + 1, halves(w)[0]] = PR[
+                    2 * (cell & 1) + w,
+                    place >> (cy.bit_length() - 1),
+                    pl.ds(8 + (place & (cy - 1)), 1),
+                    :,
+                ]
+        radius, speed, _ = wall_update(DB[0], DB[1], DB[2], DB[3])
+        SB[t, 0] = radius
+        SB[t, 1] = speed
+        SB[t, 2] = DB[2]
         start(lambda d: dep_copy(t, d))
 
         @pl.when(t > 0)
         def _():
-            wait_taken(lambda d: dep_copy(t - 1, d))
-
-        def arrived(n, carry):
-            for b in range(2):
-                first = n * 32 + b * 16
-                rows = pl.ds(pl.multiple_of(first, 16), 16)
-                low_rows = pl.ds(pl.multiple_of(SLOTS + first, 16), 16)
-                radius, speed, rate = wall_update(
-                    AR[0, rows, :], AR[1, rows, :], AR[2, rows, :], PG[low_rows, :]
-                )
-                AR[0, rows, :] = radius
-                AR[1, rows, :] = speed
-                keep = AMSK[rows, :]
-                keep = jnp.concatenate([keep, keep], axis=1) > 0.0
-                high, low = split(jnp.where(keep, rate, 0.0))
-                VHL[low_rows, :] = high
-                VHL[pl.ds(pl.multiple_of(ROWS + SLOTS + first, 16), 16), :] = low
-            return carry
-
-        lax.fori_loop(0, t, arrived, 0)
+            take_arrivals(t - 1)
+
+        gather(0)
+        gather(1)
+        for first in range(0, ROWS, 16):
+            bubbles(first, 0)
+        scatter(0)
+        for first in range(0, ROWS, 16):
+            bubbles(first, 1)
+        scatter(1)
 
         def flow_x(i, after, before):
             for q in range(nq):
@@ -502,16 +511,12 @@
                     PR[q, i, at, :] - half_gain * rise + SRC[row : row + 8, col : col + LANES]
                 )
 
-        order = [0, groups - 1] + list(range(1, groups - 1)) if groups > 1 else [0]
-        early = order[:2]
-        for k, m in enumerate(early):
-            scatter(m)
-            for i in range(k * cx // len(early), (k + 1) * cx // len(early)):
-                if 0 < i < cx - 1:
-                    flow_x(i, None, None)
-                for jb in range(jbs):
-                    flow_z(i, jb)
-                    flow_y(i, jb)
+        for i in range(cx):
+            if 0 < i < cx - 1:
+                flow_x(i, None, None)
+            for jb in range(jbs):
+                flow_z(i, jb)
+                flow_y(i, jb)
 
         pl.when(t == 0)(plan)
         wait_taken(lambda d: p_copy(t, d), (2, 3))
@@ -539,10 +544,7 @@
         flow_x(0, None, 1)
         flow_x(cx - 1, 0, None)
         flow_x(cx, 1, None)
-        late = order[2:]
         ends = [0, 1, cx - 2, cx - 1]
-        for m in late[:1]:
-            scatter(m)
         for i in ends:
             side_rows(i)
             for first in range(0, cy, 8):
@@ -552,9 +554,7 @@
         def _():
             start(lambda d: p_copy(t + 1, d), (0, 1))
 
-        for m in late[1:]:
-            scatter(m)
-        inner = [i for m in order for i in range(m * planes, (m + 1) * planes) if i not in ends]
+        inner = range(2, cx - 2)
         for i in inner:
             side_rows(i)
             for first in sorted({0, cy - 8}):
@@ -577,12 +577,11 @@
 
     lax.fori_loop(0, STEPS, step, 0)
 
-    wait_taken(lambda d: dep_copy(STEPS - 1, d))
+    take_arrivals(STEPS - 1)
     keep = AMSK[...] > 0.0
-    for k in range(2):
+    for k, state in enumerate((R, S)):
         for w in range(2):
-            col = slice(w * LANES, (w + 1) * LANES)
-            high, low = split(jnp.where(keep, AR[k, :, col], 0.0))
+            high, low = split(jnp.where(keep, state[SLOTS:ROWS, halves(w)[0]], 0.0))
             to = slice(k * BLOCK + w * LANES, k * BLOCK + (w + 1) * LANES)
             CAT[0:ARRIVE, to] = high
             CAT[ARRIVE : 2 * ARRIVE, to] = low
@@ -592,8 +591,8 @@
         placed = jnp.dot(PLACE[rows, :], CAT[...], preferred_element_type=f32)
         keep = MSK[rows, :]
         keep = jnp.concatenate([keep, keep], axis=1) >= float(STEPS)
-        R[rows, :] = jnp.where(keep, R[rows, :], 0.0) + placed[:, :BLOCK]
-        S[rows, :] = (1.0 / time_step) * (jnp.where(keep, S[rows, :], 0.0) + placed[:, BLOCK:])
+        r_out[rows, :] = jnp.where(keep, R[rows, :], 0.0) + placed[:, :BLOCK]
+        s_out[rows, :] = (1.0 / time_step) * (jnp.where(keep, S[rows, :], 0.0) + placed[:, BLOCK:])
         return carry
 
     lax.fori_loop(0, SLOT_BLOCKS, finish, 0)
@@ -642,14 +641,17 @@
         in_specs=[pl.BlockSpec(memory_space=pltpu.HBM)] * 9,
         out_specs=(vmem,) * 7,
         scratch_shapes=[
-            pltpu.VMEM((SLOTS, BLOCK), f32),
+            pltpu.VMEM((ROWS, BLOCK), f32),
+            pltpu.VMEM((ROWS, BLOCK), f32),
+            pltpu.VMEM((ROWS, BLOCK), f32),
             pltpu.VMEM((3, ARRIVE, BLOCK), f32),
             pltpu.VMEM((STEPS, 3, DEP, BLOCK), f32),
+            pltpu.VMEM((4, DEP, BLOCK), f32),
             pltpu.VMEM((ROWS, ncol), bf16),
             pltpu.VMEM((ncol, ROWS), bf16),
-            pltpu.VMEM((2 * ncol, BLOCK), bf16),
+            pltpu.VMEM((ncol, 2 * BLOCK), bf16),
             pltpu.VMEM((ROWS, BLOCK), f32),
-            pltpu.VMEM((2 * ROWS, BLOCK), bf16),
+            pltpu.VMEM((ROWS, 2 * BLOCK), bf16),
             pltpu.VMEM((ncol, BLOCK), f32),
             pltpu.VMEM((STEPS, 2, nq, 2, cy, LANES), f32),
             pltpu.VMEM((STEPS, 2, nq, cx, 2, LANES), f32),
@@ -658,7 +660,7 @@
             pltpu.VMEM((2, nq, cx, 1, LANES), f32),
             pltpu.VMEM((8, LANES), f32),
             pltpu.VMEM((4, 8, LANES), f32),
-            pltpu.VMEM((SLOTS, LANES), f32),
+            pltpu.VMEM((ROWS, LANES), f32),
             pltpu.VMEM((ARRIVE, LANES), f32),
             pltpu.VMEM((LANES, LANES), f32),
             pltpu.VMEM((16, LANES), f32),

time: 47.7 us -> 45.3 us (0.950)
  Pallas kernels: 47 us -> 44.6 us
    pallas_call x1, Pallas kernels: 44.2 us -> 41.8 us  [on_device(): pl.pallas_call(kernel, out_shape=(vmem_out((nq, cx, cy + 16, LANES), f32)...]
where the time goes in v4:
time: 45.3 us; the launch traced here: 45.2 us
  Pallas kernels  44.6 us (98%)
  between operations  0.64 us (1%)
    pallas_call x1, Pallas kernels, on_device(): pl.pallas_call(kernel, out_shape=(vmem_out((nq, cx, cy + 16, LANES), f32)...  41.8 us
    pallas_call x1, Pallas kernels, on_device(): pl.pallas_call(write_out, out_shape=(jax.ShapeDtypeStruct(pressure.shape,...  2.8 us

profile of v4, /device:TPU:1, one launch (start us, length us, event | category | flops | bytes accessed | tf_op | source)
XLA Modules:
  0.0 45.2 jit_solution(14357005163307175600)
XLA Ops:
  0.6 41.8 %shard_map.119 = (f32[4,16,48,128]{3,2,1,0:T(8,128)S(1)}, f32[4,18,32,128]{3,2,1,0:T(8,128)S(1)}, f32[4,16,48,128]{3,2,1,0:T(8,128)S(1)}, f32[4,16,32,128]{3,2,1...) custom-call(s32[1024]{0:T(1024)} %cells_h.1, s32[4,1,1,8]{3,2,1,0:T(1,128)} %slot_h.1, ...), custom_call_target="tpu_custom_call" | custom-call | flops 10737418240 | bytes 13631488 | tf_op jit(solution)/shard_map/pallas_call | solution.py:630
  42.4 2.8 %shard_map.120 = (f32[16,32,512]{2,1,0:T(8,128)}, f32[3,16,32,512]{3,2,1,0:T(8,128)}, f32[1024,256]{1,0:T(8,128)}, f32[1024,256]{1,0:T(8,128)}, s32[8,128]{1,0:T(8,128)}) custom-call(f32[4,16,48,128]{3,2,1,0:T(8,128)S(1)} %get-tuple-element.17.p, f32[4,18,32,128]{3,2,1,0:T(8,128)S(1)} %get-tuple-element.18.vx, f32[4,16,48,128]{3,2,1,0:T(8,128)S(1)} %get-tuple-element.19.vy, ...), custom_call_target="tpu_custom_call" | custom-call | bytes 13631488 | tf_op jit(solution)/shard_map/pallas_call | solution.py:708

commit v5 on v4

--- a/solution.py
+++ b/solution.py
@@ -57,7 +57,7 @@
 def kernel(
     cells_h, slot_h, way_h, cells_b, press, vel, stretch, rest, speed0,
     PR, VX, VY, VZ, r_out, s_out, c_out,
-    R, S, A, AR, SB, DB, OH, OHT, PHL, PG, VHL, SRC, XR, YS, YR, VYS, VYR,
+    R, S, A, AR, SB, DB, OH, OHT, PHL, PG, VHL, SRC, XS, XR, YS, YR, VYS, VYR,
     MT, MR, MSK, AMSK, LT, LR, PLACE, CAT, cells_s, slot_s, way_s, cells_v,
     in_sem, meta_s, meta_r, xs, xr, vs, vr, ds_, dr, fs, fr,
 ):
@@ -101,18 +101,17 @@
     inputs = [(cells_h, cells_s), (slot_h, slot_s), (way_h, way_s), (cells_b, cells_v)]
     for q in range(nq):
         inputs.append((press.at[:, :, pl.ds(q * LANES, LANES)], PR.at[q, :, pl.ds(8, cy), :]))
+    for q in range(nq):
+        lanes = pl.ds(q * LANES, LANES)
+        inputs.append((vel.at[1, :, :, lanes], VY.at[q, :, pl.ds(8, cy), :]))
     own = pl.ds(0, SLOTS)
     inputs.append((rest, A.at[own, :]))
     inputs.append((stretch, R.at[own, :]))
     inputs.append((speed0, S.at[own, :]))
-    for comp in range(3):
-        for q in range(nq):
-            dst = (
-                VX.at[q, pl.ds(1, cx), :, :],
-                VY.at[q, :, pl.ds(8, cy), :],
-                VZ.at[q],
-            )[comp]
-            inputs.append((vel.at[comp, :, :, pl.ds(q * LANES, LANES)], dst))
+    for q in range(nq):
+        lanes = pl.ds(q * LANES, LANES)
+        inputs.append((vel.at[0, :, :, lanes], VX.at[q, pl.ds(1, cx), :, :]))
+        inputs.append((vel.at[2, :, :, lanes], VZ.at[q]))
     loads = [pltpu.make_async_copy(a, b, in_sem.at[k]) for k, (a, b) in enumerate(inputs)]
     for load in loads:
         load.start()
@@ -133,6 +132,8 @@
     edge_rows = jnp.zeros((nq, cx, 8, LANES), f32)
     PR[:, :, 0:8, :] = edge_rows
     PR[:, :, 8 + cy : 16 + cy, :] = edge_rows
+    VY[:, :, 0:8, :] = edge_rows
+    VY[:, :, 8 + cy : 16 + cy, :] = edge_rows
     empty = jnp.zeros((ARRIVE, BLOCK), f32)
     R[SLOTS:ROWS, :] = empty + 1.0
     S[SLOTS:ROWS, :] = empty
@@ -153,8 +154,7 @@
 
     def p_copy(t, d):
         if d < 2:
-            src = PR.at[:, pl.ds((cx - 2, 0)[d], 2), pl.ds(8, cy), :]
-            return remote(src, XR.at[t, d], xs.at[t, d], xr.at[t, d], d)
+            return remote(XS.at[t, 1 - d], XR.at[t, d], xs.at[t, d], xr.at[t, d], d)
         return remote(YS.at[t, 3 - d], YR.at[t, d - 2], xs.at[t, d], xr.at[t, d], d)
 
     def first_copies(d):
@@ -197,6 +197,60 @@
     for d in range(2):
         for copy in first_copies(d):
             copy.start()
+    edges = ((0, 1), (cy - 2, cy - 1))
+
+    def one(row):
+        return pl.ds(row + zero_row, 1)
+
+    def pack_rows(t):
+        for side in range(2):
+            for r in range(2):
+                for q in range(nq):
+                    for i in range(cx):
+                        YS[t, side, r, q, one(i), :] = PR[q, i, one(8 + edges[side][r]), :]
+
+    def unpack_rows(t, planes_now):
+        for side in range(2):
+            for r in range(2):
+                for q in range(nq):
+                    for i in planes_now:
+                        PR[q, i, one(8 + edges[side][r]), :] = YS[t, side, r, q, one(i), :]
+
+    def column_row(i, h, jb):
+        return (i // planes) * part + (h * planes + i % planes) * cy + jb * 16
+
+    def keep_parts(i, jb, q, value):
+        high, low = split(value)
+        row = column_row(i, q // 2, jb)
+        col = (q % 2) * 2 * LANES
+        PHL[row : row + 16, col : col + LANES] = high
+        PHL[row : row + 16, col + LANES : col + 2 * LANES] = low
+
+    def rows_of(jb):
+        return slice(jb * 16, jb * 16 + 16), slice(8 + jb * 16, 24 + jb * 16)
+
+    def split_all():
+        for i in range(cx):
+            for jb in range(jbs):
+                for q in range(nq):
+                    keep_parts(i, jb, q, PR[q, i, rows_of(jb)[1], :])
+
+    for k in range(nq):
+        loads[k].wait()
+    pack_rows(0)
+    start(lambda d: p_copy(0, d), (2, 3))
+    for q in range(nq):
+        for r in range(2):
+            XS[0, 0, q, r] = PR[q, r, 8 : 8 + cy, :]
+            XS[0, 1, q, r] = PR[q, cx - 2 + r, 8 : 8 + cy, :]
+    for k in range(nq, 2 * nq):
+        loads[k].wait()
+    for q in range(nq):
+        for i in range(cx):
+            VYS[0, q, one(i), :] = VY[q, i, one(8), :]
+            VYS[1, q, one(i), :] = VY[q, i, one(7 + cy), :]
+    start(v_copy, (2, 3))
+
     for load in small_loads:
         load.wait()
 
@@ -218,35 +272,6 @@
 
     start(meta_copy)
 
-    def pack_rows(t):
-        for i in range(cx):
-            for q in range(nq):
-                YS[t, 0, q, i] = PR[q, i, 8:10, :]
-                YS[t, 1, q, i] = PR[q, i, 6 + cy : 8 + cy, :]
-
-    def column_row(i, h, jb):
-        return (i // planes) * part + (h * planes + i % planes) * cy + jb * 16
-
-    def keep_parts(i, jb, q, value):
-        high, low = split(value)
-        row = column_row(i, q // 2, jb)
-        col = (q % 2) * 2 * LANES
-        PHL[row : row + 16, col : col + LANES] = high
-        PHL[row : row + 16, col + LANES : col + 2 * LANES] = low
-
-    def rows_of(jb):
-        return slice(jb * 16, jb * 16 + 16), slice(8 + jb * 16, 24 + jb * 16)
-
-    def split_all():
-        for i in range(cx):
-            for jb in range(jbs):
-                for q in range(nq):
-                    keep_parts(i, jb, q, PR[q, i, rows_of(jb)[1], :])
-
-    for k in range(nq):
-        loads[k].wait()
-    pack_rows(0)
-    start(lambda d: p_copy(0, d), (2, 3))
     split_all()
 
     lrow = lax.broadcasted_iota(jnp.int32, (LANES, LANES), 0)
@@ -294,19 +319,7 @@
         )
     hot_columns(0, SLOT_BLOCKS)
 
-    for k in range(nq + 3, nq + 3 + 3 * nq):
-        loads[k].wait()
-
-    def pack_flow(i, carry):
-        for q in range(nq):
-            VYS[0, q, i] = VY[q, i, 8:9, :]
-            VYS[1, q, i] = VY[q, i, 7 + cy : 8 + cy, :]
-        return carry
-
-    lax.fori_loop(0, cx, pack_flow, 0, unroll=4)
-    start(v_copy, (2, 3))
-
-    for k in range(nq, nq + 3):
+    for k in range(2 * nq, 2 * nq + 3):
         loads[k].wait()
 
     def first_state(n, carry):
@@ -321,6 +334,9 @@
         return carry
 
     lax.fori_loop(0, SLOTS // 16, first_state, 0, unroll=4)
+    for k in range(2 * nq + 3, 4 * nq + 3):
+        loads[k].wait()
+
     def plan():
         wait_taken(meta_copy)
         came = (lane8 // DEP) % 4
@@ -455,13 +471,18 @@
             bubbles(first, 1)
         scatter(1)
 
-        def flow_x(i, after, before):
+        def flow_x(i):
             for q in range(nq):
                 for jb in range(jbs):
                     rows, at = rows_of(jb)
-                    ahead = PR[q, i + 1, at, :] if after is None else XR[t, 1, q, after, rows, :]
-                    back = PR[q, i - 1, at, :] if before is None else XR[t, 0, q, before, rows, :]
-                    VX[q, i + 1, rows, :] = VX[q, i + 1, rows, :] - half_gain * (ahead - back)
+                    flow = VX[q, i + 1, rows, :]
+                    if i == 0:
+                        flow = flow - half_gain * PR[q, 1, at, :]
+                    elif i == cx - 1:
+                        flow = flow + half_gain * PR[q, cx - 2, at, :]
+                    else:
+                        flow = flow - half_gain * (PR[q, i + 1, at, :] - PR[q, i - 1, at, :])
+                    VX[q, i + 1, rows, :] = flow
 
         def flow_z(i, jb):
             rows, at = rows_of(jb)
@@ -477,97 +498,110 @@
                     - PR[q, i, pl.ds(7 + jb * 16 + zero_row, 16), :]
                 )
 
-        def side_rows(i):
-            for q in range(nq):
-                below, above = YR[t, 0, q, i], YR[t, 1, q, i]
-                VY[q, i, 8:9, :] = VY[q, i, 8:9, :] + half_gain * below[1:2, :]
-                VY[q, i, 7 + cy : 8 + cy, :] = (
-                    VY[q, i, 7 + cy : 8 + cy, :] - half_gain * above[0:1, :]
-                )
-                VY[q, i, 7:8, :] = low_gate * (
-                    VY[q, i, 7:8, :] - half_gain * (PR[q, i, 8:9, :] - below[0:1, :])
-                )
-                VY[q, i, 8 + cy : 9 + cy, :] = high_gate * (
-                    VY[q, i, 8 + cy : 9 + cy, :]
-                    - half_gain * (above[1:2, :] - PR[q, i, 7 + cy : 8 + cy, :])
-                )
-
-
-        def pressure(i, first):
-            rows, at = slice(first, first + 8), slice(8 + first, 16 + first)
+        def pressure(i, jb):
+            rows, at = rows_of(jb)
             slopes = slope_z([VZ[q, i, rows, :] for q in range(nq)])
             for q in range(nq):
-                rise = (
-                    (VX[q, i + 2, rows, :] - VX[q, i, rows, :])
-                    + (
-                        VY[q, i, pl.ds(9 + first + zero_row, 8), :]
-                        - VY[q, i, pl.ds(7 + first + zero_row, 8), :]
-                    )
-                    + slopes[q]
+                rise = slopes[q] + (
+                    VY[q, i, pl.ds(9 + jb * 16 + zero_row, 16), :]
+                    - VY[q, i, pl.ds(7 + jb * 16 + zero_row, 16), :]
                 )
-                row = column_row(i, q // 2, 0) + first
+                if i + 1 < cx:
+                    rise = rise + VX[q, i + 2, rows, :]
+                if i > 0:
+                    rise = rise - VX[q, i, rows, :]
+                row = column_row(i, q // 2, jb)
                 col = (q % 2) * LANES
                 PR[q, i, at, :] = (
-                    PR[q, i, at, :] - half_gain * rise + SRC[row : row + 8, col : col + LANES]
+                    PR[q, i, at, :] - half_gain * rise + SRC[row : row + 16, col : col + LANES]
                 )
 
         for i in range(cx):
-            if 0 < i < cx - 1:
-                flow_x(i, None, None)
+            flow_x(i)
             for jb in range(jbs):
                 flow_z(i, jb)
                 flow_y(i, jb)
+        for i in range(cx):
+            for jb in range(jbs):
+                pressure(i, jb)
+        pack_rows(t + 1)
 
         pl.when(t == 0)(plan)
         wait_taken(lambda d: p_copy(t, d), (2, 3))
-        wait_sent(lambda d: p_copy(t, d), (2, 3))
 
         @pl.when(t > 0)
         def _():
             wait_taken(lambda d: p_copy(t, d), (0, 1))
-            wait_sent(lambda d: p_copy(t, d), (0, 1))
 
         @pl.when(t == 0)
         def _():
             for d in range(2):
                 for copy in first_copies(d):
                     copy.wait_recv()
-                    copy.wait_send()
             wait_taken(v_copy, (2, 3))
-            wait_sent(v_copy, (2, 3))
-            for i in range(cx):
-                for q in range(nq):
-                    VY[q, i, 7:8, :] = VYR[0, q, i]
-                    VY[q, i, 8 + cy : 9 + cy, :] = VYR[1, q, i]
-
-        flow_x(-1, None, 0)
-        flow_x(0, None, 1)
-        flow_x(cx - 1, 0, None)
-        flow_x(cx, 1, None)
-        ends = [0, 1, cx - 2, cx - 1]
-        for i in ends:
-            side_rows(i)
-            for first in range(0, cy, 8):
-                pressure(i, first)
+
+        below, above = VYR[0], VYR[1]
+        below = low_gate * (below - half_gain * (YS[t, 0, 0] - YR[t, 0, 0]))
+        above = high_gate * (above - half_gain * (YR[t, 1, 1] - YS[t, 1, 1]))
+        VYR[0] = below
+        VYR[1] = above
+        both_gains = half_gain * half_gain
+        YS[t + 1, 0, 0] = YS[t + 1, 0, 0] + half_gain * below
+        YS[t + 1, 0, 1] = YS[t + 1, 0, 1] + both_gains * YR[t, 0, 1]
+        YS[t + 1, 1, 0] = YS[t + 1, 1, 0] + both_gains * YR[t, 1, 0]
+        YS[t + 1, 1, 1] = YS[t + 1, 1, 1] - half_gain * above
+        for q in range(nq):
+            for jb in range(jbs):
+                rows, at = rows_of(jb)
+                far, near = XR[t, 0, q, 0, rows, :], XR[t, 0, q, 1, rows, :]
+                beside = VX[q, 0, rows, :] - half_gain * (XS[t, 0, q, 0, rows, :] - far)
+                VX[q, 0, rows, :] = beside
+                VX[q, 1, rows, :] = VX[q, 1, rows, :] + half_gain * near
+                first = PR[q, 0, at, :] + half_gain * beside
+                second = PR[q, 1, at, :] + both_gains * near
+                PR[q, 0, at, :] = first
+                PR[q, 1, at, :] = second
+                XS[t + 1, 0, q, 0, rows, :] = first
+                XS[t + 1, 0, q, 1, rows, :] = second
+                near, far = XR[t, 1, q, 0, rows, :], XR[t, 1, q, 1, rows, :]
+                beside = VX[q, cx + 1, rows, :] - half_gain * (far - XS[t, 1, q, 1, rows, :])
+                VX[q, cx + 1, rows, :] = beside
+                VX[q, cx, rows, :] = VX[q, cx, rows, :] - half_gain * near
+                first = PR[q, cx - 2, at, :] + both_gains * near
+                second = PR[q, cx - 1, at, :] - half_gain * beside
+                PR[q, cx - 2, at, :] = first
+                PR[q, cx - 1, at, :] = second
+                XS[t + 1, 1, q, 0, rows, :] = first
+                XS[t + 1, 1, q, 1, rows, :] = second
+        ends = ((0, 0, 0), (1, 0, 1), (cx - 2, 1, 0), (cx - 1, 1, 1))
+        for i, x_side, x_row in ends:
+            for side in range(2):
+                for r in range(2):
+                    for q in range(nq):
+                        row = one(edges[side][r])
+                        if i == 0:
+                            part_x = half_gain * VX[q, 0, row, :]
+                        elif i == 1:
+                            part_x = both_gains * XR[t, 0, q, 1, row, :]
+                        elif i == cx - 2:
+                            part_x = both_gains * XR[t, 1, q, 0, row, :]
+                        else:
+                            part_x = -half_gain * VX[q, cx + 1, row, :]
+                        value = YS[t + 1, side, r, q, one(i), :] + part_x
+                        YS[t + 1, side, r, q, one(i), :] = value
+                        XS[t + 1, x_side, q, x_row, row, :] = value
 
         @pl.when(t < STEPS - 1)
         def _():
+            start(lambda d: p_copy(t + 1, d), (2, 3))
             start(lambda d: p_copy(t + 1, d), (0, 1))
 
-        inner = range(2, cx - 2)
-        for i in inner:
-            side_rows(i)
-            for first in sorted({0, cy - 8}):
-                pressure(i, first)
-
-        @pl.when(t < STEPS - 1)
-        def _():
-            pack_rows(t + 1)
-            start(lambda d: p_copy(t + 1, d), (2, 3))
-
-        for i in inner:
-            for first in range(8, cy - 8, 8):
-                pressure(i, first)
+        unpack_rows(t + 1, range(cx))
+        for q in range(nq):
+            for i in range(cx):
+                low, high = one(8), one(7 + cy)
+                VY[q, i, low, :] = VY[q, i, low, :] + half_gain * YR[t, 0, 1, q, one(i), :]
+                VY[q, i, high, :] = VY[q, i, high, :] - half_gain * YR[t, 1, 0, q, one(i), :]
 
         @pl.when(t < STEPS - 1)
         def _():
@@ -599,6 +633,11 @@
     wait_sent(meta_copy)
     for t in range(STEPS):
         wait_sent(lambda d, t=t: dep_copy(t, d))
+        wait_sent(lambda d, t=t: p_copy(t, d), (2, 3) if t == 0 else (0, 1, 2, 3))
+    wait_sent(v_copy, (2, 3))
+    for d in range(2):
+        for copy in first_copies(d):
+            copy.wait_send()
 
 
 def write_out(p, vx, vy, vz, r, s, c, p_out, v_out, r_out, s_out, c_out, sems):
@@ -653,11 +692,12 @@
             pltpu.VMEM((ROWS, BLOCK), f32),
             pltpu.VMEM((ROWS, 2 * BLOCK), bf16),
             pltpu.VMEM((ncol, BLOCK), f32),
+            pltpu.VMEM((STEPS + 1, 2, nq, 2, cy, LANES), f32),
             pltpu.VMEM((STEPS, 2, nq, 2, cy, LANES), f32),
-            pltpu.VMEM((STEPS, 2, nq, cx, 2, LANES), f32),
-            pltpu.VMEM((STEPS, 2, nq, cx, 2, LANES), f32),
-            pltpu.VMEM((2, nq, cx, 1, LANES), f32),
-            pltpu.VMEM((2, nq, cx, 1, LANES), f32),
+            pltpu.VMEM((STEPS + 1, 2, 2, nq, cx, LANES), f32),
+            pltpu.VMEM((STEPS, 2, 2, nq, cx, LANES), f32),
+            pltpu.VMEM((2, nq, cx, LANES), f32),
+            pltpu.VMEM((2, nq, cx, LANES), f32),
             pltpu.VMEM((8, LANES), f32),
             pltpu.VMEM((4, 8, LANES), f32),
             pltpu.VMEM((ROWS, LANES), f32),

time: 45.3 us -> 44.8 us (0.989)
  Pallas kernels: 44.6 us -> 44 us
    pallas_call x1, Pallas kernels: 41.8 us -> 41.2 us  [on_device(): pl.pallas_call(kernel, out_shape=(vmem_out((nq, cx, cy + 16, LANES), f32)...]
where the time goes in v5:
time: 44.8 us; the launch traced here: 44.7 us
  Pallas kernels  44 us (98%)
  between operations  0.64 us (1%)
    pallas_call x1, Pallas kernels, on_device(): pl.pallas_call(kernel, out_shape=(vmem_out((nq, cx, cy + 16, LANES), f32)...  41.2 us
    pallas_call x1, Pallas kernels, on_device(): pl.pallas_call(write_out, out_shape=(jax.ShapeDtypeStruct(pressure.shape,...  2.8 us

profile of v5, /device:TPU:1, one launch (start us, length us, event | category | flops | bytes accessed | tf_op | source)
XLA Modules:
  0.0 44.7 jit_solution(2037204360342396807)
XLA Ops:
  0.6 41.2 %shard_map.119 = (f32[4,16,48,128]{3,2,1,0:T(8,128)S(1)}, f32[4,18,32,128]{3,2,1,0:T(8,128)S(1)}, f32[4,16,48,128]{3,2,1,0:T(8,128)S(1)}, f32[4,16,32,128]{3,2,1...) custom-call(s32[1024]{0:T(1024)} %cells_h.1, s32[4,1,1,8]{3,2,1,0:T(1,128)} %slot_h.1, ...), custom_call_target="tpu_custom_call" | custom-call | flops 10737418240 | bytes 13631488 | tf_op jit(solution)/shard_map/pallas_call | solution.py:669
  41.9 2.8 %shard_map.120 = (f32[16,32,512]{2,1,0:T(8,128)}, f32[3,16,32,512]{3,2,1,0:T(8,128)}, f32[1024,256]{1,0:T(8,128)}, f32[1024,256]{1,0:T(8,128)}, s32[8,128]{1,0:T(8,128)}) custom-call(f32[4,16,48,128]{3,2,1,0:T(8,128)S(1)} %get-tuple-element.17.p, f32[4,18,32,128]{3,2,1,0:T(8,128)S(1)} %get-tuple-element.18.vx, f32[4,16,48,128]{3,2,1,0:T(8,128)S(1)} %get-tuple-element.19.vy, ...), custom_call_target="tpu_custom_call" | custom-call | bytes 13631488 | tf_op jit(solution)/shard_map/pallas_call | solution.py:748

commit v6 on v5

--- a/solution.py
+++ b/solution.py
@@ -56,9 +56,9 @@
 
 def kernel(
     cells_h, slot_h, way_h, cells_b, press, vel, stretch, rest, speed0,
-    PR, VX, VY, VZ, r_out, s_out, c_out,
-    R, S, A, AR, SB, DB, OH, OHT, PHL, PG, VHL, SRC, XS, XR, YS, YR, VYS, VYR,
-    MT, MR, MSK, AMSK, LT, LR, PLACE, CAT, cells_s, slot_s, way_s, cells_v,
+    PR, VX, VY, VZ, R, S, MSK, PLACE, CAT, c_out,
+    A, AR, SB, DB, OH, OHT, PHL, PG, VHL, SRC, XS, XR, YS, YR, VYS, VYR,
+    MT, MR, AMSK, LT, LR, cells_s, slot_s, way_s, cells_v,
     in_sem, meta_s, meta_r, xs, xr, vs, vr, ds_, dr, fs, fr,
 ):
     _, cx, cy, nz = vel.shape
@@ -182,9 +182,16 @@
             SB.at[t], AR.at[:, pl.ds(t * 32 + d * DEP, DEP), :], ds_.at[t, d], dr.at[t, d], d
         )
 
+    odd = lax.rem(gy, 2) == 1
+    even = jnp.logical_not(odd)
+    far_hi, near_hi = has_hi & odd, has_hi & even
+    far_lo, near_lo = has_lo & even, has_lo & odd
+
     def start(make, ways=(0, 1, 2, 3)):
-        for d in ways:
-            under(sends[d], lambda d=d: make(d).start())
+        order = ((far_hi, 2), (far_lo, 3), (None, 0), (None, 1), (near_hi, 2), (near_lo, 3))
+        for flag, d in order:
+            if d in ways:
+                under(flag, lambda d=d: make(d).start())
 
     def wait_sent(make, ways=(0, 1, 2, 3)):
         for d in ways:
@@ -593,8 +600,7 @@
 
         @pl.when(t < STEPS - 1)
         def _():
-            start(lambda d: p_copy(t + 1, d), (2, 3))
-            start(lambda d: p_copy(t + 1, d), (0, 1))
+            start(lambda d: p_copy(t + 1, d))
 
         unpack_rows(t + 1, range(cx))
         for q in range(nq):
@@ -620,16 +626,6 @@
             CAT[0:ARRIVE, to] = high
             CAT[ARRIVE : 2 * ARRIVE, to] = low
 
-    def finish(m, carry):
-        rows = pl.ds(pl.multiple_of(m * LANES, LANES), LANES)
-        placed = jnp.dot(PLACE[rows, :], CAT[...], preferred_element_type=f32)
-        keep = MSK[rows, :]
-        keep = jnp.concatenate([keep, keep], axis=1) >= float(STEPS)
-        r_out[rows, :] = jnp.where(keep, R[rows, :], 0.0) + placed[:, :BLOCK]
-        s_out[rows, :] = (1.0 / time_step) * (jnp.where(keep, S[rows, :], 0.0) + placed[:, BLOCK:])
-        return carry
-
-    lax.fori_loop(0, SLOT_BLOCKS, finish, 0)
     wait_sent(meta_copy)
     for t in range(STEPS):
         wait_sent(lambda d, t=t: dep_copy(t, d))
@@ -640,18 +636,34 @@
             copy.wait_send()
 
 
-def write_out(p, vx, vy, vz, r, s, c, p_out, v_out, r_out, s_out, c_out, sems):
+def write_out(
+    p, vx, vy, vz, r, s, mask, place, cat, c, p_out, v_out, r_out, s_out, c_out, r_end, s_end, sems
+):
     _, cx, cy, nz = v_out.shape
-    pairs = [(r, r_out), (s, s_out), (c, c_out)]
+    pairs = []
     for q in range(nz // LANES):
         lanes = pl.ds(q * LANES, LANES)
         pairs.append((vx.at[q, pl.ds(1, cx), :, :], v_out.at[0, :, :, lanes]))
         pairs.append((vy.at[q, :, pl.ds(8, cy), :], v_out.at[1, :, :, lanes]))
         pairs.append((vz.at[q], v_out.at[2, :, :, lanes]))
         pairs.append((p.at[q, :, pl.ds(8, cy), :], p_out.at[:, :, lanes]))
+    pairs.append((c, c_out))
     copies = [pltpu.make_async_copy(a, b, sems.at[k]) for k, (a, b) in enumerate(pairs)]
     for copy in copies:
         copy.start()
+    count = 256
+    for first in range(0, SLOTS, count):
+        rows = slice(first, first + count)
+        placed = jnp.dot(place[rows, :], cat[...], preferred_element_type=f32)
+        keep = mask[rows, :]
+        keep = jnp.concatenate([keep, keep], axis=1) >= float(STEPS)
+        r_end[rows, :] = jnp.where(keep, r[rows, :], 0.0) + placed[:, :BLOCK]
+        s_end[rows, :] = (1.0 / time_step) * (jnp.where(keep, s[rows, :], 0.0) + placed[:, BLOCK:])
+        for a, b in ((r_end, r_out), (s_end, s_out)):
+            rows_of = pl.ds(first, count)
+            copy = pltpu.make_async_copy(a.at[rows_of, :], b.at[rows_of, :], sems.at[len(copies)])
+            copy.start()
+            copies.append(copy)
     for copy in copies:
         copy.wait()
 
@@ -673,15 +685,16 @@
             vmem_out((nq, cx + 2, cy, LANES), f32),
             vmem_out((nq, cx, cy + 16, LANES), f32),
             vmem_out((nq, cx, cy, LANES), f32),
-            vmem_out((SLOTS, BLOCK), f32),
-            vmem_out((SLOTS, BLOCK), f32),
+            vmem_out((ROWS, BLOCK), f32),
+            vmem_out((ROWS, BLOCK), f32),
+            vmem_out((ROWS, LANES), f32),
+            vmem_out((SLOTS, 2 * ARRIVE), bf16),
+            vmem_out((2 * ARRIVE, 2 * BLOCK), bf16),
             vmem_out((SLOT_BLOCKS, LANES), jnp.int32),
         ),
         in_specs=[pl.BlockSpec(memory_space=pltpu.HBM)] * 9,
-        out_specs=(vmem,) * 7,
+        out_specs=(vmem,) * 10,
         scratch_shapes=[
-            pltpu.VMEM((ROWS, BLOCK), f32),
-            pltpu.VMEM((ROWS, BLOCK), f32),
             pltpu.VMEM((ROWS, BLOCK), f32),
             pltpu.VMEM((3, ARRIVE, BLOCK), f32),
             pltpu.VMEM((STEPS, 3, DEP, BLOCK), f32),
@@ -700,12 +713,9 @@
             pltpu.VMEM((2, nq, cx, LANES), f32),
             pltpu.VMEM((8, LANES), f32),
             pltpu.VMEM((4, 8, LANES), f32),
-            pltpu.VMEM((ROWS, LANES), f32),
             pltpu.VMEM((ARRIVE, LANES), f32),
             pltpu.VMEM((LANES, LANES), f32),
             pltpu.VMEM((16, LANES), f32),
-            pltpu.VMEM((SLOTS, 2 * ARRIVE), bf16),
-            pltpu.VMEM((2 * ARRIVE, 2 * BLOCK), bf16),
             pltpu.SMEM((SLOTS,), jnp.int32),
             pltpu.SMEM((STEPS, 1, 1, DEP), jnp.int32),
             pltpu.SMEM((STEPS, 1, 1, DEP), jnp.int32),
@@ -754,10 +764,14 @@
             jax.ShapeDtypeStruct(stretch.shape, f32),
             jax.ShapeDtypeStruct((SLOT_BLOCKS, LANES), jnp.int32),
         ),
-        in_specs=[vmem] * 7,
+        in_specs=[vmem] * 10,
         out_specs=(hbm,) * 5,
-        scratch_shapes=[dma((4 * nq + 3,))],
-        compiler_params=pltpu.CompilerParams(vmem_limit_bytes=4 * 2**20),
+        scratch_shapes=[
+            pltpu.VMEM((SLOTS, BLOCK), f32),
+            pltpu.VMEM((SLOTS, BLOCK), f32),
+            dma((4 * nq + 1 + 8,)),
+        ],
+        compiler_params=pltpu.CompilerParams(vmem_limit_bytes=8 * 2**20),
         cost_estimate=pl.CostEstimate(flops=0, bytes_accessed=13 * 2**20, transcendentals=0),
     )(*parts)
     return p, v, r, s, c.reshape(-1)

time: 44.8 us -> 43.4 us (0.969)
  Pallas kernels: 44 us -> 42.7 us
    pallas_call x1, Pallas kernels: 41.2 us -> 39.8 us  [on_device(): pl.pallas_call(kernel, out_shape=(vmem_out((nq, cx, cy + 16, LANES), f32)...]
where the time goes in v6:
time: 43.4 us; the launch traced here: 43.3 us
  Pallas kernels  42.7 us (98%)
  between operations  0.64 us (1%)
    pallas_call x1, Pallas kernels, on_device(): pl.pallas_call(kernel, out_shape=(vmem_out((nq, cx, cy + 16, LANES), f32)...  39.8 us
    pallas_call x1, Pallas kernels, on_device(): pl.pallas_call(write_out, out_shape=(jax.ShapeDtypeStruct(pressure.shape,...  2.86 us

profile of v6, /device:TPU:1, one launch (start us, length us, event | category | flops | bytes accessed | tf_op | source)
XLA Modules:
  0.0 43.3 jit_solution(3347835655508919268)
XLA Ops:
  0.6 39.8 %shard_map.119 = (f32[4,16,48,128]{3,2,1,0:T(8,128)S(1)}, f32[4,18,32,128]{3,2,1,0:T(8,128)S(1)}, f32[4,16,48,128]{3,2,1,0:T(8,128)S(1)}, f32[4,16,32,128]{3,2,1...) custom-call(s32[1024]{0:T(1024)} %cells_h.1, ...), custom_call_target="tpu_custom_call" | custom-call | flops 10737418240 | bytes 13631488 | tf_op jit(solution)/shard_map/pallas_call | solution.py:681
  40.5 2.9 %shard_map.120 = (f32[16,32,512]{2,1,0:T(8,128)}, f32[3,16,32,512]{3,2,1,0:T(8,128)}, f32[1024,256]{1,0:T(8,128)}, f32[1024,256]{1,0:T(8,128)}, s32[8,128]{1,0:T(8,128)}) custom-call(f32[4,16,48,128]{3,2,1,0:T(8,128)S(1)} %get-tuple-element.20.p, f32[4,18,32,128]{3,2,1,0:T(8,128)S(1)} %get-tuple-element.21.vx, f32[4,16,48,128]{3,2,1,0:T(8,128)S(1)} %get-tuple-element.22.vy, ...), custom_call_target="tpu_custom_call" | custom-call | bytes 13631488 | tf_op jit(solution)/shard_map/pallas_call | solution.py:758

commit v7 on v6

--- a/solution.py
+++ b/solution.py
@@ -150,12 +150,17 @@
         )
 
     def meta_copy(d):
-        return remote(MT, MR.at[d], meta_s.at[d], meta_r.at[d], d)
+        return [remote(MT, MR.at[d], meta_s.at[d], meta_r.at[d], d)]
+
+    pieces = nq
 
     def p_copy(t, d):
-        if d < 2:
-            return remote(XS.at[t, 1 - d], XR.at[t, d], xs.at[t, d], xr.at[t, d], d)
-        return remote(YS.at[t, 3 - d], YR.at[t, d - 2], xs.at[t, d], xr.at[t, d], d)
+        for k in range(pieces):
+            sems = xs.at[t, d, k], xr.at[t, d, k]
+            if d < 2:
+                yield remote(XS.at[t, 1 - d, k], XR.at[t, d, k], *sems, d)
+            else:
+                yield remote(YS.at[t, 3 - d, :, k], YR.at[t, d - 2, :, k], *sems, d)
 
     def first_copies(d):
         side = (cx - 2, 0)[d]
@@ -175,12 +180,11 @@
             )
 
     def v_copy(d):
-        return remote(VYS.at[3 - d], VYR.at[d - 2], vs.at[d], vr.at[d], d)
+        return [remote(VYS.at[3 - d], VYR.at[d - 2], vs.at[d], vr.at[d], d)]
 
     def dep_copy(t, d):
-        return remote(
-            SB.at[t], AR.at[:, pl.ds(t * 32 + d * DEP, DEP), :], ds_.at[t, d], dr.at[t, d], d
-        )
+        to = AR.at[:, pl.ds(t * 32 + d * DEP, DEP), :]
+        return [remote(SB.at[t], to, ds_.at[t, d], dr.at[t, d], d)]
 
     odd = lax.rem(gy, 2) == 1
     even = jnp.logical_not(odd)
@@ -191,15 +195,15 @@
         order = ((far_hi, 2), (far_lo, 3), (None, 0), (None, 1), (near_hi, 2), (near_lo, 3))
         for flag, d in order:
             if d in ways:
-                under(flag, lambda d=d: make(d).start())
+                under(flag, lambda d=d: [copy.start() for copy in make(d)] and None)
 
     def wait_sent(make, ways=(0, 1, 2, 3)):
         for d in ways:
-            under(sends[d], lambda d=d: make(d).wait_send())
+            under(sends[d], lambda d=d: [copy.wait_send() for copy in make(d)] and None)
 
     def wait_taken(make, ways=(0, 1, 2, 3)):
         for d in ways:
-            under(takes[d], lambda d=d: make(d).wait_recv())
+            under(takes[d], lambda d=d: [copy.wait_recv() for copy in make(d)] and None)
 
     for d in range(2):
         for copy in first_copies(d):
@@ -209,19 +213,24 @@
     def one(row):
         return pl.ds(row + zero_row, 1)
 
+    pitch = cy + 16
+    PR_rows = PR.reshape(nq * cx * pitch, LANES)
+    VY_rows = VY.reshape(nq * cx * pitch, LANES)
+
+    def across(q, row):
+        return pl.ds(q * cx * pitch + 8 + row, cx, stride=pitch), slice(None)
+
     def pack_rows(t):
         for side in range(2):
             for r in range(2):
                 for q in range(nq):
-                    for i in range(cx):
-                        YS[t, side, r, q, one(i), :] = PR[q, i, one(8 + edges[side][r]), :]
-
-    def unpack_rows(t, planes_now):
+                    YS[t, side, r, q] = PR_rows[across(q, edges[side][r])]
+
+    def unpack_rows(t):
         for side in range(2):
             for r in range(2):
                 for q in range(nq):
-                    for i in planes_now:
-                        PR[q, i, one(8 + edges[side][r]), :] = YS[t, side, r, q, one(i), :]
+                    PR_rows[across(q, edges[side][r])] = YS[t, side, r, q]
 
     def column_row(i, h, jb):
         return (i // planes) * part + (h * planes + i % planes) * cy + jb * 16
@@ -253,9 +262,8 @@
     for k in range(nq, 2 * nq):
         loads[k].wait()
     for q in range(nq):
-        for i in range(cx):
-            VYS[0, q, one(i), :] = VY[q, i, one(8), :]
-            VYS[1, q, one(i), :] = VY[q, i, one(7 + cy), :]
+        VYS[0, q] = VY_rows[across(q, 0)]
+        VYS[1, q] = VY_rows[across(q, cy - 1)]
     start(v_copy, (2, 3))
 
     for load in small_loads:
@@ -602,12 +610,11 @@
         def _():
             start(lambda d: p_copy(t + 1, d))
 
-        unpack_rows(t + 1, range(cx))
+        unpack_rows(t + 1)
         for q in range(nq):
-            for i in range(cx):
-                low, high = one(8), one(7 + cy)
-                VY[q, i, low, :] = VY[q, i, low, :] + half_gain * YR[t, 0, 1, q, one(i), :]
-                VY[q, i, high, :] = VY[q, i, high, :] - half_gain * YR[t, 1, 0, q, one(i), :]
+            low, high = across(q, 0), across(q, cy - 1)
+            VY_rows[low] = VY_rows[low] + half_gain * YR[t, 0, 1, q]
+            VY_rows[high] = VY_rows[high] - half_gain * YR[t, 1, 0, q]
 
         @pl.when(t < STEPS - 1)
         def _():
@@ -723,8 +730,8 @@
             dma((4 * nq + 7,)),
             dma((4,)),
             dma((4,)),
-            dma((STEPS, 4)),
-            dma((STEPS, 4)),
+            dma((STEPS, 4, nq)),
+            dma((STEPS, 4, nq)),
             dma((4,)),
             dma((4,)),
             dma((STEPS, 4)),

time: 43.4 us -> 44.4 us (1.023)
  Pallas kernels: 42.7 us -> 43.7 us
    pallas_call x1, Pallas kernels: 39.8 us -> 40.8 us  [on_device(): pl.pallas_call(kernel, out_shape=(vmem_out((nq, cx, cy + 16, LANES), f32)...]
where the time goes in v7:
time: 44.4 us; the launch traced here: 44.3 us
  Pallas kernels  43.7 us (98%)
  between operations  0.64 us (1%)
    pallas_call x1, Pallas kernels, on_device(): pl.pallas_call(kernel, out_shape=(vmem_out((nq, cx, cy + 16, LANES), f32)...  40.8 us
    pallas_call x1, Pallas kernels, on_device(): pl.pallas_call(write_out, out_shape=(jax.ShapeDtypeStruct(pressure.shape,...  2.86 us

profile of v7, /device:TPU:1, one launch (start us, length us, event | category | flops | bytes accessed | tf_op | source)
XLA Modules:
  0.0 44.3 jit_solution(11119519858637285726)
XLA Ops:
  0.6 40.8 %shard_map.119 = (f32[4,16,48,128]{3,2,1,0:T(8,128)S(1)}, f32[4,18,32,128]{3,2,1,0:T(8,128)S(1)}, f32[4,16,48,128]{3,2,1,0:T(8,128)S(1)}, f32[4,16,32,128]{3,2,1...) custom-call(s32[1024]{0:T(1024)} %cells_h.1, ...), custom_call_target="tpu_custom_call" | custom-call | flops 10737418240 | bytes 13631488 | tf_op jit(solution)/shard_map/pallas_call | solution.py:688
  41.4 2.9 %shard_map.120 = (f32[16,32,512]{2,1,0:T(8,128)}, f32[3,16,32,512]{3,2,1,0:T(8,128)}, f32[1024,256]{1,0:T(8,128)}, f32[1024,256]{1,0:T(8,128)}, s32[8,128]{1,0:T(8,128)}) custom-call(f32[4,16,48,128]{3,2,1,0:T(8,128)S(1)} %get-tuple-element.20.p, f32[4,18,32,128]{3,2,1,0:T(8,128)S(1)} %get-tuple-element.21.vx, f32[4,16,48,128]{3,2,1,0:T(8,128)S(1)} %get-tuple-element.22.vy, ...), custom_call_target="tpu_custom_call" | custom-call | bytes 13631488 | tf_op jit(solution)/shard_map/pallas_call | solution.py:765

commit v8 on v7

--- a/solution.py
+++ b/solution.py
@@ -56,7 +56,7 @@
 
 def kernel(
     cells_h, slot_h, way_h, cells_b, press, vel, stretch, rest, speed0,
-    PR, VX, VY, VZ, R, S, MSK, PLACE, CAT, c_out,
+    PR, VX, VY, VZ, R, S, MSK, CAT, INFO,
     A, AR, SB, DB, OH, OHT, PHL, PG, VHL, SRC, XS, XR, YS, YR, VYS, VYR,
     MT, MR, AMSK, LT, LR, cells_s, slot_s, way_s, cells_v,
     in_sem, meta_s, meta_r, xs, xr, vs, vr, ds_, dr, fs, fr,
@@ -140,6 +140,7 @@
     A[SLOTS:ROWS, :] = empty
     MSK[SLOTS:ROWS, :] = jnp.full((ARRIVE, LANES), -1.0, f32)
     OHT[:, SLOTS:ROWS] = jnp.zeros((ncol, ARRIVE), bf16)
+    VHL[ROWS - 32 : ROWS, :] = jnp.zeros((32, 2 * BLOCK), bf16)
     OH[SLOTS:ROWS, :] = jnp.zeros((ARRIVE, ncol), bf16)
     pl.semaphore_wait(barrier, 2 + has_lo.astype(jnp.int32) + has_hi.astype(jnp.int32))
 
@@ -152,15 +153,12 @@
     def meta_copy(d):
         return [remote(MT, MR.at[d], meta_s.at[d], meta_r.at[d], d)]
 
-    pieces = nq
-
     def p_copy(t, d):
-        for k in range(pieces):
-            sems = xs.at[t, d, k], xr.at[t, d, k]
-            if d < 2:
-                yield remote(XS.at[t, 1 - d, k], XR.at[t, d, k], *sems, d)
-            else:
-                yield remote(YS.at[t, 3 - d, :, k], YR.at[t, d - 2, :, k], *sems, d)
+        if d < 2:
+            src, dst = XS.at[t, 1 - d], XR.at[t, d]
+        else:
+            src, dst = YS.at[t, 3 - d], YR.at[t, d - 2]
+        return [remote(src, dst, xs.at[t, d], xr.at[t, d], d)]
 
     def first_copies(d):
         side = (cx - 2, 0)[d]
@@ -251,21 +249,6 @@
                 for q in range(nq):
                     keep_parts(i, jb, q, PR[q, i, rows_of(jb)[1], :])
 
-    for k in range(nq):
-        loads[k].wait()
-    pack_rows(0)
-    start(lambda d: p_copy(0, d), (2, 3))
-    for q in range(nq):
-        for r in range(2):
-            XS[0, 0, q, r] = PR[q, r, 8 : 8 + cy, :]
-            XS[0, 1, q, r] = PR[q, cx - 2 + r, 8 : 8 + cy, :]
-    for k in range(nq, 2 * nq):
-        loads[k].wait()
-    for q in range(nq):
-        VYS[0, q] = VY_rows[across(q, 0)]
-        VYS[1, q] = VY_rows[across(q, cy - 1)]
-    start(v_copy, (2, 3))
-
     for load in small_loads:
         load.wait()
 
@@ -287,8 +270,6 @@
 
     start(meta_copy)
 
-    split_all()
-
     lrow = lax.broadcasted_iota(jnp.int32, (LANES, LANES), 0)
     lcol = lax.broadcasted_iota(jnp.int32, (LANES, LANES), 1)
     wide = lax.broadcasted_iota(jnp.int32, (16, ncol), 1).astype(f32)
@@ -334,6 +315,21 @@
         )
     hot_columns(0, SLOT_BLOCKS)
 
+    for k in range(nq):
+        loads[k].wait()
+    pack_rows(0)
+    start(lambda d: p_copy(0, d), (2, 3))
+    for q in range(nq):
+        for r in range(2):
+            XS[0, 0, q, r] = PR[q, r, 8 : 8 + cy, :]
+            XS[0, 1, q, r] = PR[q, cx - 2 + r, 8 : 8 + cy, :]
+    for k in range(nq, 2 * nq):
+        loads[k].wait()
+    for q in range(nq):
+        VYS[0, q] = VY_rows[across(q, 0)]
+        VYS[1, q] = VY_rows[across(q, cy - 1)]
+    start(v_copy, (2, 3))
+
     for k in range(2 * nq, 2 * nq + 3):
         loads[k].wait()
 
@@ -358,49 +354,15 @@
         alab = jnp.where(
             came == 0, MR[0], jnp.where(came == 1, MR[1], jnp.where(came == 2, MR[2], MR[3]))
         )
-        present = alab > 0.0
-        upper = jnp.where(lrow <= lcol, 1.0, 0.0)
-        upper_block = jnp.where(lrow // 32 == lcol // 32, upper, 0.0).astype(bf16)
-        upper = upper.astype(bf16)
-        ones = jnp.ones((LANES, LANES), bf16)
-        present_f = jnp.where(present, 1.0, 0.0)
-        arank = jnp.dot(present_f.astype(bf16), upper_block, preferred_element_type=f32) - 1.0
-        arank = jnp.where(present, arank, -5.0)
-        vacant = label == 0
-        ranks = []
-        for t in range(STEPS):
-            vacant = vacant | (leave_at == t)
-            flag = jnp.where(vacant, 1.0, 0.0).astype(bf16)
-            rank = jnp.dot(flag, upper, preferred_element_type=f32) - 1.0
-            total = jnp.dot(flag, ones, preferred_element_type=f32)
-            for r in range(SLOT_BLOCKS - 1):
-                rank = rank + jnp.where(sub8 > r, total[r : r + 1, :], 0.0)
-            ranks.append(jnp.where(vacant, rank, -1.0))
-            count = jnp.sum(jnp.where(lane8 // 32 == t, present_f, 0.0), axis=1, keepdims=True)
-            vacant = vacant & (rank >= count)
-
         acode = code_of(alab.astype(jnp.int32))
-        turn(ranks + [acode, alab])
+        turn([acode, alab])
         LR[8:16, :] = acode
-        hot_rows(SLOT_BLOCKS, 32)
+        hot_rows(SLOT_BLOCKS, 0)
         hot_columns(SLOT_BLOCKS, SLOT_BLOCKS + 1)
-        AMSK[...] = jnp.broadcast_to(LT[:, 40:41], (LANES, LANES))
-
-        group = lcol // 32
-        alab_high, alab_low = split(alab)
-        final = jnp.where(leave_at == STEPS, label, 0).astype(f32)
-        nt = (((1,), (1,)), ((), ()))
-        for r in range(SLOT_BLOCKS):
-            mine = jnp.broadcast_to(LT[:, r : r + 1], (LANES, LANES))
-            for t in range(1, STEPS):
-                mine = jnp.where(group == t, LT[:, 8 * t + r : 8 * t + r + 1], mine)
-            hot = jnp.where(mine == arank[0:1, :], 1.0, 0.0).astype(bf16)
-            PLACE[r * LANES : (r + 1) * LANES, 0:LANES] = hot
-            PLACE[r * LANES : (r + 1) * LANES, LANES : 2 * LANES] = hot
-            placed = lax.dot_general(alab_high, hot, nt, preferred_element_type=f32)
-            placed = placed + lax.dot_general(alab_low, hot, nt, preferred_element_type=f32)
-            final = final + jnp.where(sub8 == r, placed, 0.0)
-        c_out[...] = final.astype(jnp.int32) - 1
+        AMSK[...] = jnp.broadcast_to(LT[:, 8:9], (LANES, LANES))
+        INFO[0] = label.astype(f32)
+        INFO[1] = leave_at.astype(f32)
+        INFO[2] = alab
 
     def slope_z(tiles):
         height = tiles[0].shape[0]
@@ -430,28 +392,7 @@
         both = jnp.dot(OHT[...], VHL[:, pair], preferred_element_type=f32)
         SRC[:, narrow] = both[:, :LANES] + both[:, LANES:]
 
-    def take_arrivals(t):
-        wait_taken(lambda d: dep_copy(t, d))
-        rows = pl.ds(pl.multiple_of(t * 32, 32), 32)
-        to = pl.ds(pl.multiple_of(SLOTS + t * 32, 32), 32)
-        R[to, :] = AR[0, rows, :]
-        S[to, :] = AR[1, rows, :]
-        A[to, :] = AR[2, rows, :]
-        MSK[to, :] = jnp.where(AMSK[rows, :] > 0.0, 2.0 * STEPS, -1.0)
-
-    def step(t, carry):
-        limit = t.astype(f32)
-
-        def bubbles(first, w):
-            rows = slice(first, first + 16)
-            col = halves(w)[0]
-            radius, speed, rate = wall_update(R[rows, col], S[rows, col], A[rows, col], PG[rows, col])
-            R[rows, col] = radius
-            S[rows, col] = speed
-            high, low = split(jnp.where(MSK[rows, :] >= limit, rate, 0.0))
-            VHL[rows, 2 * w * LANES : (2 * w + 1) * LANES] = high
-            VHL[rows, (2 * w + 1) * LANES : (2 * w + 2) * LANES] = low
-
+    def leavers(t, to):
         for k in range(DEP):
             slot = jnp.maximum(slot_s[t, 0, 0, k], 0)
             cell = jnp.maximum(cells_s[slot], 0)
@@ -468,21 +409,50 @@
                     :,
                 ]
         radius, speed, _ = wall_update(DB[0], DB[1], DB[2], DB[3])
-        SB[t, 0] = radius
-        SB[t, 1] = speed
-        SB[t, 2] = DB[2]
-        start(lambda d: dep_copy(t, d))
+        SB[to, 0] = radius
+        SB[to, 1] = speed
+        SB[to, 2] = DB[2]
+
+    def take_arrivals(t):
+        wait_taken(lambda d: dep_copy(t, d))
+        rows = pl.ds(pl.multiple_of(t * 32, 32), 32)
+        to = pl.ds(pl.multiple_of(SLOTS + t * 32, 32), 32)
+        R[to, :] = AR[0, rows, :]
+        S[to, :] = AR[1, rows, :]
+        A[to, :] = AR[2, rows, :]
+        MSK[to, :] = jnp.where(AMSK[rows, :] > 0.0, 2.0 * STEPS, -1.0)
+
+    def step(t, carry):
+        limit = t.astype(f32)
+
+        def bubbles(first, w):
+            rows = slice(first, first + 16)
+            col = halves(w)[0]
+            radius, speed, rate = wall_update(R[rows, col], S[rows, col], A[rows, col], PG[rows, col])
+            R[rows, col] = radius
+            S[rows, col] = speed
+            high, low = split(jnp.where(MSK[rows, :] >= limit, rate, 0.0))
+            VHL[rows, 2 * w * LANES : (2 * w + 1) * LANES] = high
+            VHL[rows, (2 * w + 1) * LANES : (2 * w + 2) * LANES] = low
 
         @pl.when(t > 0)
         def _():
             take_arrivals(t - 1)
 
+        split_all()
+        last = t // (STEPS - 1)
+        leavers(t, t + last)
         gather(0)
+
+        @pl.when(last == 0)
+        def _():
+            start(lambda d: dep_copy(t, d))
+
         gather(1)
-        for first in range(0, ROWS, 16):
+        for first in range(0, ROWS - 32, 16):
             bubbles(first, 0)
         scatter(0)
-        for first in range(0, ROWS, 16):
+        for first in range(0, ROWS - 32, 16):
             bubbles(first, 1)
         scatter(1)
 
@@ -616,9 +586,18 @@
             VY_rows[low] = VY_rows[low] + half_gain * YR[t, 0, 1, q]
             VY_rows[high] = VY_rows[high] - half_gain * YR[t, 1, 0, q]
 
-        @pl.when(t < STEPS - 1)
+        @pl.when(t == STEPS - 2)
         def _():
-            split_all()
+            leavers(t + 1, t + 1)
+            start(lambda d: dep_copy(t + 1, d))
+
+        wait_sent(lambda d: dep_copy(t, d))
+
+        @pl.when(t > 0)
+        def _():
+            wait_sent(lambda d: p_copy(t, d), (0, 1))
+
+        wait_sent(lambda d: p_copy(t, d), (2, 3))
 
         return carry
 
@@ -634,9 +613,6 @@
             CAT[ARRIVE : 2 * ARRIVE, to] = low
 
     wait_sent(meta_copy)
-    for t in range(STEPS):
-        wait_sent(lambda d, t=t: dep_copy(t, d))
-        wait_sent(lambda d, t=t: p_copy(t, d), (2, 3) if t == 0 else (0, 1, 2, 3))
     wait_sent(v_copy, (2, 3))
     for d in range(2):
         for copy in first_copies(d):
@@ -644,7 +620,7 @@
 
 
 def write_out(
-    p, vx, vy, vz, r, s, mask, place, cat, c, p_out, v_out, r_out, s_out, c_out, r_end, s_end, sems
+    p, vx, vy, vz, r, s, mask, cat, info, p_out, v_out, r_out, s_out, c_out, r_end, s_end, c_end, lt, sems
 ):
     _, cx, cy, nz = v_out.shape
     pairs = []
@@ -654,23 +630,66 @@
         pairs.append((vy.at[q, :, pl.ds(8, cy), :], v_out.at[1, :, :, lanes]))
         pairs.append((vz.at[q], v_out.at[2, :, :, lanes]))
         pairs.append((p.at[q, :, pl.ds(8, cy), :], p_out.at[:, :, lanes]))
-    pairs.append((c, c_out))
     copies = [pltpu.make_async_copy(a, b, sems.at[k]) for k, (a, b) in enumerate(pairs)]
     for copy in copies:
         copy.start()
-    count = 256
-    for first in range(0, SLOTS, count):
-        rows = slice(first, first + count)
-        placed = jnp.dot(place[rows, :], cat[...], preferred_element_type=f32)
+
+    lane8 = lax.broadcasted_iota(jnp.int32, (8, LANES), 1)
+    sub8 = lax.broadcasted_iota(jnp.int32, (8, LANES), 0)
+    lrow = lax.broadcasted_iota(jnp.int32, (LANES, LANES), 0)
+    lcol = lax.broadcasted_iota(jnp.int32, (LANES, LANES), 1)
+    label, leave_at, alab = info[0], info[1], info[2]
+    present = alab > 0.0
+    upper = jnp.where(lrow <= lcol, 1.0, 0.0)
+    upper_block = jnp.where(lrow // 32 == lcol // 32, upper, 0.0).astype(bf16)
+    upper = upper.astype(bf16)
+    ones = jnp.ones((LANES, LANES), bf16)
+    present_f = jnp.where(present, 1.0, 0.0)
+    arank = jnp.dot(present_f.astype(bf16), upper_block, preferred_element_type=f32) - 1.0
+    arank = jnp.where(present, arank, -5.0)
+    vacant = label == 0.0
+    ranks = []
+    for t in range(STEPS):
+        vacant = vacant | (leave_at == float(t))
+        flag = jnp.where(vacant, 1.0, 0.0).astype(bf16)
+        rank = jnp.dot(flag, upper, preferred_element_type=f32) - 1.0
+        total = jnp.dot(flag, ones, preferred_element_type=f32)
+        for k in range(SLOT_BLOCKS - 1):
+            rank = rank + jnp.where(sub8 > k, total[k : k + 1, :], 0.0)
+        ranks.append(jnp.where(vacant, rank, -1.0))
+        count = jnp.sum(jnp.where(lane8 // 32 == t, present_f, 0.0), axis=1, keepdims=True)
+        vacant = vacant & (rank >= count)
+    lt[...] = jnp.concatenate(ranks + [jnp.zeros((LANES - 8 * STEPS, LANES), f32)], axis=0).T
+
+    group = lcol // 32
+    alab_high, alab_low = split(alab)
+    final = jnp.where(leave_at == float(STEPS), label, 0.0)
+    nt = (((1,), (1,)), ((), ()))
+    for k in range(SLOT_BLOCKS):
+        rows = slice(k * LANES, (k + 1) * LANES)
+        mine = jnp.broadcast_to(lt[:, k : k + 1], (LANES, LANES))
+        for t in range(1, STEPS):
+            mine = jnp.where(group == t, lt[:, 8 * t + k : 8 * t + k + 1], mine)
+        hot = jnp.where(mine == arank[0:1, :], 1.0, 0.0).astype(bf16)
+        there = lax.dot_general(alab_high, hot, nt, preferred_element_type=f32)
+        there = there + lax.dot_general(alab_low, hot, nt, preferred_element_type=f32)
+        final = final + jnp.where(sub8 == k, there, 0.0)
+        both = jnp.concatenate([hot, hot], axis=1)
+        placed = jnp.dot(both, cat[...], preferred_element_type=f32)
         keep = mask[rows, :]
         keep = jnp.concatenate([keep, keep], axis=1) >= float(STEPS)
         r_end[rows, :] = jnp.where(keep, r[rows, :], 0.0) + placed[:, :BLOCK]
         s_end[rows, :] = (1.0 / time_step) * (jnp.where(keep, s[rows, :], 0.0) + placed[:, BLOCK:])
-        for a, b in ((r_end, r_out), (s_end, s_out)):
-            rows_of = pl.ds(first, count)
-            copy = pltpu.make_async_copy(a.at[rows_of, :], b.at[rows_of, :], sems.at[len(copies)])
-            copy.start()
-            copies.append(copy)
+        if k % 4 == 3:
+            rows_of = pl.ds((k - 3) * LANES, 4 * LANES)
+            for a, b in ((r_end, r_out), (s_end, s_out)):
+                copy = pltpu.make_async_copy(a.at[rows_of, :], b.at[rows_of, :], sems.at[len(copies)])
+                copy.start()
+                copies.append(copy)
+    c_end[...] = final.astype(jnp.int32) - 1
+    copy = pltpu.make_async_copy(c_end, c_out, sems.at[len(copies)])
+    copy.start()
+    copies.append(copy)
     for copy in copies:
         copy.wait()
 
@@ -695,16 +714,15 @@
             vmem_out((ROWS, BLOCK), f32),
             vmem_out((ROWS, BLOCK), f32),
             vmem_out((ROWS, LANES), f32),
-            vmem_out((SLOTS, 2 * ARRIVE), bf16),
             vmem_out((2 * ARRIVE, 2 * BLOCK), bf16),
-            vmem_out((SLOT_BLOCKS, LANES), jnp.int32),
+            vmem_out((3, SLOT_BLOCKS, LANES), f32),
         ),
         in_specs=[pl.BlockSpec(memory_space=pltpu.HBM)] * 9,
-        out_specs=(vmem,) * 10,
+        out_specs=(vmem,) * 9,
         scratch_shapes=[
             pltpu.VMEM((ROWS, BLOCK), f32),
             pltpu.VMEM((3, ARRIVE, BLOCK), f32),
-            pltpu.VMEM((STEPS, 3, DEP, BLOCK), f32),
+            pltpu.VMEM((STEPS + 1, 3, DEP, BLOCK), f32),
             pltpu.VMEM((4, DEP, BLOCK), f32),
             pltpu.VMEM((ROWS, ncol), bf16),
             pltpu.VMEM((ncol, ROWS), bf16),
@@ -730,8 +748,8 @@
             dma((4 * nq + 7,)),
             dma((4,)),
             dma((4,)),
-            dma((STEPS, 4, nq)),
-            dma((STEPS, 4, nq)),
+            dma((STEPS, 4)),
+            dma((STEPS, 4)),
             dma((4,)),
             dma((4,)),
             dma((STEPS, 4)),
@@ -771,12 +789,14 @@
             jax.ShapeDtypeStruct(stretch.shape, f32),
             jax.ShapeDtypeStruct((SLOT_BLOCKS, LANES), jnp.int32),
         ),
-        in_specs=[vmem] * 10,
+        in_specs=[vmem] * 9,
         out_specs=(hbm,) * 5,
         scratch_shapes=[
             pltpu.VMEM((SLOTS, BLOCK), f32),
             pltpu.VMEM((SLOTS, BLOCK), f32),
-            dma((4 * nq + 1 + 8,)),
+            pltpu.VMEM((SLOT_BLOCKS, LANES), jnp.int32),
+            pltpu.VMEM((LANES, LANES), f32),
+            dma((4 * nq + 5,)),
         ],
         compiler_params=pltpu.CompilerParams(vmem_limit_bytes=8 * 2**20),
         cost_estimate=pl.CostEstimate(flops=0, bytes_accessed=13 * 2**20, transcendentals=0),

time: 44.4 us -> 42.9 us (0.966)
  Pallas kernels: 43.7 us -> 42.2 us
    pallas_call x1, Pallas kernels: 40.8 us -> 39.4 us  [on_device(): pl.pallas_call(kernel, out_shape=(vmem_out((nq, cx, cy + 16, LANES), f32)...]
where the time goes in v8:
time: 42.9 us; the launch traced here: 42.8 us
  Pallas kernels  42.2 us (98%)
  between operations  0.64 us (1%)
    pallas_call x1, Pallas kernels, on_device(): pl.pallas_call(kernel, out_shape=(vmem_out((nq, cx, cy + 16, LANES), f32)...  39.4 us
    pallas_call x1, Pallas kernels, on_device(): pl.pallas_call(write_out, out_shape=(jax.ShapeDtypeStruct(pressure.shape,...  2.83 us

profile of v8, /device:TPU:1, one launch (start us, length us, event | category | flops | bytes accessed | tf_op | source)
XLA Modules:
  0.0 42.8 jit_solution(6696291568015264119)
XLA Ops:
  0.6 39.4 %shard_map.119 = (f32[4,16,48,128]{3,2,1,0:T(8,128)S(1)}, f32[4,18,32,128]{3,2,1,0:T(8,128)S(1)}, f32[4,16,48,128]{3,2,1,0:T(8,128)S(1)}, f32[4,16,32,128]{3,2,1...) custom-call(s32[1024]{0:T(1024)} %cells_h.1, ...), custom_call_target="tpu_custom_call" | custom-call | flops 10737418240 | bytes 13631488 | tf_op jit(solution)/shard_map/pallas_call | solution.py:707
  40.0 2.8 %shard_map.120 = (f32[16,32,512]{2,1,0:T(8,128)}, f32[3,16,32,512]{3,2,1,0:T(8,128)}, f32[1024,256]{1,0:T(8,128)}, f32[1024,256]{1,0:T(8,128)}, s32[8,128]{1,0:T(8,128)}) custom-call(f32[4,16,48,128]{3,2,1,0:T(8,128)S(1)} %get-tuple-element.19.p, f32[4,18,32,128]{3,2,1,0:T(8,128)S(1)} %get-tuple-element.20.vx, f32[4,16,48,128]{3,2,1,0:T(8,128)S(1)} %get-tuple-element.21.vy, ...), custom_call_target="tpu_custom_call" | custom-call | bytes 13631488 | tf_op jit(solution)/shard_map/pallas_call | solution.py:783

commit v9 on v8

--- a/solution.py
+++ b/solution.py
@@ -211,24 +211,19 @@
     def one(row):
         return pl.ds(row + zero_row, 1)
 
-    pitch = cy + 16
-    PR_rows = PR.reshape(nq * cx * pitch, LANES)
-    VY_rows = VY.reshape(nq * cx * pitch, LANES)
-
-    def across(q, row):
-        return pl.ds(q * cx * pitch + 8 + row, cx, stride=pitch), slice(None)
-
     def pack_rows(t):
         for side in range(2):
             for r in range(2):
                 for q in range(nq):
-                    YS[t, side, r, q] = PR_rows[across(q, edges[side][r])]
+                    for i in range(cx):
+                        YS[t, side, r, q, one(i), :] = PR[q, i, one(8 + edges[side][r]), :]
 
     def unpack_rows(t):
         for side in range(2):
             for r in range(2):
                 for q in range(nq):
-                    PR_rows[across(q, edges[side][r])] = YS[t, side, r, q]
+                    for i in range(cx):
+                        PR[q, i, one(8 + edges[side][r]), :] = YS[t, side, r, q, one(i), :]
 
     def column_row(i, h, jb):
         return (i // planes) * part + (h * planes + i % planes) * cy + jb * 16
@@ -326,8 +321,9 @@
     for k in range(nq, 2 * nq):
         loads[k].wait()
     for q in range(nq):
-        VYS[0, q] = VY_rows[across(q, 0)]
-        VYS[1, q] = VY_rows[across(q, cy - 1)]
+        for i in range(cx):
+            VYS[0, q, one(i), :] = VY[q, i, one(8), :]
+            VYS[1, q, one(i), :] = VY[q, i, one(7 + cy), :]
     start(v_copy, (2, 3))
 
     for k in range(2 * nq, 2 * nq + 3):
@@ -364,17 +360,32 @@
         INFO[1] = leave_at.astype(f32)
         INFO[2] = alab
 
-    def slope_z(tiles):
-        height = tiles[0].shape[0]
-        lane = lax.broadcasted_iota(jnp.int32, (height, LANES), 1)
-        zero = jnp.zeros((height, LANES), f32)
-        ahead = [pltpu.roll(v, LANES - 1, 1) for v in tiles] + [zero]
-        behind = [zero] + [pltpu.roll(v, 1, 1) for v in tiles]
-        return [
-            jnp.where(lane == LANES - 1, ahead[q + 1], ahead[q])
-            - jnp.where(lane == 0, behind[q], behind[q + 1])
-            for q in range(nq)
-        ]
+    lane = lax.broadcasted_iota(jnp.int32, (16, LANES), 1)
+    zero = jnp.zeros((16, LANES), f32)
+
+    def rise_before(tiles):
+        turned = [pltpu.roll(v, 2, 1) for v in tiles]
+        before = [jnp.where(lane < 2, turned[q - 1], turned[q]) for q in range(nq)]
+        before[0] = jnp.where(lane == 1, zero, before[0])
+        here = [jnp.where(lane == 0, zero, tiles[0])] + tiles[1:]
+        return [a - b for a, b in zip(here, before)]
+
+    def rise_after(tiles):
+        turned = [pltpu.roll(v, LANES - 2, 1) for v in tiles]
+        after = [jnp.where(lane >= LANES - 2, turned[(q + 1) % nq], turned[q]) for q in range(nq)]
+        after[-1] = jnp.where(lane == LANES - 1, zero, after[-1])
+        here = [jnp.where(lane == 0, zero, tiles[0])] + tiles[1:]
+        return [a - b for a, b in zip(after, here)]
+
+    def shift_z(i, carry):
+        for jb in range(jbs):
+            rows = rows_of(jb)[0]
+            turned = [pltpu.roll(VZ[q, i, rows, :], 1, 1) for q in range(nq)]
+            for q in range(nq):
+                VZ[q, i, rows, :] = jnp.where(lane == 0, turned[q - 1], turned[q])
+        return carry
+
+    lax.fori_loop(0, cx, shift_z, 0, unroll=4)
 
     low_gate = jnp.where(has_lo, 1.0, 0.0).astype(f32)
     high_gate = jnp.where(has_hi, 1.0, 0.0).astype(f32)
@@ -471,7 +482,7 @@
 
         def flow_z(i, jb):
             rows, at = rows_of(jb)
-            slopes = slope_z([PR[q, i, at, :] for q in range(nq)])
+            slopes = rise_before([PR[q, i, at, :] for q in range(nq)])
             for q in range(nq):
                 VZ[q, i, rows, :] = VZ[q, i, rows, :] - half_gain * slopes[q]
 
@@ -485,7 +496,7 @@
 
         def pressure(i, jb):
             rows, at = rows_of(jb)
-            slopes = slope_z([VZ[q, i, rows, :] for q in range(nq)])
+            slopes = rise_after([VZ[q, i, rows, :] for q in range(nq)])
             for q in range(nq):
                 rise = slopes[q] + (
                     VY[q, i, pl.ds(9 + jb * 16 + zero_row, 16), :]
@@ -512,10 +523,13 @@
         pack_rows(t + 1)
 
         pl.when(t == 0)(plan)
+        wait_sent(lambda d: p_copy(t, d), (2, 3))
         wait_taken(lambda d: p_copy(t, d), (2, 3))
 
         @pl.when(t > 0)
         def _():
+            wait_sent(lambda d: dep_copy(t - 1, d))
+            wait_sent(lambda d: p_copy(t, d), (0, 1))
             wait_taken(lambda d: p_copy(t, d), (0, 1))
 
         @pl.when(t == 0)
@@ -582,22 +596,15 @@
 
         unpack_rows(t + 1)
         for q in range(nq):
-            low, high = across(q, 0), across(q, cy - 1)
-            VY_rows[low] = VY_rows[low] + half_gain * YR[t, 0, 1, q]
-            VY_rows[high] = VY_rows[high] - half_gain * YR[t, 1, 0, q]
+            for i in range(cx):
+                low, high = one(8), one(7 + cy)
+                VY[q, i, low, :] = VY[q, i, low, :] + half_gain * YR[t, 0, 1, q, one(i), :]
+                VY[q, i, high, :] = VY[q, i, high, :] - half_gain * YR[t, 1, 0, q, one(i), :]
 
         @pl.when(t == STEPS - 2)
         def _():
             leavers(t + 1, t + 1)
             start(lambda d: dep_copy(t + 1, d))
-
-        wait_sent(lambda d: dep_copy(t, d))
-
-        @pl.when(t > 0)
-        def _():
-            wait_sent(lambda d: p_copy(t, d), (0, 1))
-
-        wait_sent(lambda d: p_copy(t, d), (2, 3))
 
         return carry
 
@@ -613,6 +620,7 @@
             CAT[ARRIVE : 2 * ARRIVE, to] = low
 
     wait_sent(meta_copy)
+    wait_sent(lambda d: dep_copy(STEPS - 1, d))
     wait_sent(v_copy, (2, 3))
     for d in range(2):
         for copy in first_copies(d):
@@ -620,7 +628,7 @@
 
 
 def write_out(
-    p, vx, vy, vz, r, s, mask, cat, info, p_out, v_out, r_out, s_out, c_out, r_end, s_end, c_end, lt, sems
+    p, vx, vy, vz, r, s, mask, cat, info, p_out, v_out, r_out, s_out, c_out, r_end, s_end, z_end, c_end, lt, sems
 ):
     _, cx, cy, nz = v_out.shape
     pairs = []
@@ -628,11 +636,26 @@
         lanes = pl.ds(q * LANES, LANES)
         pairs.append((vx.at[q, pl.ds(1, cx), :, :], v_out.at[0, :, :, lanes]))
         pairs.append((vy.at[q, :, pl.ds(8, cy), :], v_out.at[1, :, :, lanes]))
-        pairs.append((vz.at[q], v_out.at[2, :, :, lanes]))
         pairs.append((p.at[q, :, pl.ds(8, cy), :], p_out.at[:, :, lanes]))
     copies = [pltpu.make_async_copy(a, b, sems.at[k]) for k, (a, b) in enumerate(pairs)]
     for copy in copies:
         copy.start()
+
+    nq = nz // LANES
+    lane = lax.broadcasted_iota(jnp.int32, (cy, LANES), 1)
+
+    def shift_z(i, carry):
+        turned = [pltpu.roll(vz[q, i], LANES - 1, 1) for q in range(nq)]
+        for q in range(nq):
+            z_end[q, i] = jnp.where(lane == LANES - 1, turned[(q + 1) % nq], turned[q])
+        return carry
+
+    lax.fori_loop(0, cx, shift_z, 0, unroll=2)
+    for q in range(nq):
+        to = v_out.at[2, :, :, pl.ds(q * LANES, LANES)]
+        copy = pltpu.make_async_copy(z_end.at[q], to, sems.at[len(copies)])
+        copy.start()
+        copies.append(copy)
 
     lane8 = lax.broadcasted_iota(jnp.int32, (8, LANES), 1)
     sub8 = lax.broadcasted_iota(jnp.int32, (8, LANES), 0)
@@ -794,6 +817,7 @@
         scratch_shapes=[
             pltpu.VMEM((SLOTS, BLOCK), f32),
             pltpu.VMEM((SLOTS, BLOCK), f32),
+            pltpu.VMEM((nq, cx, cy, LANES), f32),
             pltpu.VMEM((SLOT_BLOCKS, LANES), jnp.int32),
             pltpu.VMEM((LANES, LANES), f32),
             dma((4 * nq + 5,)),

time: 42.9 us -> 44.2 us (1.030)
  Pallas kernels: 42.2 us -> 43.2 us
    pallas_call x1, Pallas kernels: 2.83 us -> 3.66 us  [on_device(): pl.pallas_call(write_out, out_shape=(jax.ShapeDtypeStruct(pressure.shape,...]
where the time goes in v9:
time: 44.2 us; the launch traced here: 43.9 us
  Pallas kernels  43.2 us (98%)
  between operations  0.64 us (1%)
    pallas_call x1, Pallas kernels, on_device(): pl.pallas_call(kernel, out_shape=(vmem_out((nq, cx, cy + 16, LANES), f32)...  39.6 us
    pallas_call x1, Pallas kernels, on_device(): pl.pallas_call(write_out, out_shape=(jax.ShapeDtypeStruct(pressure.shape,...  3.66 us

profile of v9, /device:TPU:1, one launch (start us, length us, event | category | flops | bytes accessed | tf_op | source)
XLA Modules:
  0.0 43.9 jit_solution(11366029065757650419)
XLA Ops:
  0.6 39.6 %shard_map.119 = (f32[4,16,48,128]{3,2,1,0:T(8,128)S(1)}, f32[4,18,32,128]{3,2,1,0:T(8,128)S(1)}, f32[4,16,48,128]{3,2,1,0:T(8,128)S(1)}, f32[4,16,32,128]{3,2,1...) custom-call(s32[1024]{0:T(1024)} %cells_h.1, ...), custom_call_target="tpu_custom_call" | custom-call | flops 10737418240 | bytes 13631488 | tf_op jit(solution)/shard_map/pallas_call | solution.py:730
  40.2 3.7 %shard_map.120 = (f32[16,32,512]{2,1,0:T(8,128)}, f32[3,16,32,512]{3,2,1,0:T(8,128)}, f32[1024,256]{1,0:T(8,128)}, f32[1024,256]{1,0:T(8,128)}, s32[8,128]{1,0:T(8,128)}) custom-call(f32[4,16,48,128]{3,2,1,0:T(8,128)S(1)} %get-tuple-element.19.p, f32[4,18,32,128]{3,2,1,0:T(8,128)S(1)} %get-tuple-element.20.vx, f32[4,16,48,128]{3,2,1,0:T(8,128)S(1)} %get-tuple-element.21.vy, ...), custom_call_target="tpu_custom_call" | custom-call | bytes 13631488 | tf_op jit(solution)/shard_map/pallas_call | solution.py:806

commit v10 on v8

--- a/solution.py
+++ b/solution.py
@@ -382,15 +382,15 @@
     def halves(w):
         return slice(w * LANES, (w + 1) * LANES), slice(2 * w * LANES, 2 * (w + 1) * LANES)
 
-    def gather(w):
+    def gather(w, rows=slice(0, ROWS)):
         narrow, pair = halves(w)
-        both = jnp.dot(OH[...], PHL[:, pair], preferred_element_type=f32)
-        PG[:, narrow] = both[:, :LANES] + both[:, LANES:]
-
-    def scatter(w):
+        both = jnp.dot(OH[rows, :], PHL[:, pair], preferred_element_type=f32)
+        PG[rows, narrow] = both[:, :LANES] + both[:, LANES:]
+
+    def scatter(w, rows):
         narrow, pair = halves(w)
-        both = jnp.dot(OHT[...], VHL[:, pair], preferred_element_type=f32)
-        SRC[:, narrow] = both[:, :LANES] + both[:, LANES:]
+        both = jnp.dot(OHT[rows, :], VHL[:, pair], preferred_element_type=f32)
+        SRC[rows, narrow] = both[:, :LANES] + both[:, LANES:]
 
     def leavers(t, to):
         for k in range(DEP):
@@ -448,13 +448,17 @@
         def _():
             start(lambda d: dep_copy(t, d))
 
-        gather(1)
-        for first in range(0, ROWS - 32, 16):
-            bubbles(first, 0)
-        scatter(0)
-        for first in range(0, ROWS - 32, 16):
-            bubbles(first, 1)
-        scatter(1)
+        def pieces(count, size):
+            return [slice(k * size // count, (k + 1) * size // count) for k in range(count)]
+
+        for rows in pieces(3, ROWS):
+            gather(1, rows)
+            for first in range(rows.start, min(rows.stop, ROWS - 32), 16):
+                bubbles(first, 0)
+        for rows, part_rows in zip(pieces(2, ncol), ((0, 560), (560, ROWS - 32))):
+            scatter(0, rows)
+            for first in range(*part_rows, 16):
+                bubbles(first, 1)
 
         def flow_x(i):
             for q in range(nq):
@@ -501,11 +505,13 @@
                     PR[q, i, at, :] - half_gain * rise + SRC[row : row + 16, col : col + LANES]
                 )
 
-        for i in range(cx):
-            flow_x(i)
-            for jb in range(jbs):
-                flow_z(i, jb)
-                flow_y(i, jb)
+        for rows, part_planes in zip(pieces(2, ncol), pieces(2, cx)):
+            scatter(1, rows)
+            for i in range(part_planes.start, part_planes.stop):
+                flow_x(i)
+                for jb in range(jbs):
+                    flow_z(i, jb)
+                    flow_y(i, jb)
         for i in range(cx):
             for jb in range(jbs):
                 pressure(i, jb)

time: 42.9 us -> 42.1 us (0.981)
  Pallas kernels: 42.2 us -> 41.1 us
    pallas_call x1, Pallas kernels: 39.4 us -> 38.3 us  [on_device(): pl.pallas_call(kernel, out_shape=(vmem_out((nq, cx, cy + 16, LANES), f32)...]
where the time goes in v10:
time: 42.1 us; the launch traced here: 41.7 us
  Pallas kernels  41.1 us (98%)
  between operations  0.64 us (2%)
    pallas_call x1, Pallas kernels, on_device(): pl.pallas_call(kernel, out_shape=(vmem_out((nq, cx, cy + 16, LANES), f32)...  38.3 us
    pallas_call x1, Pallas kernels, on_device(): pl.pallas_call(write_out, out_shape=(jax.ShapeDtypeStruct(pressure.shape,...  2.83 us

profile of v10, /device:TPU:1, one launch (start us, length us, event | category | flops | bytes accessed | tf_op | source)
XLA Modules:
  0.0 41.7 jit_solution(13853067300129437835)
XLA Ops:
  0.6 38.3 %shard_map.119 = (f32[4,16,48,128]{3,2,1,0:T(8,128)S(1)}, f32[4,18,32,128]{3,2,1,0:T(8,128)S(1)}, f32[4,16,48,128]{3,2,1,0:T(8,128)S(1)}, f32[4,16,32,128]{3,2,1...) custom-call(s32[1024]{0:T(1024)} %cells_h.1, ...), custom_call_target="tpu_custom_call" | custom-call | flops 10737418240 | bytes 13631488 | tf_op jit(solution)/shard_map/pallas_call | solution.py:713
  38.9 2.8 %shard_map.120 = (f32[16,32,512]{2,1,0:T(8,128)}, f32[3,16,32,512]{3,2,1,0:T(8,128)}, f32[1024,256]{1,0:T(8,128)}, f32[1024,256]{1,0:T(8,128)}, s32[8,128]{1,0:T(8,128)}) custom-call(f32[4,16,48,128]{3,2,1,0:T(8,128)S(1)} %get-tuple-element.19.p, f32[4,18,32,128]{3,2,1,0:T(8,128)S(1)} %get-tuple-element.20.vx, f32[4,16,48,128]{3,2,1,0:T(8,128)S(1)} %get-tuple-element.21.vy, ...), custom_call_target="tpu_custom_call" | custom-call | bytes 13631488 | tf_op jit(solution)/shard_map/pallas_call | solution.py:789

commit v11 on v10

--- a/solution.py
+++ b/solution.py
@@ -140,7 +140,7 @@
     A[SLOTS:ROWS, :] = empty
     MSK[SLOTS:ROWS, :] = jnp.full((ARRIVE, LANES), -1.0, f32)
     OHT[:, SLOTS:ROWS] = jnp.zeros((ncol, ARRIVE), bf16)
-    VHL[ROWS - 32 : ROWS, :] = jnp.zeros((32, 2 * BLOCK), bf16)
+    VHL[SLOTS:ROWS, :] = jnp.zeros((ARRIVE, 2 * BLOCK), bf16)
     OH[SLOTS:ROWS, :] = jnp.zeros((ARRIVE, ncol), bf16)
     pl.semaphore_wait(barrier, 2 + has_lo.astype(jnp.int32) + has_hi.astype(jnp.int32))
 
@@ -387,9 +387,9 @@
         both = jnp.dot(OH[rows, :], PHL[:, pair], preferred_element_type=f32)
         PG[rows, narrow] = both[:, :LANES] + both[:, LANES:]
 
-    def scatter(w, rows):
+    def scatter(w, rows, count):
         narrow, pair = halves(w)
-        both = jnp.dot(OHT[rows, :], VHL[:, pair], preferred_element_type=f32)
+        both = jnp.dot(OHT[rows, :count], VHL[:count, pair], preferred_element_type=f32)
         SRC[rows, narrow] = both[:, :LANES] + both[:, LANES:]
 
     def leavers(t, to):
@@ -415,15 +415,19 @@
 
     def take_arrivals(t):
         wait_taken(lambda d: dep_copy(t, d))
-        rows = pl.ds(pl.multiple_of(t * 32, 32), 32)
-        to = pl.ds(pl.multiple_of(SLOTS + t * 32, 32), 32)
+        rows, to = slice(t * 32, t * 32 + 32), slice(SLOTS + t * 32, SLOTS + t * 32 + 32)
         R[to, :] = AR[0, rows, :]
         S[to, :] = AR[1, rows, :]
         A[to, :] = AR[2, rows, :]
         MSK[to, :] = jnp.where(AMSK[rows, :] > 0.0, 2.0 * STEPS, -1.0)
 
-    def step(t, carry):
-        limit = t.astype(f32)
+    def when(flag):
+        return lambda action: action() if flag else None
+
+    def step(t):
+        limit = float(t)
+        live = SLOTS + 32 * t
+        final = t == STEPS - 1
 
         def bubbles(first, w):
             rows = slice(first, first + 16)
@@ -435,29 +439,31 @@
             VHL[rows, 2 * w * LANES : (2 * w + 1) * LANES] = high
             VHL[rows, (2 * w + 1) * LANES : (2 * w + 2) * LANES] = low
 
-        @pl.when(t > 0)
+        @when(t > 0)
         def _():
             take_arrivals(t - 1)
 
         split_all()
         last = t // (STEPS - 1)
-        leavers(t, t + last)
-        gather(0)
-
-        @pl.when(last == 0)
+        if not final:
+            leavers(t, t)
+        gather(0, slice(0, live))
+
+        @when(last == 0)
         def _():
             start(lambda d: dep_copy(t, d))
 
         def pieces(count, size):
-            return [slice(k * size // count, (k + 1) * size // count) for k in range(count)]
-
-        for rows in pieces(3, ROWS):
+            ends = [k * size // count // 16 * 16 for k in range(count)] + [size]
+            return [slice(ends[k], ends[k + 1]) for k in range(count)]
+
+        for rows in pieces(2, live):
             gather(1, rows)
-            for first in range(rows.start, min(rows.stop, ROWS - 32), 16):
+            for first in range(rows.start, rows.stop, 16):
                 bubbles(first, 0)
-        for rows, part_rows in zip(pieces(2, ncol), ((0, 560), (560, ROWS - 32))):
-            scatter(0, rows)
-            for first in range(*part_rows, 16):
+        for rows, part_rows in zip(pieces(2, ncol), pieces(2, live)):
+            scatter(0, rows, SLOTS if t == 0 else ROWS)
+            for first in range(part_rows.start, part_rows.stop, 16):
                 bubbles(first, 1)
 
         def flow_x(i):
@@ -506,7 +512,7 @@
                 )
 
         for rows, part_planes in zip(pieces(2, ncol), pieces(2, cx)):
-            scatter(1, rows)
+            scatter(1, rows, SLOTS if t == 0 else ROWS)
             for i in range(part_planes.start, part_planes.stop):
                 flow_x(i)
                 for jb in range(jbs):
@@ -517,14 +523,14 @@
                 pressure(i, jb)
         pack_rows(t + 1)
 
-        pl.when(t == 0)(plan)
+        when(t == 0)(plan)
         wait_taken(lambda d: p_copy(t, d), (2, 3))
 
-        @pl.when(t > 0)
+        @when(t > 0)
         def _():
             wait_taken(lambda d: p_copy(t, d), (0, 1))
 
-        @pl.when(t == 0)
+        @when(t == 0)
         def _():
             for d in range(2):
                 for copy in first_copies(d):
@@ -552,8 +558,10 @@
                 second = PR[q, 1, at, :] + both_gains * near
                 PR[q, 0, at, :] = first
                 PR[q, 1, at, :] = second
-                XS[t + 1, 0, q, 0, rows, :] = first
-                XS[t + 1, 0, q, 1, rows, :] = second
+                if not final:
+                    XS[t + 1, 0, q, 0, rows, :] = first
+                if not final:
+                    XS[t + 1, 0, q, 1, rows, :] = second
                 near, far = XR[t, 1, q, 0, rows, :], XR[t, 1, q, 1, rows, :]
                 beside = VX[q, cx + 1, rows, :] - half_gain * (far - XS[t, 1, q, 1, rows, :])
                 VX[q, cx + 1, rows, :] = beside
@@ -562,8 +570,10 @@
                 second = PR[q, cx - 1, at, :] - half_gain * beside
                 PR[q, cx - 2, at, :] = first
                 PR[q, cx - 1, at, :] = second
-                XS[t + 1, 1, q, 0, rows, :] = first
-                XS[t + 1, 1, q, 1, rows, :] = second
+                if not final:
+                    XS[t + 1, 1, q, 0, rows, :] = first
+                if not final:
+                    XS[t + 1, 1, q, 1, rows, :] = second
         ends = ((0, 0, 0), (1, 0, 1), (cx - 2, 1, 0), (cx - 1, 1, 1))
         for i, x_side, x_row in ends:
             for side in range(2):
@@ -580,9 +590,10 @@
                             part_x = -half_gain * VX[q, cx + 1, row, :]
                         value = YS[t + 1, side, r, q, one(i), :] + part_x
                         YS[t + 1, side, r, q, one(i), :] = value
-                        XS[t + 1, x_side, q, x_row, row, :] = value
-
-        @pl.when(t < STEPS - 1)
+                        if not final:
+                            XS[t + 1, x_side, q, x_row, row, :] = value
+
+        @when(t < STEPS - 1)
         def _():
             start(lambda d: p_copy(t + 1, d))
 
@@ -592,22 +603,21 @@
             VY_rows[low] = VY_rows[low] + half_gain * YR[t, 0, 1, q]
             VY_rows[high] = VY_rows[high] - half_gain * YR[t, 1, 0, q]
 
-        @pl.when(t == STEPS - 2)
+        @when(t == STEPS - 2)
         def _():
             leavers(t + 1, t + 1)
             start(lambda d: dep_copy(t + 1, d))
 
         wait_sent(lambda d: dep_copy(t, d))
 
-        @pl.when(t > 0)
+        @when(t > 0)
         def _():
             wait_sent(lambda d: p_copy(t, d), (0, 1))
 
         wait_sent(lambda d: p_copy(t, d), (2, 3))
 
-        return carry
-
-    lax.fori_loop(0, STEPS, step, 0)
+    for t in range(STEPS):
+        step(t)
 
     take_arrivals(STEPS - 1)
     keep = AMSK[...] > 0.0

time: 42.1 us -> 42 us (level)
  no operation moved by 1% of the time
where the time goes in v11:
time: 42 us; the launch traced here: 41.8 us
  Pallas kernels  41 us (98%)
  between operations  0.82 us (2%)
    pallas_call x1, Pallas kernels, on_device(): pl.pallas_call(kernel, out_shape=(vmem_out((nq, cx, cy + 16, LANES), f32)...  38.2 us
    pallas_call x1, Pallas kernels, on_device(): pl.pallas_call(write_out, out_shape=(jax.ShapeDtypeStruct(pressure.shape,...  2.83 us

profile of v11, /device:TPU:1, one launch (start us, length us, event | category | flops | bytes accessed | tf_op | source)
XLA Modules:
  0.0 41.8 jit_solution(3276835781176863366)
XLA Ops:
  0.6 38.2 %shard_map.119 = (f32[4,16,48,128]{3,2,1,0:T(8,128)S(1)}, f32[4,18,32,128]{3,2,1,0:T(8,128)S(1)}, f32[4,16,48,128]{3,2,1,0:T(8,128)S(1)}, f32[4,16,32,128]{3,2,1...) custom-call(s32[1024]{0:T(1024)} %cells_h.1, ...), custom_call_target="tpu_custom_call" | custom-call | flops 10737418240 | bytes 13631488 | tf_op jit(solution)/shard_map/pallas_call | solution.py:723
  38.8 2.8 %shard_map.120 = (f32[16,32,512]{2,1,0:T(8,128)}, f32[3,16,32,512]{3,2,1,0:T(8,128)}, f32[1024,256]{1,0:T(8,128)}, f32[1024,256]{1,0:T(8,128)}, s32[8,128]{1,0:T(8,128)}) custom-call(f32[4,16,48,128]{3,2,1,0:T(8,128)S(1)} %get-tuple-element.19.p, f32[4,18,32,128]{3,2,1,0:T(8,128)S(1)} %get-tuple-element.20.vx, f32[4,16,48,128]{3,2,1,0:T(8,128)S(1)} %get-tuple-element.21.vy, ...), custom_call_target="tpu_custom_call" | custom-call | bytes 13631488 | tf_op jit(solution)/shard_map/pallas_call | solution.py:799

commit v12 on v11

--- a/solution.py
+++ b/solution.py
@@ -249,6 +249,21 @@
                 for q in range(nq):
                     keep_parts(i, jb, q, PR[q, i, rows_of(jb)[1], :])
 
+    for k in range(nq):
+        loads[k].wait()
+    pack_rows(0)
+    start(lambda d: p_copy(0, d), (2, 3))
+    for q in range(nq):
+        for r in range(2):
+            XS[0, 0, q, r] = PR[q, r, 8 : 8 + cy, :]
+            XS[0, 1, q, r] = PR[q, cx - 2 + r, 8 : 8 + cy, :]
+    for k in range(nq, 2 * nq):
+        loads[k].wait()
+    for q in range(nq):
+        VYS[0, q] = VY_rows[across(q, 0)]
+        VYS[1, q] = VY_rows[across(q, cy - 1)]
+    start(v_copy, (2, 3))
+
     for load in small_loads:
         load.wait()
 
@@ -314,21 +329,6 @@
             LT[:, 8 + r : 9 + r], (LANES, LANES)
         )
     hot_columns(0, SLOT_BLOCKS)
-
-    for k in range(nq):
-        loads[k].wait()
-    pack_rows(0)
-    start(lambda d: p_copy(0, d), (2, 3))
-    for q in range(nq):
-        for r in range(2):
-            XS[0, 0, q, r] = PR[q, r, 8 : 8 + cy, :]
-            XS[0, 1, q, r] = PR[q, cx - 2 + r, 8 : 8 + cy, :]
-    for k in range(nq, 2 * nq):
-        loads[k].wait()
-    for q in range(nq):
-        VYS[0, q] = VY_rows[across(q, 0)]
-        VYS[1, q] = VY_rows[across(q, cy - 1)]
-    start(v_copy, (2, 3))
 
     for k in range(2 * nq, 2 * nq + 3):
         loads[k].wait()
@@ -598,15 +598,16 @@
             start(lambda d: p_copy(t + 1, d))
 
         unpack_rows(t + 1)
+
+        @when(t == STEPS - 2)
+        def _():
+            leavers(t + 1, t + 1)
+            start(lambda d: dep_copy(t + 1, d))
+
         for q in range(nq):
             low, high = across(q, 0), across(q, cy - 1)
             VY_rows[low] = VY_rows[low] + half_gain * YR[t, 0, 1, q]
             VY_rows[high] = VY_rows[high] - half_gain * YR[t, 1, 0, q]
-
-        @when(t == STEPS - 2)
-        def _():
-            leavers(t + 1, t + 1)
-            start(lambda d: dep_copy(t + 1, d))
 
         wait_sent(lambda d: dep_copy(t, d))
 

time: 42 us -> 42 us (level)
  no operation moved by 1% of the time
where the time goes in v12:
time: 42 us; the launch traced here: 41.9 us
  Pallas kernels  41 us (98%)
  between operations  0.82 us (2%)
    pallas_call x1, Pallas kernels, on_device(): pl.pallas_call(kernel, out_shape=(vmem_out((nq, cx, cy + 16, LANES), f32)...  38.2 us
    pallas_call x1, Pallas kernels, on_device(): pl.pallas_call(write_out, out_shape=(jax.ShapeDtypeStruct(pressure.shape,...  2.83 us

profile of v12, /device:TPU:1, one launch (start us, length us, event | category | flops | bytes accessed | tf_op | source)
XLA Modules:
  0.0 41.9 jit_solution(10027192548910814219)
XLA Ops:
  0.6 38.2 %shard_map.119 = (f32[4,16,48,128]{3,2,1,0:T(8,128)S(1)}, f32[4,18,32,128]{3,2,1,0:T(8,128)S(1)}, f32[4,16,48,128]{3,2,1,0:T(8,128)S(1)}, f32[4,16,32,128]{3,2,1...) custom-call(s32[1024]{0:T(1024)} %cells_h.1, ...), custom_call_target="tpu_custom_call" | custom-call | flops 10737418240 | bytes 13631488 | tf_op jit(solution)/shard_map/pallas_call | solution.py:724
  38.8 2.8 %shard_map.120 = (f32[16,32,512]{2,1,0:T(8,128)}, f32[3,16,32,512]{3,2,1,0:T(8,128)}, f32[1024,256]{1,0:T(8,128)}, f32[1024,256]{1,0:T(8,128)}, s32[8,128]{1,0:T(8,128)}) custom-call(f32[4,16,48,128]{3,2,1,0:T(8,128)S(1)} %get-tuple-element.19.p, f32[4,18,32,128]{3,2,1,0:T(8,128)S(1)} %get-tuple-element.20.vx, f32[4,16,48,128]{3,2,1,0:T(8,128)S(1)} %get-tuple-element.21.vy, ...), custom_call_target="tpu_custom_call" | custom-call | bytes 13631488 | tf_op jit(solution)/shard_map/pallas_call | solution.py:800

commit v13 on v12

--- a/solution.py
+++ b/solution.py
@@ -423,6 +423,10 @@
 
     def when(flag):
         return lambda action: action() if flag else None
+
+    def settle(t):
+        wait_sent(lambda d: dep_copy(t, d))
+        wait_sent(lambda d: p_copy(t, d), (2, 3) if t == 0 else (0, 1, 2, 3))
 
     def step(t):
         limit = float(t)
@@ -609,13 +613,8 @@
             VY_rows[low] = VY_rows[low] + half_gain * YR[t, 0, 1, q]
             VY_rows[high] = VY_rows[high] - half_gain * YR[t, 1, 0, q]
 
-        wait_sent(lambda d: dep_copy(t, d))
-
-        @when(t > 0)
-        def _():
-            wait_sent(lambda d: p_copy(t, d), (0, 1))
-
-        wait_sent(lambda d: p_copy(t, d), (2, 3))
+        if t > 0:
+            settle(t - 1)
 
     for t in range(STEPS):
         step(t)
@@ -629,6 +628,7 @@
             CAT[0:ARRIVE, to] = high
             CAT[ARRIVE : 2 * ARRIVE, to] = low
 
+    settle(STEPS - 1)
     wait_sent(meta_copy)
     wait_sent(v_copy, (2, 3))
     for d in range(2):

time: 42 us -> 42 us (level)
  no operation moved by 1% of the time
where the time goes in v13:
time: 42 us; the launch traced here: 41.9 us
  Pallas kernels  41 us (98%)
  between operations  0.82 us (2%)
    pallas_call x1, Pallas kernels, on_device(): pl.pallas_call(kernel, out_shape=(vmem_out((nq, cx, cy + 16, LANES), f32)...  38.2 us
    pallas_call x1, Pallas kernels, on_device(): pl.pallas_call(write_out, out_shape=(jax.ShapeDtypeStruct(pressure.shape,...  2.83 us

profile of v13, /device:TPU:1, one launch (start us, length us, event | category | flops | bytes accessed | tf_op | source)
XLA Modules:
  0.0 41.9 jit_solution(15473246265399641278)
XLA Ops:
  0.6 38.2 %shard_map.119 = (f32[4,16,48,128]{3,2,1,0:T(8,128)S(1)}, f32[4,18,32,128]{3,2,1,0:T(8,128)S(1)}, f32[4,16,48,128]{3,2,1,0:T(8,128)S(1)}, f32[4,16,32,128]{3,2,1...) custom-call(s32[1024]{0:T(1024)} %cells_h.1, ...), custom_call_target="tpu_custom_call" | custom-call | flops 10737418240 | bytes 13631488 | tf_op jit(solution)/shard_map/pallas_call | solution.py:724
  38.8 2.8 %shard_map.120 = (f32[16,32,512]{2,1,0:T(8,128)}, f32[3,16,32,512]{3,2,1,0:T(8,128)}, f32[1024,256]{1,0:T(8,128)}, f32[1024,256]{1,0:T(8,128)}, s32[8,128]{1,0:T(8,128)}) custom-call(f32[4,16,48,128]{3,2,1,0:T(8,128)S(1)} %get-tuple-element.19.p, f32[4,18,32,128]{3,2,1,0:T(8,128)S(1)} %get-tuple-element.20.vx, f32[4,16,48,128]{3,2,1,0:T(8,128)S(1)} %get-tuple-element.21.vy, ...), custom_call_target="tpu_custom_call" | custom-call | bytes 13631488 | tf_op jit(solution)/shard_map/pallas_call | solution.py:800
